TPU v7x, 32 devices: a whole 2x2x4 slice. The times are simulated.
32 devices in a mesh: rep: 4 (over x, core), shard: 8 (over z, y).
Axes of the slice: x: 2, y: 2, z: 4, core: 2. Of those that a mesh axis runs over, the one named last changes fastest.
Arguments:
- token_ids: int32 [4, 2, 512], P('rep', None, 'shard'), may hold values from 0 to 31999
- targets: int32 [4, 2, 512], P('rep', None, 'shard'), may hold values from 0 to 31999
- valid_mask: int32 [4, 2, 512], P('rep', None, 'shard'), may hold values from 0 to 1
- mem_index: int32 [4, 2, 512, 8, 32], P('rep', None, 'shard'), may hold values from 0 to 4095
- memory: bfloat16 [2, 8, 4096, 128], replicated, may hold values from -6 to 6
- w_qkv: float32 [1024, 3072], P(('rep', 'shard')), may hold values from -0.1875 to 0.1875
- w_out: float32 [1024, 1024], P(('rep', 'shard')), may hold values from -0.75 to 0.75
- w_up: float32 [1024, 4096], P(('rep', 'shard')), may hold values from -0.1875 to 0.1875
- w_down: float32 [4096, 1024], P(('rep', 'shard')), may hold values from -0.09375 to 0.09375
- embed_table: float32 [32000, 1024], P(('rep', 'shard')), may hold values from -0.375 to 0.375
- gain_vector: float32 [3080], replicated, may hold values from -2 to 2
- mom_qkv: float32 [1024, 3072], P(('rep', 'shard')), may hold values from -4.5776367e-05 to 4.5776367e-05
- mom_out: float32 [1024, 1024], P(('rep', 'shard')), may hold values from -4.5776367e-05 to 4.5776367e-05
- mom_up: float32 [1024, 4096], P(('rep', 'shard')), may hold values from -4.5776367e-05 to 4.5776367e-05
- mom_down: float32 [4096, 1024], P(('rep', 'shard')), may hold values from -4.5776367e-05 to 4.5776367e-05
- mom_table: float32 [32000, 1024], P(('rep', 'shard')), may hold values from -4.5776367e-05 to 4.5776367e-05
- mom_gains: float32 [3080], replicated, may hold values from -0.00021362305 to 0.00021362305
- err_qkv: float32 [4, 8, 4, 32, 3072], P('rep', 'shard'), may hold values from -0.00207883623 to 0.00207883623
- err_out: float32 [4, 8, 4, 32, 1024], P('rep', 'shard'), may hold values from -0.00207883623 to 0.00207883623
- err_up: float32 [4, 8, 4, 32, 4096], P('rep', 'shard'), may hold values from -0.00207883623 to 0.00207883623
- err_down: float32 [4, 8, 4, 128, 1024], P('rep', 'shard'), may hold values from -0.00207883623 to 0.00207883623
- err_table: float32 [4, 8, 4, 1000, 1024], P('rep', 'shard'), may hold values from -0.00207883623 to 0.00207883623
- fac_qkv: float32 [3072, 8], replicated, may hold values from -6 to 6
- fac_out: float32 [1024, 8], replicated, may hold values from -6 to 6
- fac_up: float32 [4096, 8], replicated, may hold values from -6 to 6
- fac_down: float32 [1024, 8], replicated, may hold values from -6 to 6
- fac_table: float32 [1024, 8], replicated, may hold values from -6 to 6
Outputs:
- loss_sum: float32 [], replicated
- valid_count: float32 [], replicated
- clip_norm: float32 [], replicated
- new_mom_qkv: float32 [1024, 3072], P(('rep', 'shard'))
- new_mom_out: float32 [1024, 1024], P(('rep', 'shard'))
- new_mom_up: float32 [1024, 4096], P(('rep', 'shard'))
- new_mom_down: float32 [4096, 1024], P(('rep', 'shard'))
- new_mom_table: float32 [32000, 1024], P(('rep', 'shard'))
- new_mom_gains: float32 [3080], replicated
- new_w_qkv: float32 [1024, 3072], P(('rep', 'shard'))
- new_w_out: float32 [1024, 1024], P(('rep', 'shard'))
- new_w_up: float32 [1024, 4096], P(('rep', 'shard'))
- new_w_down: float32 [4096, 1024], P(('rep', 'shard'))
- new_table: float32 [32000, 1024], P(('rep', 'shard'))
- new_gains: float32 [3080], replicated
- new_err_qkv: float32 [4, 8, 4, 32, 3072], P('rep', 'shard')
- new_err_out: float32 [4, 8, 4, 32, 1024], P('rep', 'shard')
- new_err_up: float32 [4, 8, 4, 32, 4096], P('rep', 'shard')
- new_err_down: float32 [4, 8, 4, 128, 1024], P('rep', 'shard')
- new_err_table: float32 [4, 8, 4, 1000, 1024], P('rep', 'shard')
- new_fac_qkv: float32 [3072, 8], replicated
- new_fac_out: float32 [1024, 8], replicated
- new_fac_up: float32 [4096, 8], replicated
- new_fac_down: float32 [1024, 8], replicated
- new_fac_table: float32 [1024, 8], replicated
All inputs are finite; a program needn't handle non-finite values.
Results may differ from a plain program's by a relative error of at most 0.006.
The roundings to bfloat16 on the way count: a program that leaves them out, or rounds other values in their place, can miss the bound.
Values may be sent and summed in bfloat16 or wider, within the bound.
No kernel may reach another device: no remote copies, remote signals or barrier semaphores. Data moves between devices by JAX's collectives and lax.ppermute only.
A program may use at most 320 MiB of HBM per device.

v0:
```python
import math

import jax
import jax.numpy as jnp
from jax import lax
from jax.sharding import PartitionSpec as P

HEADS = 8


EPSILON = 1e-06
MOMENTUM = 0.9
LEARN_RATE = 5000.0
CLIP_LEVEL = 0.02
PRECISE_FORMAT = lax.Precision.HIGHEST
BROAD_NUMBER_TYPE = jnp.float32
NARROW_FORMAT = jnp.bfloat16


def combined_all(array, axis, combine):
    everything = jax.tree.map(lambda part: lax.all_gather(part, axis), array)
    leading = jax.tree.map(lambda part: part[0], everything)

    def step(k, so_far):
        return combine(so_far, jax.tree.map(lambda part: part[k], everything))

    return lax.fori_loop(1, lax.axis_size(axis), step, leading)


def matmul(left, right):
    return jnp.dot(left, right, preferred_element_type=BROAD_NUMBER_TYPE)


def matmul_back(left, right):
    return lax.dot_general(
        left, right, (((1,), (1,)), ((), ())), preferred_element_type=BROAD_NUMBER_TYPE
    )


def matmul_outer(left, right):
    return lax.dot_general(
        left, right, (((0,), (0,)), ((), ())), preferred_element_type=BROAD_NUMBER_TYPE
    )


def precise_dot(left, right):
    return jnp.dot(left, right, precision=PRECISE_FORMAT, preferred_element_type=BROAD_NUMBER_TYPE)


def precise_back(left, right):
    return lax.dot_general(
        left,
        right,
        (((1,), (1,)), ((), ())),
        precision=PRECISE_FORMAT,
        preferred_element_type=BROAD_NUMBER_TYPE,
    )


def precise_outer(left, right):
    return lax.dot_general(
        left,
        right,
        (((0,), (0,)), ((), ())),
        precision=PRECISE_FORMAT,
        preferred_element_type=BROAD_NUMBER_TYPE,
    )


def norm_rows(values, gain):
    inverse = lax.rsqrt(jnp.mean(values * values, axis=-1, keepdims=True) + EPSILON)
    return (values * inverse * gain, inverse)


def norm_back(values, inverse, gain, upstream):
    scaled = upstream * gain
    gain_part = jnp.sum(upstream * values * inverse, axis=0)
    result = inverse * scaled - values * inverse**3 * jnp.mean(
        scaled * values, axis=-1, keepdims=True
    )
    return (result, gain_part)


def softmax_last(attention_scores):
    powers = jnp.exp(attention_scores - jnp.max(attention_scores, axis=-1, keepdims=True))
    return powers / jnp.sum(powers, axis=-1, keepdims=True)


def spread_entries(entry_weights, mem_picks, mem_size):
    slots = jnp.arange(mem_size, dtype=jnp.int32)
    return jnp.sum(jnp.where(mem_picks[..., None] == slots, entry_weights[..., None], 0.0), axis=2)


def read_table(entry_weights, mem_picks, lookup_table):
    dense = spread_entries(entry_weights, mem_picks, lookup_table.shape[1])
    upper_bound = dense.astype(NARROW_FORMAT)
    lower_bound = (dense - upper_bound.astype(BROAD_NUMBER_TYPE)).astype(NARROW_FORMAT)
    return jnp.einsum(
        "ybi,bio->ybo", upper_bound, lookup_table, preferred_element_type=BROAD_NUMBER_TYPE
    ) + jnp.einsum(
        "ybi,bio->ybo", lower_bound, lookup_table, preferred_element_type=BROAD_NUMBER_TYPE
    )


def pick_entries(row_total, lookup_table, mem_picks):
    entry_listing = jnp.einsum(
        "bfy,fny->bfn", row_total, lookup_table, preferred_element_type=BROAD_NUMBER_TYPE
    )
    return jnp.take_along_axis(entry_listing, mem_picks, axis=2)


def attend(query_rows, key_collection, value_collection, memory, mem_picks):
    scale_factor = query_rows.shape[-1] ** (-0.5)
    length = query_rows.shape[0]
    causal_mask = jnp.arange(length)[:, None] >= jnp.arange(length)[None, :]
    attention_scores = (
        jnp.einsum(
            "yfa,tfa->fyt", query_rows, key_collection, preferred_element_type=BROAD_NUMBER_TYPE
        )
        * scale_factor
    )
    attention_weights = softmax_last(jnp.where(causal_mask[None], attention_scores, -1e30))
    local_output = jnp.einsum(
        "ros,srf->orf",
        attention_weights.astype(NARROW_FORMAT),
        value_collection,
        preferred_element_type=BROAD_NUMBER_TYPE,
    )
    mem_scores = pick_entries(query_rows, memory[0], mem_picks) * scale_factor
    mem_probs = softmax_last(mem_scores)
    memory_output = read_table(
        mem_probs.astype(NARROW_FORMAT).astype(BROAD_NUMBER_TYPE), mem_picks, memory[1]
    )
    return (local_output, memory_output, attention_weights, mem_probs)


def attend_back(
    query_rows, key_collection, value_collection, memory, mem_picks, local_gradient, mem_grad
):
    scale_factor = query_rows.shape[-1] ** (-0.5)
    unused_local, unused_mem, attention_weights, mem_probs = attend(
        query_rows, key_collection, value_collection, memory, mem_picks
    )
    probability_gradient = jnp.einsum(
        "yfa,tfa->fyt", local_gradient, value_collection, preferred_element_type=BROAD_NUMBER_TYPE
    )
    score_gradient = (
        attention_weights
        * (
            probability_gradient
            - jnp.sum(attention_weights * probability_gradient, axis=-1, keepdims=True)
        )
    ).astype(NARROW_FORMAT)
    value_grad = jnp.einsum(
        "njt,jnc->tnc",
        attention_weights.astype(NARROW_FORMAT),
        local_gradient,
        preferred_element_type=BROAD_NUMBER_TYPE,
    )
    key_grad = (
        jnp.einsum(
            "njt,jnc->tnc", score_gradient, query_rows, preferred_element_type=BROAD_NUMBER_TYPE
        )
        * scale_factor
    )
    mem_prob_grad = pick_entries(mem_grad, memory[1], mem_picks)
    mem_score_grad = (
        mem_probs * (mem_prob_grad - jnp.sum(mem_probs * mem_prob_grad, axis=-1, keepdims=True))
    ).astype(NARROW_FORMAT)
    query_grad = (
        jnp.einsum(
            "ros,srf->orf", score_gradient, key_collection, preferred_element_type=BROAD_NUMBER_TYPE
        )
        + read_table(mem_score_grad.astype(BROAD_NUMBER_TYPE), mem_picks, memory[0])
    ) * scale_factor
    return (query_grad, key_grad, value_grad)


def layer_forward(start_rows, layer_mats, gain_vector, memory, mem_picks):
    qkv_weight, out_weight, up_weight, down_weight = layer_mats
    length, model_width = start_rows.shape
    opening = jax.nn.sigmoid(gain_vector[3 * model_width :])
    normed_one, inverse_one = norm_rows(start_rows, gain_vector[:model_width])
    hidden_one = normed_one.astype(NARROW_FORMAT)
    projected = (
        matmul(hidden_one, qkv_weight)
        .astype(NARROW_FORMAT)
        .reshape(length, 3, HEADS, model_width // HEADS)
    )
    local_output, memory_output, unused_probs, unused_mem = attend(
        projected[:, 0], projected[:, 1], projected[:, 2], memory, mem_picks
    )
    mixture = opening[:, None] * memory_output + (1.0 - opening[:, None]) * local_output
    attended = mixture.reshape(length, model_width).astype(NARROW_FORMAT)
    after_attn = start_rows + matmul(attended, out_weight)
    normed_two, inverse_two = norm_rows(after_attn, gain_vector[model_width : 2 * model_width])
    hidden_two = normed_two.astype(NARROW_FORMAT)
    up_value = matmul(hidden_two, up_weight)
    activated = jax.nn.gelu(up_value).astype(NARROW_FORMAT)
    after_mlp = after_attn + matmul(activated, down_weight)
    saved_values = (
        start_rows,
        inverse_one,
        hidden_one,
        projected,
        local_output,
        memory_output,
        attended,
        after_attn,
        inverse_two,
        hidden_two,
        up_value,
        activated,
    )
    return (after_mlp, saved_values)


def layer_back(saved_values, mlp_grad, layer_mats, gain_vector, memory, mem_picks):
    (
        start_rows,
        inverse_one,
        hidden_one,
        projected,
        local_output,
        memory_output,
        attended,
        after_attn,
        inverse_two,
        hidden_two,
        up_value,
        activated,
    ) = saved_values
    qkv_weight, out_weight, up_weight, down_weight = layer_mats
    length, model_width = start_rows.shape
    opening = jax.nn.sigmoid(gain_vector[3 * model_width :])
    down_in = mlp_grad.astype(NARROW_FORMAT)
    down_grad = matmul_outer(activated, down_in)
    act_grad = matmul_back(down_in, down_weight)
    unused_value, gelu_pull = jax.vjp(jax.nn.gelu, up_value)
    (up_grad_wide,) = gelu_pull(act_grad)
    up_in = up_grad_wide.astype(NARROW_FORMAT)
    up_grad = matmul_outer(hidden_two, up_in)
    norm_two_grad, gain_two_grad = norm_back(
        after_attn,
        inverse_two,
        gain_vector[model_width : 2 * model_width],
        matmul_back(up_in, up_weight),
    )
    attn_grad = mlp_grad + norm_two_grad
    out_in = attn_grad.astype(NARROW_FORMAT)
    out_grad = matmul_outer(attended, out_in)
    mixture_grad = matmul_back(out_in, out_weight).reshape(length, HEADS, model_width // HEADS)
    gate_grad = (
        jnp.sum(mixture_grad * (memory_output - local_output), axis=(0, 2))
        * opening
        * (1.0 - opening)
    )
    mem_grad = (opening[:, None] * mixture_grad).astype(NARROW_FORMAT)
    local_gradient = ((1.0 - opening[:, None]) * mixture_grad).astype(NARROW_FORMAT)
    query_grad, key_grad, value_grad = attend_back(
        projected[:, 0],
        projected[:, 1],
        projected[:, 2],
        memory,
        mem_picks,
        local_gradient,
        mem_grad,
    )
    qkv_in = (
        jnp.stack([query_grad, key_grad, value_grad], axis=1)
        .reshape(length, 3 * model_width)
        .astype(NARROW_FORMAT)
    )
    qkv_grad = matmul_outer(hidden_one, qkv_in)
    norm_one_grad, gain_one_grad = norm_back(
        start_rows, inverse_one, gain_vector[:model_width], matmul_back(qkv_in, qkv_weight)
    )
    return (
        attn_grad + norm_one_grad,
        (qkv_grad, out_grad, up_grad, down_grad),
        (gain_one_grad, gain_two_grad, gate_grad),
    )


def fetch_weights(narrow_masters):
    return (
        lax.all_gather(narrow_masters[0], ("rep", "shard"), axis=0, tiled=True),
        lax.all_gather(narrow_masters[1], ("rep", "shard"), axis=0, tiled=True),
        lax.all_gather(narrow_masters[2], ("rep", "shard"), axis=0, tiled=True),
        lax.all_gather(narrow_masters[3], ("rep", "shard"), axis=0, tiled=True),
    )


def to_slab(gradient, rep_count, shard_count):
    height, breadth = gradient.shape
    return gradient.reshape(
        rep_count, shard_count, height // (rep_count * shard_count), breadth
    ).transpose(1, 0, 2, 3)


def reduce_grads(gradients, rep_count, shard_count):
    return (
        lax.psum_scatter(
            to_slab(gradients[0], rep_count, shard_count), "shard", scatter_dimension=0, tiled=True
        ),
        lax.psum_scatter(
            to_slab(gradients[1], rep_count, shard_count), "shard", scatter_dimension=0, tiled=True
        ),
        lax.psum_scatter(
            to_slab(gradients[2], rep_count, shard_count), "shard", scatter_dimension=0, tiled=True
        ),
        lax.psum_scatter(
            to_slab(gradients[3], rep_count, shard_count), "shard", scatter_dimension=0, tiled=True
        ),
    )


def merge_stats(first_part, second_part):
    peak_value = jnp.maximum(first_part[0], second_part[0])
    exp_total = first_part[1] * jnp.exp(first_part[0] - peak_value) + second_part[1] * jnp.exp(
        second_part[0] - peak_value
    )
    return (peak_value, exp_total, first_part[2] + second_part[2])


def orthonormal(left_sum, gram_sum):
    lower_tri = jnp.linalg.cholesky(gram_sum)
    return lax.linalg.triangular_solve(lower_tri, left_sum.T, left_side=True, lower=True).T


def shards(
    token_ids,
    targets,
    valid_mask,
    mem_index,
    memory,
    w_qkv,
    w_out,
    w_up,
    w_down,
    embed_table,
    gain_vector,
    mom_qkv,
    mom_out,
    mom_up,
    mom_down,
    mom_table,
    mom_gains,
    err_qkv,
    err_out,
    err_up,
    err_down,
    err_table,
    fac_qkv,
    fac_out,
    fac_up,
    fac_down,
    fac_table,
):
    rep_count = lax.axis_size("rep")
    shard_count = lax.axis_size("shard")
    rep_at = lax.axis_index("rep")
    shard_at = lax.axis_index("shard")
    micro_count = token_ids.shape[1]
    length = token_ids.shape[2]
    model_width = w_out.shape[1]
    everyone = (
        lax.all_gather(token_ids, ("rep", "shard"), axis=0, tiled=True),
        lax.all_gather(targets, ("rep", "shard"), axis=0, tiled=True),
        lax.all_gather(valid_mask, ("rep", "shard"), axis=0, tiled=True),
    )
    valid_count = jnp.sum(everyone[2]).astype(BROAD_NUMBER_TYPE)

    def own_group(source):
        block_part = lax.dynamic_slice_in_dim(source, rep_at * shard_count, shard_count, 0)
        return jnp.transpose(block_part, (1, 0, 2)).reshape(micro_count, shard_count * length)

    group_ids = own_group(everyone[0])
    group_targets = own_group(everyone[1])
    group_valid = own_group(everyone[2]).astype(BROAD_NUMBER_TYPE)
    block_rows = embed_table.shape[0]
    vocab_local = lax.all_gather(embed_table.astype(NARROW_FORMAT), "rep", axis=0, tiled=True)

    def locate(id_values):
        block_index = id_values // block_rows
        owned_rows = block_index % shard_count == shard_at
        column = block_index // shard_count * block_rows + id_values % block_rows
        return (owned_rows, column)

    narrow_masters = (
        w_qkv.astype(NARROW_FORMAT),
        w_out.astype(NARROW_FORMAT),
        w_up.astype(NARROW_FORMAT),
        w_down.astype(NARROW_FORMAT),
    )
    gain_final = gain_vector[2 * model_width : 3 * model_width]
    embed_scale = math.sqrt(model_width)
    vocab_columns = jnp.arange(vocab_local.shape[0])
    table_grad = jnp.zeros(vocab_local.shape, BROAD_NUMBER_TYPE)
    gain_grad = jnp.zeros(gain_vector.shape, BROAD_NUMBER_TYPE)
    loss_own = jnp.zeros((), BROAD_NUMBER_TYPE)
    totals = None
    slabs = None
    for micro_at in range(micro_count):
        ids_micro = group_ids[micro_at]
        valid_micro = group_valid[micro_at]
        owned_rows, column = locate(ids_micro)
        picked_rows = jnp.where(
            owned_rows[:, None], vocab_local[column], jnp.zeros((), NARROW_FORMAT)
        )
        start_rows = embed_scale * lax.psum_scatter(
            picked_rows, "shard", scatter_dimension=0, tiled=True
        ).astype(jnp.float32)
        mem_picks = mem_index[0, micro_at]
        layer_mats = fetch_weights(narrow_masters)
        after_mlp, saved_values = layer_forward(
            start_rows, layer_mats, gain_vector, memory, mem_picks
        )
        final_norm, final_inverse = norm_rows(after_mlp, gain_final)
        final_all = lax.all_gather(final_norm.astype(NARROW_FORMAT), "shard", axis=0, tiled=True)
        logits = matmul_back(final_all, vocab_local)
        target_owned, target_column = locate(group_targets[micro_at])
        hit_mask = (vocab_columns[None, :] == target_column[:, None]) & target_owned[:, None]
        peak_value = jnp.max(logits, axis=-1)
        exp_total = jnp.sum(jnp.exp(logits - peak_value[:, None]), axis=-1)
        picked_logit = jnp.sum(jnp.where(hit_mask, logits, 0.0), axis=-1)
        peak_value, exp_total, picked_logit = combined_all(
            (peak_value, exp_total, picked_logit), "shard", merge_stats
        )
        log_total = peak_value + jnp.log(exp_total)
        row_losses = valid_micro * (log_total - picked_logit)
        loss_own = loss_own + jnp.sum(
            lax.dynamic_slice_in_dim(row_losses, shard_at * length, length, 0)
        )
        logit_grad = (
            (jnp.exp(logits - log_total[:, None]) - hit_mask.astype(BROAD_NUMBER_TYPE))
            * (valid_micro / valid_count)[:, None]
        ).astype(NARROW_FORMAT)
        table_grad = table_grad + matmul_outer(logit_grad, final_all)
        final_grad = lax.psum_scatter(
            matmul(logit_grad, vocab_local), "shard", scatter_dimension=0, tiled=True
        )
        mlp_grad, final_gain_grad = norm_back(after_mlp, final_inverse, gain_final, final_grad)
        layer_mats = fetch_weights(narrow_masters)
        start_grad, weight_grads, gain_parts = layer_back(
            saved_values, mlp_grad, layer_mats, gain_vector, memory, mem_picks
        )
        gain_grad = gain_grad + jnp.concatenate(
            [gain_parts[0], gain_parts[1], final_gain_grad, gain_parts[2]]
        )
        piece_owned, piece_column = locate(ids_micro)
        table_grad = table_grad.at[piece_column].add(
            jnp.where(
                piece_owned[:, None], lax.all_gather(start_grad, "shard", axis=0, tiled=True), 0.0
            )
            * embed_scale
        )
        totals = weight_grads if totals is None else jax.tree.map(jnp.add, totals, weight_grads)
    slabs = reduce_grads(totals, rep_count, shard_count)
    slab_list = [element.reshape(-1, element.shape[-1]) for element in slabs] + [table_grad]
    errors = (err_qkv, err_out, err_up, err_down, err_table)
    moved_slabs = [
        slab_list[index_at] + errors[index_at].reshape(slab_list[index_at].shape)
        for index_at in range(5)
    ]
    left_sums = lax.psum(
        (
            precise_dot(moved_slabs[0], fac_qkv),
            precise_dot(moved_slabs[1], fac_out),
            precise_dot(moved_slabs[2], fac_up),
            precise_dot(moved_slabs[3], fac_down),
            precise_dot(moved_slabs[4], fac_table),
        ),
        "rep",
    )
    gram_sums = lax.psum(
        (
            precise_outer(left_sums[0], left_sums[0]),
            precise_outer(left_sums[1], left_sums[1]),
            precise_outer(left_sums[2], left_sums[2]),
            precise_outer(left_sums[3], left_sums[3]),
            precise_outer(left_sums[4], left_sums[4]),
        ),
        "shard",
    )
    orthos = [orthonormal(left_sums[index_at], gram_sums[index_at]) for index_at in range(5)]
    right_sums = lax.psum(
        (
            precise_outer(moved_slabs[0], orthos[0]),
            precise_outer(moved_slabs[1], orthos[1]),
            precise_outer(moved_slabs[2], orthos[2]),
            precise_outer(moved_slabs[3], orthos[3]),
            precise_outer(moved_slabs[4], orthos[4]),
            gain_grad,
        ),
        ("rep", "shard"),
    )
    gain_sum = right_sums[5]
    approxes = [precise_back(orthos[index_at], right_sums[index_at]) for index_at in range(5)]
    new_errors = [
        (moved_slabs[index_at] - approxes[index_at]).reshape(errors[index_at].shape)
        for index_at in range(5)
    ]
    own_blocks = []
    block_squares = jnp.zeros((), BROAD_NUMBER_TYPE)
    for approx in approxes:
        own_height = approx.shape[0] // rep_count
        own_block = lax.dynamic_slice_in_dim(approx, rep_at * own_height, own_height, 0)
        own_blocks.append(own_block)
        block_squares = block_squares + jnp.sum(own_block * own_block)
    square_total, loss_sum = lax.psum((block_squares, loss_own), ("rep", "shard"))
    clip_norm = jnp.sqrt(square_total + jnp.sum(gain_sum * gain_sum))
    shrink = jnp.minimum(1.0, CLIP_LEVEL / clip_norm)
    gradients = own_blocks + [gain_sum]
    moments = (mom_qkv, mom_out, mom_up, mom_down, mom_table, mom_gains)
    masters = (w_qkv, w_out, w_up, w_down, embed_table, gain_vector)
    new_moments = [
        MOMENTUM * moments[index_at] + shrink * gradients[index_at] for index_at in range(6)
    ]
    new_weights = [masters[index_at] - LEARN_RATE * new_moments[index_at] for index_at in range(6)]
    return (
        loss_sum,
        valid_count,
        clip_norm,
        new_moments[0],
        new_moments[1],
        new_moments[2],
        new_moments[3],
        new_moments[4],
        new_moments[5],
        new_weights[0],
        new_weights[1],
        new_weights[2],
        new_weights[3],
        new_weights[4],
        new_weights[5],
        new_errors[0],
        new_errors[1],
        new_errors[2],
        new_errors[3],
        new_errors[4],
        right_sums[0],
        right_sums[1],
        right_sums[2],
        right_sums[3],
        right_sums[4],
    )


def solution(mesh):
    return jax.shard_map(
        shards,
        mesh=mesh,
        in_specs=(
            P("rep", None, "shard"),
            P("rep", None, "shard"),
            P("rep", None, "shard"),
            P("rep", None, "shard", None, None),
            P(),
            P(("rep", "shard"), None),
            P(("rep", "shard"), None),
            P(("rep", "shard"), None),
            P(("rep", "shard"), None),
            P(("rep", "shard"), None),
            P(),
            P(("rep", "shard"), None),
            P(("rep", "shard"), None),
            P(("rep", "shard"), None),
            P(("rep", "shard"), None),
            P(("rep", "shard"), None),
            P(),
            P("rep", "shard", None, None, None),
            P("rep", "shard", None, None, None),
            P("rep", "shard", None, None, None),
            P("rep", "shard", None, None, None),
            P("rep", "shard", None, None, None),
            P(),
            P(),
            P(),
            P(),
            P(),
        ),
        out_specs=(
            P(),
            P(),
            P(),
            P(("rep", "shard"), None),
            P(("rep", "shard"), None),
            P(("rep", "shard"), None),
            P(("rep", "shard"), None),
            P(("rep", "shard"), None),
            P(),
            P(("rep", "shard"), None),
            P(("rep", "shard"), None),
            P(("rep", "shard"), None),
            P(("rep", "shard"), None),
            P(("rep", "shard"), None),
            P(),
            P("rep", "shard", None, None, None),
            P("rep", "shard", None, None, None),
            P("rep", "shard", None, None, None),
            P("rep", "shard", None, None, None),
            P("rep", "shard", None, None, None),
            P(),
            P(),
            P(),
            P(),
            P(),
        ),
        check_vma=False,
    )
```

profile of v0, /device:TPU:0, one launch (start us, length us, event | category | flops | bytes accessed | tf_op | source)
XLA Modules:
  0.0 4188.1 jit_solution(14722594096023240249)
XLA Ops:
  12.0 69.9 %all_gather.85 = s32[32,2,64]{2,1,0:T(2,128)S(1)} all-gather(s32[1,2,64]{2,1,0:T(2,128)S(1)} %copy-done.174), channel_id=1, replica_groups=mesh['rep'=4,'shard'=8] {'rep','shard'}, dimensions={0}, use_global_device_ids=true | all-gather | bytes 16896 | tf_op jit(solution)/shard_map/all_gather | solution.py:368
  108.2 59.2 %reduce-scatter.19.cloned.1.call-done = bf16[64,1024]{1,0:T(8,128)(2,1)} async-done(((bf16[512,1024]{1,0:T(8,128)(2,1)}), bf16[64,1024]{1,0:T(8,128)(2,1)}) %reduce-scatter.19.cloned.1.call-update) | async-done | bytes 131088 | tf_op jit(solution)/shard_map/reduce_scatter | solution.py:411
  174.0 61.8 %reduce-scatter.17.cloned.1.call-done = bf16[64,1024]{1,0:T(8,128)(2,1)} async-done(((bf16[512,1024]{1,0:T(8,128)(2,1)}), bf16[64,1024]{1,0:T(8,128)(2,1)}) %reduce-scatter.17.cloned.1.call-update) | async-done | bytes 131088 | tf_op jit(solution)/shard_map/reduce_scatter | solution.py:411
  252.8 228.3 %gather_fusion.2 = f32[16384]{0:T(1024)S(1)} fusion(f32[64,8,4096]{2,0,1:T(8,128)} %fusion.34, s32[16384]{0:T(1024)S(1)} %reshape.904), kind=kCustom, calls=%fused_computation.clone | custom fusion | bytes 327680 | tf_op jit(solution)/shard_map/jit(take_along_axis)/gather | solution.py:109
  482.3 63.1 %select_reduce_fusion.3 = f32[64,8,4096]{2,1,0:T(8,128)} fusion(f32[64,8,32]{2,1,0:T(8,128)S(1)} %get-tuple-element.560, s32[64,8,32]{2,1,0:T(8,128)S(1)} %bitcast.512), kind=kLoop, calls=%fused_computation.28 | loop fusion | flops 199229440 | bytes 8519680 | tf_op jit(solution)/shard_map/reduce_sum | solution.py:91
  555.2 227.2 %gather_fusion.3 = f32[16384]{0:T(1024)S(1)} fusion(f32[64,8,4096]{2,0,1:T(8,128)} %fusion.37, s32[16384]{0:T(1024)S(1)} %reshape.909), kind=kCustom, calls=%fused_computation.1.clone | custom fusion | bytes 327680 | tf_op jit(solution)/shard_map/jit(take_along_axis)/gather | solution.py:109
  804.9 63.2 %select_reduce_fusion.2 = f32[64,8,4096]{2,1,0:T(8,128)} fusion(f32[64,8,32]{2,1,0:T(8,128)S(1)} %get-tuple-element.556, s32[64,8,32]{2,1,0:T(8,128)S(1)} %bitcast.514), kind=kLoop, calls=%fused_computation.26 | loop fusion | flops 199229440 | bytes 8519680 | tf_op jit(solution)/shard_map/reduce_sum | solution.py:91
  925.3 65.7 %all_gather.84 = s32[32,2,64]{2,1,0:T(2,128)S(1)} all-gather(s32[1,2,64]{2,1,0:T(2,128)S(1)} %copy-done.175), channel_id=1, replica_groups=mesh['rep'=4,'shard'=8] {'rep','shard'}, dimensions={0}, use_global_device_ids=true | all-gather | bytes 16896 | tf_op jit(solution)/shard_map/all_gather | solution.py:370
  992.3 63.7 %all_gather.96 = s32[32,2,64]{2,1,0:T(2,128)S(1)} all-gather(s32[1,2,64]{2,1,0:T(2,128)S(1)} %copy-done.176), channel_id=1, replica_groups=mesh['rep'=4,'shard'=8] {'rep','shard'}, dimensions={0}, use_global_device_ids=true | all-gather | bytes 16896 | tf_op jit(solution)/shard_map/all_gather | solution.py:369
  1071.7 26.3 all-gather.7
  1098.5 26.0 all-gather.8
  1125.1 26.0 all-gather.6
  1165.3 26.0 all-gather.10
  1191.3 26.0 all-gather.11
  1217.9 26.4 all-gather.9
  1306.7 26.4 reduce-scatter.21.cloned.1.call-done
  1333.1 70.8 %reduce-scatter.23.cloned.1.call-done = f32[64,1024]{1,0:T(8,128)} async-done(((f32[512,1024]{1,0:T(8,128)}), f32[64,1024]{1,0:T(8,128)}) %reduce-scatter.23.cloned.1.call-update) | async-done | bytes 262160 | tf_op jit(solution)/shard_map/reduce_scatter | solution.py:440
  1454.8 226.3 %gather_fusion.5 = f32[16384]{0:T(1024)S(1)} fusion(f32[64,8,4096]{2,0,1:T(8,128)} %fusion.43, s32[16384]{0:T(1024)S(1)} %reshape.909), kind=kCustom, calls=%fused_computation.3.clone | custom fusion | bytes 327680 | tf_op jit(solution)/shard_map/jit(take_along_axis)/gather | solution.py:109
  1686.7 63.1 %select_reduce_fusion = f32[64,8,4096]{2,1,0:T(8,128)} fusion(f32[64,8,32]{2,1,0:T(8,128)S(1)} %fusion.139, s32[64,8,32]{2,1,0:T(8,128)S(1)} %bitcast.515), kind=kLoop, calls=%fused_computation.24 | loop fusion | flops 199229440 | bytes 8519680 | tf_op jit(solution)/shard_map/reduce_sum | solution.py:91
  1774.6 226.7 %gather_fusion.4 = f32[16384]{0:T(1024)S(1)} fusion(f32[64,8,4096]{2,0,1:T(8,128)} %fusion.40, s32[16384]{0:T(1024)S(1)} %copy-done.2), kind=kCustom, calls=%fused_computation.2.clone | custom fusion | bytes 327680 | tf_op jit(solution)/shard_map/jit(take_along_axis)/gather | solution.py:109
  2006.8 63.1 %select_reduce_fusion.1 = f32[64,8,4096]{2,1,0:T(8,128)} fusion(f32[64,8,32]{2,1,0:T(8,128)S(1)} %fusion.141, s32[64,8,32]{2,1,0:T(8,128)S(1)} %bitcast.513), kind=kLoop, calls=%fused_computation.25 | loop fusion | flops 199229440 | bytes 8519680 | tf_op jit(solution)/shard_map/reduce_sum | solution.py:91
  2102.5 20.5 bitcast_add_fusion
  2183.0 17.8 scatter_custom_fusion
  2203.3 17.6 scatter_custom_fusion.1
  2220.8 17.8 fusion.344
  2248.0 20.7 all-reduce.15.cloned.1.call-done
  2270.1 1482.2 %all-reduce.21.cloned.1.call-done = (f32[8,4,32,3072]{3,2,0,1:T(8,128)}, f32[8,4,32,4096]{3,2,0,1:T(8,128)}, f32[8,4,32,1024]{3,2,0,1:T(8,128)}, f32[8,4,128,1024]{3,2,0,1:T(8,128)}) async-done(((f32[8,4,32,3072]{3,2,0,1:T(8,128)}, f32[8,4,32,4096]{3,2,0,1:T(8,128)}, f32[8,4,32,1024]{3,2,0,1:T(8,128)}, f32[8,4,128,1024]{3,2,0,1:T(8,128)}), (f32[8,4,32,3072]{3,2,0,1:T(8,128)}, f32[8,4,32,4096]{3,2,0,1:T(8,128)}, ...) | async-done | bytes 50331664
  3780.8 34.7 all-reduce.7
  3852.8 114.9 %all-reduce.17.cloned.1.call-done = (f32[1024,8]{0,1:T(8,128)}, f32[1024,8]{0,1:T(8,128)}, f32[1024,8]{0,1:T(8,128)}) async-done(((f32[1024,8]{0,1:T(8,128)}, f32[1024,8]{0,1:T(8,128)}, f32[1024,8]{0,1:T(8,128)}), (f32[1024,8]{0,1:T(8,128)}, f32[1024,8]{0,1:T(8,128)}, f32[1024,8]{0,1:T(8,128)})) %all-reduce.17.cloned.1.call-update) | async-done | bytes 98320 | tf_op jit(solution)/shard_map/psum | solution.py:487
  3971.6 22.3 fusion.330
  4000.6 98.3 %all-reduce.19.cloned.1.call-done = (f32[3072,8]{0,1:T(8,128)}, f32[4096,8]{0,1:T(8,128)}) async-done(((f32[3072,8]{0,1:T(8,128)}, f32[4096,8]{0,1:T(8,128)}), (f32[3072,8]{0,1:T(8,128)}, f32[4096,8]{0,1:T(8,128)})) %all-reduce.19.cloned.1.call-update) | async-done | bytes 229392 | tf_op jit(solution)/shard_map/psum | solution.py:487
  4113.5 41.4 all-reduce.4
  (781 shorter events, 558.5 us)
Async XLA Ops:
  8.0 3757.2 %copy-start = (f32[4096,8]{0,1:T(8,128)S(1)}, f32[4096,8]{0,1:T(8,128)}, u32[]{:S(2)}) copy-start(f32[4096,8]{0,1:T(8,128)} %param.60) | copy-start | bytes 393220
  8.1 75.7 %all-gather.22.cloned.1.call-start = ((), (), s32[]{:S(2)}) async-start(), calls=%async_computation.4 | async-start | bytes 10240000 | tf_op jit(solution)/shard_map/all_gather | solution.py:382
  11.9 155.5 %reduce-scatter.19.cloned.1.call-start = ((), (), s32[]{:S(2)}) async-start(), calls=%async_computation.11 | async-start | bytes 1179648 | tf_op jit(solution)/shard_map/reduce_scatter | solution.py:411
  92.5 76.5 %all-gather.24.cloned.1.call-start = ((), (), s32[]{:S(2)}) async-start(), calls=%async_computation.6 | async-start | bytes 6488064 | tf_op jit(solution)/shard_map/all_gather | solution.py:287
  93.3 142.4 %reduce-scatter.17.cloned.1.call-start = ((), (), s32[]{:S(2)}) async-start(), calls=%async_computation.5 | async-start | bytes 1179648 | tf_op jit(solution)/shard_map/reduce_scatter | solution.py:411
  102.2 800.2 %all-gather.26.cloned.1.call-start = ((), (), s32[]{:S(2)}) async-start(), calls=%async_computation.7 | async-start | bytes 2162688 | tf_op jit(solution)/shard_map/all_gather | solution.py:288
  102.9 805.0 %all-gather.28.cloned.1.call-start = ((), (), s32[]{:S(2)}) async-start(), calls=%async_computation.8 | async-start | bytes 8650752 | tf_op jit(solution)/shard_map/all_gather | solution.py:289
  103.7 809.3 %all-gather.30.cloned.1.call-start = ((), (), s32[]{:S(2)}) async-start(), calls=%async_computation.9 | async-start | bytes 8650752 | tf_op jit(solution)/shard_map/all_gather | solution.py:290
  104.6 953.6 %all-gather.32.cloned.1.call-start = ((), (), s32[]{:S(2)}) async-start(), calls=%async_computation.10 | async-start | bytes 1179648 | tf_op jit(solution)/shard_map/all_gather | solution.py:420
  106.8 375.5 %copy-start.18 = (s32[1,1,64,8,32]{4,3,2,1,0:T(8,128)}, s32[1,1,64,8,32]{4,3,2,1,0:T(8,128)S(1)}, u32[]{:S(2)}) copy-start(s32[1,1,64,8,32]{4,3,2,1,0:T(8,128)S(1)} %copy.225) | copy-start | bytes 196612
  106.9 374.4 %copy-start.100 = (pred[64,8,32]{2,1,0:T(8,128)(4,1)}, pred[64,8,32]{2,1,0:T(8,128)(4,1)S(1)}, u32[]{:S(2)}) copy-start(pred[64,8,32]{2,1,0:T(8,128)(4,1)S(1)} %compare_and_fusion.1) | copy-start | bytes 49156
  555.1 228.4 %copy-start.107 = (bf16[64,1,8,128]{3,2,1,0:T(8,128)(2,1)S(1)}, bf16[64,1,8,128]{3,2,1,0:T(8,128)(2,1)}, u32[]{:S(2)}) copy-start(bf16[64,1,8,128]{3,2,1,0:T(8,128)(2,1)} %get-tuple-element.512) | copy-start | bytes 393220
  555.1 228.6 %copy-start.62 = (bf16[64,1,8,128]{3,2,1,0:T(8,128)(2,1)S(1)}, bf16[64,1,8,128]{3,2,1,0:T(8,128)(2,1)}, u32[]{:S(2)}) copy-start(bf16[64,1,8,128]{3,2,1,0:T(8,128)(2,1)} %copy-done.61) | copy-start | bytes 393220
  555.1 228.7 %copy-start.86 = (bf16[64,1,8,128]{3,2,1,0:T(8,128)(2,1)S(1)}, bf16[64,1,8,128]{3,2,1,0:T(8,128)(2,1)}, u32[]{:S(2)}) copy-start(bf16[64,1,8,128]{3,2,1,0:T(8,128)(2,1)} %get-tuple-element.516) | copy-start | bytes 393220
  555.2 229.7 %copy-start.109 = (bf16[64,1,8,128]{3,2,1,0:T(8,128)(2,1)S(1)}, bf16[64,1,8,128]{3,2,1,0:T(8,128)(2,1)}, u32[]{:S(2)}) copy-start(bf16[64,1,8,128]{3,2,1,0:T(8,128)(2,1)} %get-tuple-element.515) | copy-start | bytes 393220
  555.2 229.9 %copy-start.102 = (pred[64,8,32]{2,1,0:T(8,128)(4,1)S(1)}, pred[64,8,32]{2,1,0:T(8,128)(4,1)}, u32[]{:S(2)}) copy-start(pred[64,8,32]{2,1,0:T(8,128)(4,1)} %compare_and_fusion) | copy-start | bytes 49156
  904.6 522.4 %copy-start.9 = (f32[64,1024]{1,0:T(8,128)}, f32[64,1024]{1,0:T(8,128)S(1)}, u32[]{:S(2)}) copy-start(f32[64,1024]{1,0:T(8,128)S(1)} %get-tuple-element.563) | copy-start | bytes 786436
  907.4 519.6 %copy-start.11 = (f32[64,1024]{1,0:T(8,128)}, f32[64,1024]{1,0:T(8,128)S(1)}, u32[]{:S(2)}) copy-start(f32[64,1024]{1,0:T(8,128)S(1)} %get-tuple-element.567) | copy-start | bytes 786436
  913.0 500.3 %copy-start.13 = (f32[64,4096]{1,0:T(8,128)}, f32[64,4096]{1,0:T(8,128)S(1)}, u32[]{:S(2)}) copy-start(f32[64,4096]{1,0:T(8,128)S(1)} %fusion.311) | copy-start | bytes 3145732
  922.1 484.7 %copy-start.15 = (f32[64,4096]{1,0:T(8,128)}, f32[64,4096]{1,0:T(8,128)S(1)}, u32[]{:S(2)}) copy-start(f32[64,4096]{1,0:T(8,128)S(1)} %fusion.312) | copy-start | bytes 3145732
  925.3 226.4 %all-gather.34.cloned.1.call-start = ((), (), s32[]{:S(2)}) async-start(), calls=%async_computation.12 | async-start | bytes 1179648 | tf_op jit(solution)/shard_map/all_gather | solution.py:420
  1056.8 276.3 %reduce-scatter.21.cloned.1.call-start = ((), (), s32[]{:S(2)}) async-start(), calls=%async_computation.13 | async-start | bytes 2359296 | tf_op jit(solution)/shard_map/reduce_scatter | solution.py:440
  1268.4 135.4 %reduce-scatter.23.cloned.1.call-start = ((), (), s32[]{:S(2)}) async-start(), calls=%async_computation.14 | async-start | bytes 2359296 | tf_op jit(solution)/shard_map/reduce_scatter | solution.py:440
  1291.4 891.5 %all-gather.36.cloned.1.call-start = ((), (), s32[]{:S(2)}) async-start(), calls=%async_computation.15 | async-start | bytes 2359296 | tf_op jit(solution)/shard_map/all_gather | solution.py:454
  1454.8 231.9 %copy-start.22 = (s32[1,1,64,8,32]{4,3,2,1,0:T(8,128)S(1)}, s32[1,1,64,8,32]{4,3,2,1,0:T(8,128)}, u32[]{:S(2)}) copy-start(s32[1,1,64,8,32]{4,3,2,1,0:T(8,128)} %copy-done.20) | copy-start | bytes 196612
  1774.5 232.3 %copy-start.19 = (s32[1,1,64,8,32]{4,3,2,1,0:T(8,128)S(1)}, s32[1,1,64,8,32]{4,3,2,1,0:T(8,128)}, u32[]{:S(2)}) copy-start(s32[1,1,64,8,32]{4,3,2,1,0:T(8,128)} %copy-done.18) | copy-start | bytes 196612
  2102.4 100.8 %all-gather.38.cloned.1.call-start = ((), (), s32[]{:S(2)}) async-start(), calls=%async_computation.16 | async-start | bytes 2359296 | tf_op jit(solution)/shard_map/all_gather | solution.py:454
  2139.5 129.3 %all-reduce.15.cloned.1.call-start = ((), (), s32[]{:S(2)}) async-start(), calls=%async_computation.17 | async-start | bytes 262144 | tf_op jit(solution)/shard_map/psum | solution.py:466
  2238.6 1513.6 %all-reduce.21.cloned.1.call-start = ((), (), s32[]{:S(2)}) async-start(), calls=%async_computation.20 | async-start | bytes 100663296
  2243.9 1517.4 %copy-start.56 = (f32[1,1,4,32,3072]{4,3,2,1,0:T(8,128)S(1)}, f32[1,1,4,32,3072]{4,3,2,1,0:T(8,128)}, u32[]{:S(2)}) copy-start(f32[1,1,4,32,3072]{4,3,2,1,0:T(8,128)} %param.53) | copy-start | bytes 4718596
  2243.9 1723.8 %all-reduce.17.cloned.1.call-start = ((), (), s32[]{:S(2)}) async-start(), calls=%async_computation.18 | async-start | bytes 196608 | tf_op jit(solution)/shard_map/psum | solution.py:487
  3849.6 249.4 %all-reduce.19.cloned.1.call-start = ((), (), s32[]{:S(2)}) async-start(), calls=%async_computation.19 | async-start | bytes 458752 | tf_op jit(solution)/shard_map/psum | solution.py:487
  (192 other events, 5551.8 us)
Sparse Core Ops, SparseCore 0:
  12.0 59.8 all-gather.21
  92.6 74.6 reduce-scatter.18
  171.7 63.9 reduce-scatter.16
  925.4 40.6 all-gather.31
  1056.9 38.0 all-gather.33
  1268.6 64.4 reduce-scatter.20
  1337.2 66.6 reduce-scatter.22
  2102.5 50.2 all-gather.35
  2155.4 47.7 all-gather.37
  2238.8 29.9 all-reduce.14
  2274.4 1477.8 all-reduce.20
Sparse Core Ops, SparseCore 1:
  96.5 67.1 all-gather.23
  167.1 56.9 all-gather.25
  227.5 76.4 all-gather.27
  307.5 76.0 all-gather.29
  3849.7 118.0 all-reduce.16
  3974.8 124.0 all-reduce.18
where the time goes:
time: 4230 us; the launch traced here: 4190 us
  waiting for transfers between devices  1940 us (46%)
  local copies, waits for them, and re-layouts  980 us (23%)
  blocking collectives  443 us (10%)
  other arithmetic  416 us (10%)
  matrix products  382 us (9%)
    unnamed x18, waiting for transfers between devices  1480 us
    gather x10, local copies, waits for them, and re-layouts, pick_entries(): return jnp.take_along_axis(entry_listing, mem_picks, axis=2)  909 us
    reduce_sum x4, other arithmetic, spread_entries(): jnp.sum(jnp.where(mem_picks[..., None] == slots, entry_weights[..., None]...  252 us
    psum x2, waiting for transfers between devices, shards(): lax.psum((precise_outer(moved_slabs[0], orthos[0]), precise_outer(moved_s...  213 us
    all_gather x6, blocking collectives, combined_all(): everything = jax.tree.map(lambda part: lax.all_gather(part, axis), array)  157 us
    reduce_scatter x2, waiting for transfers between devices, shards(): lax.psum_scatter(picked_rows, 'shard', scatter_dimension=0, tiled=True)  121 us
    dot_general x10, matrix products, matmul_outer(): lax.dot_general(left, right, (((0,), (0,)), ((), ())), preferred_element_...  100 us
    reduce_scatter x2, waiting for transfers between devices, shards(): lax.psum_scatter(matmul(logit_grad, vocab_local), 'shard', scatter_dimens...  97.1 us
  transfers between devices with their start and end apart: 17, of which 9 were waited for; matrix products, arithmetic and copies ran while one was open for 21% of the time, Pallas kernels for 0%

commit v1 on v0

v1 whole, which is shorter than its diff:
```python
import functools
import math

import jax
import jax.numpy as jnp
from jax import lax
from jax.experimental import pallas as pl
from jax.experimental.pallas import tpu as pltpu
from jax.sharding import PartitionSpec as P

HEADS = 8
RANK = 8
LANES = 128
EPSILON = 1e-06
MOMENTUM = 0.9
LEARN_RATE = 5000.0
CLIP_LEVEL = 0.02
F32 = jnp.float32
BF16 = jnp.bfloat16
FINE = lax.Precision.HIGHEST


def dot_over(left, right, left_dim, right_dim, precision=None):
    return lax.dot_general(
        left,
        right,
        (((left_dim,), (right_dim,)), ((), ())),
        precision=precision,
        preferred_element_type=F32,
    )


def matmul(left, right):
    return dot_over(left, right, 1, 0)


def matmul_back(left, right):
    return dot_over(left, right, 1, 1)


def matmul_outer(left, right):
    return dot_over(left, right, 0, 0)


def three_parts(values):
    first = lax.reduce_precision(values, 8, 7)
    rest = values - first
    second = lax.reduce_precision(rest, 8, 7)
    third = rest - second
    return [first.astype(BF16), second.astype(BF16), third.astype(BF16)]


def rows_by_narrow(rows, narrow, narrow_dim):
    stacked = jnp.concatenate(three_parts(rows), axis=0)
    wide = dot_over(stacked, narrow, 1, narrow_dim)
    count = rows.shape[0]
    return wide[:count] + (wide[count : 2 * count] + wide[2 * count :])


def swap(array, axis, bit):
    size = lax.axis_size(axis)
    return lax.ppermute(array, axis, [(i, i ^ bit) for i in range(size)])


def bits_of(axis):
    size = lax.axis_size(axis)
    return [1 << k for k in range(size.bit_length() - 1)]


def two_orders(axis):
    bits = bits_of(axis)
    return bits, ([bits[1], bits[0]] + bits[2:] if len(bits) > 1 else bits)


def scatter_sum(blocks, axis, order):
    indices = list(range(blocks.shape[0]))
    for bit in order:
        away = [k for k, j in enumerate(indices) if j & bit]
        kept = [k for k, j in enumerate(indices) if not j & bit]
        arrived = swap(jnp.stack([blocks[k] for k in away]), axis, bit)
        blocks = jnp.stack([blocks[k] for k in kept]) + arrived
        indices = [indices[k] for k in kept]
    return blocks[0]


def scatter_sum_halves(blocks, axis):
    half = blocks.shape[-1] // 2
    first, second = two_orders(axis)
    return jnp.concatenate(
        [
            scatter_sum(blocks[..., :half], axis, first),
            scatter_sum(blocks[..., half:], axis, second),
        ],
        axis=-1,
    )


def gather_blocks(block, axis, order):
    current, indices = block[None], [0]
    for bit in order:
        current = jnp.concatenate([current, swap(current, axis, bit)], axis=0)
        indices = indices + [j ^ bit for j in indices]
    return [current[indices.index(j)] for j in range(len(indices))]


def gather_halves(block, axis):
    half = block.shape[-1] // 2
    first, second = two_orders(axis)
    left = gather_blocks(block[..., :half], axis, first[::-1])
    right = gather_blocks(block[..., half:], axis, second[::-1])
    return jnp.concatenate(
        [jnp.concatenate(left, axis=0), jnp.concatenate(right, axis=0)], axis=-1
    )


def sum_over(array, axis):
    for bit in bits_of(axis):
        array = array + swap(array, axis, bit)
    return array


def spread_small(array, axis):
    size = lax.axis_size(axis)
    copies = jnp.broadcast_to(array[None], (size,) + array.shape)
    return lax.all_to_all(copies, axis, 0, 0, tiled=False)


def norm_rows(values, gain):
    inverse = lax.rsqrt(jnp.mean(values * values, axis=-1, keepdims=True) + EPSILON)
    return (values * inverse * gain, inverse)


def norm_back(values, inverse, gain, upstream):
    scaled = upstream * gain
    gain_part = jnp.sum(upstream * values * inverse, axis=0)
    result = inverse * scaled - values * inverse**3 * jnp.mean(
        scaled * values, axis=-1, keepdims=True
    )
    return (result, gain_part)


def local_probs(queries, keys, length, scale):
    rows = queries.shape[0]
    scores = matmul_back(queries, keys) * scale
    row = lax.broadcasted_iota(jnp.int32, (rows, rows), 0)
    column = lax.broadcasted_iota(jnp.int32, (rows, rows), 1)
    allowed = (row >= column) & (row // length == column // length)
    scores = jnp.where(allowed, scores, -1e30)
    powers = jnp.exp(scores - jnp.max(scores, axis=-1, keepdims=True))
    return powers / jnp.sum(powers, axis=-1, keepdims=True)


def attend_kernel(
    length,
    queries_ref,
    keys_ref,
    values_ref,
    mem_keys_ref,
    mem_values_ref,
    block_ref,
    lane_ref,
    opening_ref,
    attended_ref,
    difference_ref,
    weights_ref,
    scores_ref,
    rounded_ref,
):
    queries = queries_ref[...]
    tokens, width = queries.shape
    slots = mem_keys_ref.shape[2]
    lane_blocks = slots // LANES
    scale = width ** (-0.5)
    scores_ref[...] = matmul_back(queries, mem_keys_ref[0, 0]) * scale

    def group(at, carry):
        rows = pl.ds(pl.multiple_of(at * 8, 8), 8)
        picks = block_ref.shape[2]
        block_hot = (
            lax.broadcasted_iota(jnp.int32, (lane_blocks * 8, picks), 0)
            == block_ref[0, pl.ds(at, 1), :]
        )
        lane_hot = (
            lax.broadcasted_iota(jnp.int32, (LANES, picks), 0) == lane_ref[0, pl.ds(at, 1), :]
        )
        counts = matmul_back(
            jnp.where(block_hot, 1.0, 0.0).astype(BF16), jnp.where(lane_hot, 1.0, 0.0).astype(BF16)
        )
        counts = jnp.concatenate([counts[k * 8 : k * 8 + 8] for k in range(lane_blocks)], axis=1)
        scores = jnp.where(counts > 0.0, scores_ref[rows, :], -1e30)
        powers = jnp.exp(scores - jnp.max(scores, axis=-1, keepdims=True))
        total = jnp.sum(powers * counts, axis=-1, keepdims=True)
        probs = powers * (1.0 / total)
        weights_ref[0, rows, :] = probs * counts
        rounded_ref[rows, :] = probs.astype(BF16).astype(F32) * counts
        return carry

    lax.fori_loop(0, tokens // 8, group, 0)
    memory_out = matmul(rounded_ref[...].astype(BF16), mem_values_ref[0, 0])
    probs = local_probs(queries, keys_ref[...], length, scale)
    local_out = matmul(probs.astype(BF16), values_ref[...])
    opening = opening_ref[...]
    attended_ref[...] = (opening * memory_out + (1.0 - opening) * local_out).astype(BF16)
    difference_ref[...] = memory_out - local_out


def attend_back_kernel(
    length,
    queries_ref,
    keys_ref,
    values_ref,
    mem_keys_ref,
    mem_values_ref,
    weights_ref,
    upstream_ref,
    difference_ref,
    opening_ref,
    query_ref,
    key_ref,
    value_ref,
    gate_ref,
    slope_ref,
):
    queries, keys, values = queries_ref[...], keys_ref[...], values_ref[...]
    tokens, width = queries.shape
    scale = width ** (-0.5)
    opening = opening_ref[...]
    upstream = upstream_ref[...]
    gate_ref[...] = jnp.sum(upstream * difference_ref[...], axis=0, keepdims=True)
    memory_up = (opening * upstream).astype(BF16)
    local_up = ((1.0 - opening) * upstream).astype(BF16)
    slope_ref[...] = matmul_back(memory_up, mem_values_ref[0, 0])

    def group(at, carry):
        rows = pl.ds(pl.multiple_of(at * 8, 8), 8)
        weights, slope = weights_ref[0, rows, :], slope_ref[rows, :]
        middle = jnp.sum(weights * slope, axis=-1, keepdims=True)
        slope_ref[rows, :] = weights * (slope - middle)
        return carry

    lax.fori_loop(0, tokens // 8, group, 0)
    memory_part = matmul(slope_ref[...].astype(BF16), mem_keys_ref[0, 0])
    probs = local_probs(queries, keys, length, scale)
    slope = matmul_back(local_up, values)
    slope = (probs * (slope - jnp.sum(probs * slope, axis=-1, keepdims=True))).astype(BF16)
    query_ref[...] = ((matmul(slope, keys) + memory_part) * scale).astype(BF16)
    key_ref[...] = (matmul_outer(slope, queries) * scale).astype(BF16)
    value_ref[...] = matmul_outer(probs.astype(BF16), local_up).astype(BF16)


def head_specs(tokens, width, slots):
    column = [
        pl.BlockSpec((tokens, width), functools.partial(lambda part, h: (0, part * HEADS + h), part))
        for part in range(3)
    ]
    store = [
        pl.BlockSpec((1, 1, slots, width), functools.partial(lambda part, h: (part, h, 0, 0), part))
        for part in range(2)
    ]
    return column, store


def attend(projected, memory, block_codes, lane_codes, opening_row, length):
    tokens = projected.shape[0]
    width = memory.shape[3]
    slots = memory.shape[2]
    column, store = head_specs(tokens, width, slots)
    codes = pl.BlockSpec((1,) + block_codes.shape[1:], lambda h: (h, 0, 0))
    head = pl.BlockSpec((tokens, width), lambda h: (0, h))
    return pl.pallas_call(
        functools.partial(attend_kernel, length),
        grid=(HEADS,),
        in_specs=column + store + [codes, codes, pl.BlockSpec((1, width), lambda h: (0, h))],
        out_specs=[head, head, pl.BlockSpec((1, tokens, slots), lambda h: (h, 0, 0))],
        out_shape=[
            jax.ShapeDtypeStruct((tokens, HEADS * width), BF16),
            jax.ShapeDtypeStruct((tokens, HEADS * width), F32),
            jax.ShapeDtypeStruct((HEADS, tokens, slots), F32),
        ],
        scratch_shapes=[pltpu.VMEM((tokens, slots), F32), pltpu.VMEM((tokens, slots), F32)],
        compiler_params=pltpu.CompilerParams(vmem_limit_bytes=40 * 2**20),
        cost_estimate=pl.CostEstimate(
            flops=5 * HEADS * tokens * slots * width,
            bytes_accessed=4 * HEADS * slots * (width + tokens),
            transcendentals=HEADS * tokens * slots,
        ),
        name="attend",
    )(projected, projected, projected, memory, memory, block_codes, lane_codes, opening_row)


def attend_back(projected, memory, weights, upstream, difference, opening_row, length):
    tokens = projected.shape[0]
    width = memory.shape[3]
    slots = memory.shape[2]
    column, store = head_specs(tokens, width, slots)
    head = pl.BlockSpec((tokens, width), lambda h: (0, h))
    row = pl.BlockSpec((1, width), lambda h: (0, h))
    return pl.pallas_call(
        functools.partial(attend_back_kernel, length),
        grid=(HEADS,),
        in_specs=column
        + store
        + [pl.BlockSpec((1, tokens, slots), lambda h: (h, 0, 0)), head, head, row],
        out_specs=[head, head, head, row],
        out_shape=[jax.ShapeDtypeStruct((tokens, HEADS * width), BF16)] * 3
        + [jax.ShapeDtypeStruct((1, HEADS * width), F32)],
        scratch_shapes=[pltpu.VMEM((tokens, slots), F32)],
        compiler_params=pltpu.CompilerParams(vmem_limit_bytes=40 * 2**20),
        cost_estimate=pl.CostEstimate(
            flops=4 * HEADS * tokens * slots * width,
            bytes_accessed=4 * HEADS * slots * (width + tokens),
            transcendentals=0,
        ),
        name="attend_back",
    )(projected, projected, projected, memory, memory, weights, upstream, difference, opening_row)


def shards(
    token_ids,
    targets,
    valid_mask,
    mem_index,
    memory,
    w_qkv,
    w_out,
    w_up,
    w_down,
    embed_table,
    gain_vector,
    mom_qkv,
    mom_out,
    mom_up,
    mom_down,
    mom_table,
    mom_gains,
    err_qkv,
    err_out,
    err_up,
    err_down,
    err_table,
    fac_qkv,
    fac_out,
    fac_up,
    fac_down,
    fac_table,
):
    rep_count = lax.axis_size("rep")
    shard_count = lax.axis_size("shard")
    rep_at = lax.axis_index("rep")
    shard_at = lax.axis_index("shard")
    micro_count, length = token_ids.shape[1:]
    tokens = micro_count * length
    model_width = w_out.shape[1]
    block_rows = embed_table.shape[0]
    masters = (w_qkv, w_out, w_up, w_down, embed_table, gain_vector)
    errors = (err_qkv, err_out, err_up, err_down, err_table)
    factors = (fac_qkv, fac_out, fac_up, fac_down, fac_table)
    relative = shard_at ^ jnp.arange(shard_count)

    own_rows = jnp.stack(
        [token_ids.reshape(tokens), targets.reshape(tokens), valid_mask.reshape(tokens)]
    )
    group_rows = jnp.take(spread_small(own_rows, "shard"), relative, axis=0)
    group_ids = group_rows[:, 0].reshape(-1)
    group_targets = group_rows[:, 1].reshape(-1)
    group_valid = group_rows[:, 2].reshape(-1).astype(F32)
    valid_count = sum_over(jnp.full((8, LANES), jnp.sum(group_valid)), "rep")[0, 0]

    vocab = lax.all_gather(embed_table.astype(BF16), "rep", axis=0, tiled=True)
    vocab_rows = vocab.shape[0]
    qkv_weight, out_weight, up_weight, down_weight = [
        lax.all_gather(matrix.astype(BF16), ("rep", "shard"), axis=0, tiled=True)
        for matrix in masters[:4]
    ]

    flat_errors = [error.reshape(-1, error.shape[-1]) for error in errors]
    error_left = [
        dot_over(factor, error, 0, 1, FINE) for factor, error in zip(factors, flat_errors)
    ]

    vocab_slots = jnp.arange(vocab_rows)

    def hits(id_values):
        block_index = id_values // block_rows
        column = block_index // shard_count * block_rows + id_values % block_rows
        column = jnp.where(block_index % shard_count == shard_at, column, -1)
        return column[:, None] == vocab_slots[None, :]

    token_hot = hits(group_ids).astype(BF16)
    embed_scale = math.sqrt(model_width)
    picked_rows = matmul(token_hot, vocab).astype(BF16)
    start_rows = embed_scale * scatter_sum_halves(
        picked_rows.reshape(shard_count, tokens, model_width), "shard"
    ).astype(F32)

    gain_attn = gain_vector[:model_width]
    gain_mlp = gain_vector[model_width : 2 * model_width]
    gain_final = gain_vector[2 * model_width : 3 * model_width]
    opening = jax.nn.sigmoid(gain_vector[3 * model_width :])
    head_width = model_width // HEADS
    opening_row = jnp.repeat(opening, head_width)[None]
    picks = jnp.transpose(mem_index.reshape(tokens, HEADS, -1), (1, 0, 2))
    picks = picks.reshape(HEADS, tokens // 8, -1)
    token_of_pick = jnp.arange(picks.shape[2]) // mem_index.shape[-1]
    block_codes = picks // LANES * 8 + token_of_pick
    lane_codes = picks % LANES

    normed_one, inverse_one = norm_rows(start_rows, gain_attn)
    hidden_one = normed_one.astype(BF16)
    projected = matmul(hidden_one, qkv_weight).astype(BF16)
    attended, difference, mem_weights = attend(
        projected, memory, block_codes, lane_codes, opening_row, length
    )
    after_attn = start_rows + matmul(attended, out_weight)
    normed_two, inverse_two = norm_rows(after_attn, gain_mlp)
    hidden_two = normed_two.astype(BF16)
    up_value = matmul(hidden_two, up_weight)
    activated = jax.nn.gelu(up_value).astype(BF16)
    after_mlp = after_attn + matmul(activated, down_weight)
    final_norm, final_inverse = norm_rows(after_mlp, gain_final)

    final_all = gather_halves(final_norm.astype(BF16), "shard")
    logits = matmul_back(final_all, vocab)
    target_hit = hits(group_targets)
    peak_value = jnp.max(logits, axis=-1)
    exp_total = jnp.sum(jnp.exp(logits - peak_value[:, None]), axis=-1)
    picked_logit = jnp.sum(jnp.where(target_hit, logits, 0.0), axis=-1)
    for bit in bits_of("shard"):
        mine = jnp.stack([peak_value, exp_total, picked_logit])
        theirs = swap(mine, "shard", bit).reshape(3, shard_count, tokens)
        theirs = jnp.concatenate([theirs[:, j ^ bit] for j in range(shard_count)], axis=1)
        new_peak = jnp.maximum(peak_value, theirs[0])
        exp_total = exp_total * jnp.exp(peak_value - new_peak) + theirs[1] * jnp.exp(
            theirs[0] - new_peak
        )
        peak_value, picked_logit = new_peak, picked_logit + theirs[2]
    log_total = peak_value + jnp.log(exp_total)
    loss_own = jnp.sum((group_valid * (log_total - picked_logit))[:tokens])
    logit_grad = (
        (jnp.exp(logits - log_total[:, None]) - target_hit.astype(F32))
        * (group_valid / valid_count)[:, None]
    ).astype(BF16)
    final_grad = scatter_sum_halves(
        matmul(logit_grad, vocab).reshape(shard_count, tokens, model_width), "shard"
    )

    mlp_grad, gain_final_grad = norm_back(after_mlp, final_inverse, gain_final, final_grad)
    down_in = mlp_grad.astype(BF16)
    act_grad = matmul_back(down_in, down_weight)
    unused_value, gelu_pull = jax.vjp(jax.nn.gelu, up_value)
    up_in = gelu_pull(act_grad)[0].astype(BF16)
    norm_two_grad, gain_mlp_grad = norm_back(
        after_attn, inverse_two, gain_mlp, matmul_back(up_in, up_weight)
    )
    attn_grad = mlp_grad + norm_two_grad
    out_in = attn_grad.astype(BF16)
    mixture_grad = matmul_back(out_in, out_weight)
    query_in, key_in, value_in, gate_row = attend_back(
        projected, memory, mem_weights, mixture_grad, difference, opening_row, length
    )
    gate_grad = jnp.sum(gate_row.reshape(HEADS, head_width), axis=1) * opening * (1.0 - opening)
    qkv_in = jnp.concatenate([query_in, key_in, value_in], axis=1)
    norm_one_grad, gain_attn_grad = norm_back(
        start_rows, inverse_one, gain_attn, matmul_back(qkv_in, qkv_weight)
    )
    start_grad = embed_scale * (attn_grad + norm_one_grad)
    gain_grad = jnp.concatenate([gain_attn_grad, gain_mlp_grad, gain_final_grad, gate_grad])

    lefts = (hidden_one, attended, hidden_two, activated)
    rights = (qkv_in, out_in, up_in, down_in)

    heights = [left.shape[1] // (rep_count * shard_count) for left in lefts]
    by_owner = jnp.concatenate(
        [
            left.reshape(tokens, rep_count, shard_count, height)
            .transpose(2, 0, 1, 3)
            .reshape(shard_count, tokens, rep_count * height)
            for left, height in zip(lefts, heights)
        ],
        axis=2,
    )
    own_columns = jnp.stack(
        [
            swap(lax.dynamic_index_in_dim(by_owner, shard_at ^ j, 0, False), "shard", j)
            if j
            else lax.dynamic_index_in_dim(by_owner, shard_at, 0, False)
            for j in range(shard_count)
        ]
    )
    own_columns = jnp.take(own_columns, relative, axis=0).reshape(shard_count * tokens, -1)
    rights_all = [lax.all_gather(right, "shard", axis=0, tiled=True) for right in rights]
    slab_widths = [rep_count * height for height in heights]
    starts = [sum(slab_widths[:k]) for k in range(5)]

    left_blocks = []
    for left, right, factor, height in zip(lefts, rights, factors, heights):
        narrowed = rows_by_narrow(factor.T, right, 1)
        part = rows_by_narrow(narrowed, left, 0)
        part = part.reshape(RANK, rep_count, shard_count, height).transpose(2, 0, 1, 3)
        left_blocks.append(part.reshape(shard_count, RANK, rep_count * height))
    left_blocks = jnp.take(jnp.concatenate(left_blocks, axis=2), relative, axis=0)
    own_left = scatter_sum(left_blocks, "shard", bits_of("shard"))
    own_left = own_left + jnp.concatenate(error_left[:4], axis=1)
    start_narrow = dot_over(fac_table, start_grad, 0, 1, FINE)
    start_narrow = jnp.concatenate(
        gather_blocks(start_narrow, "shard", bits_of("shard")[::-1]), axis=1
    )
    final_narrow = rows_by_narrow(fac_table.T, final_all, 1)
    table_left = (
        error_left[4]
        + rows_by_narrow(final_narrow, logit_grad, 0)
        + rows_by_narrow(start_narrow, token_hot, 0)
    )
    left_sum = sum_over(jnp.concatenate([own_left, table_left], axis=1), "rep")
    own_left, table_left = left_sum[:, : starts[4]], left_sum[:, starts[4] :]
    table_gram = dot_over(table_left, table_left, 1, 1, FINE)
    payload = jnp.concatenate([own_left, jnp.pad(table_gram, ((0, 0), (0, LANES - RANK)))], axis=1)
    payloads = jnp.stack(gather_blocks(payload, "shard", bits_of("shard")[::-1]))
    table_gram = jnp.sum(payloads[:, :, starts[4] : starts[4] + RANK], axis=0)
    everyone = jnp.take(payloads[:, :, : starts[4]], relative, axis=0)
    full_lefts = [
        everyone[:, :, starts[k] : starts[k + 1]]
        .reshape(shard_count, RANK, rep_count, heights[k])
        .transpose(1, 2, 0, 3)
        .reshape(RANK, -1)
        for k in range(4)
    ]
    grams = jnp.stack(
        [dot_over(full, full, 1, 1, FINE) for full in full_lefts] + [table_gram]
    )
    lower_tri = jnp.linalg.cholesky(grams)
    inverse_tri = lax.linalg.triangular_solve(
        lower_tri,
        jnp.broadcast_to(jnp.eye(RANK, dtype=F32), grams.shape),
        left_side=True,
        lower=True,
    )
    full_orthos = [dot_over(inverse_tri[k], full_lefts[k], 1, 0, FINE) for k in range(4)]
    slab_orthos = [
        dot_over(inverse_tri[k], own_left[:, starts[k] : starts[k + 1]], 1, 0, FINE)
        for k in range(4)
    ] + [dot_over(inverse_tri[4], table_left, 1, 0, FINE)]

    start_all = gather_halves(start_grad.astype(BF16), "shard")
    moved_table = (
        matmul_outer(logit_grad, final_all) + matmul_outer(token_hot, start_all) + flat_errors[4]
    )

    rights_sum = []
    for k in range(4):
        narrowed = rows_by_narrow(full_orthos[k], lefts[k], 1)
        rights_sum.append(
            rows_by_narrow(narrowed, rights[k], 0)
            + dot_over(slab_orthos[k], flat_errors[k], 1, 0, FINE)
        )
    rights_sum.append(dot_over(slab_orthos[4], moved_table, 1, 0, FINE))
    table_square = dot_over(slab_orthos[4], slab_orthos[4], 1, 1, FINE)
    extra = jnp.concatenate([gain_grad, loss_own[None], table_square.reshape(-1)])
    widths = [right.shape[1] for right in rights_sum]
    total_width = sum(widths) + -(-extra.shape[0] // RANK)
    piece = -(-total_width // (shard_count * LANES)) * LANES
    extra_width = piece * shard_count - sum(widths)
    extra = jnp.pad(extra, (0, extra_width * RANK - extra.shape[0])).reshape(RANK, extra_width)
    pieces = jnp.concatenate(rights_sum + [extra], axis=1)
    pieces = pieces.reshape(RANK, shard_count, piece).transpose(1, 0, 2)
    own_piece = scatter_sum(jnp.take(pieces, relative, axis=0), "shard", bits_of("shard"))
    own_piece = sum_over(own_piece, "rep")
    pieces = jnp.stack(gather_blocks(own_piece, "shard", bits_of("shard")[::-1]))
    pieces = jnp.take(pieces, relative, axis=0).transpose(1, 0, 2).reshape(RANK, -1)
    right_sums = [pieces[:, sum(widths[:k]) : sum(widths[: k + 1])] for k in range(5)]
    extra = pieces[:, sum(widths) :].reshape(-1)
    gain_count = gain_grad.shape[0]
    gain_sum, loss_sum = extra[:gain_count], extra[gain_count]
    table_square = extra[gain_count + 1 : gain_count + 1 + RANK * RANK].reshape(RANK, RANK)
    squares = [dot_over(full, full, 1, 1, FINE) for full in full_orthos]
    squares.append(table_square / rep_count)
    square_total = jnp.sum(gain_sum * gain_sum)
    for square, right in zip(squares, right_sums):
        square_total = square_total + jnp.sum(dot_over(square, right, 1, 0, FINE) * right)
    clip_norm = jnp.sqrt(square_total)
    shrink = jnp.minimum(1.0, CLIP_LEVEL / clip_norm)

    new_errors, own_blocks = [], []
    for k in range(5):
        if k < 4:
            columns = own_columns[:, starts[k] : starts[k + 1]]
            moved = matmul_outer(columns, rights_all[k]) + flat_errors[k]
        else:
            moved = moved_table
        approx = dot_over(slab_orthos[k], right_sums[k], 0, 0, FINE)
        new_errors.append((moved - approx).reshape(errors[k].shape))
        height = approx.shape[0] // rep_count
        own_blocks.append(lax.dynamic_slice_in_dim(approx, rep_at * height, height, 0))
    gradients = own_blocks + [gain_sum]
    moments = (mom_qkv, mom_out, mom_up, mom_down, mom_table, mom_gains)
    new_moments = [MOMENTUM * moments[k] + shrink * gradients[k] for k in range(6)]
    new_weights = [masters[k] - LEARN_RATE * new_moments[k] for k in range(6)]
    return (
        loss_sum,
        valid_count,
        clip_norm,
        *new_moments,
        *new_weights,
        *new_errors,
        *[right.T for right in right_sums],
    )


def solution(mesh):
    everyone = P(("rep", "shard"), None)
    group = P("rep", None, "shard")
    buffer = P("rep", "shard", None, None, None)
    return jax.shard_map(
        shards,
        mesh=mesh,
        in_specs=(group,) * 3
        + (P("rep", None, "shard", None, None), P())
        + (everyone,) * 5
        + (P(),)
        + (everyone,) * 5
        + (P(),)
        + (buffer,) * 5
        + (P(),) * 5,
        out_specs=(P(),) * 3
        + (everyone,) * 5
        + (P(),)
        + (everyone,) * 5
        + (P(),)
        + (buffer,) * 5
        + (P(),) * 5,
        check_vma=False,
    )
```

time: 4230 us -> 1000 us (0.24)
  waiting for transfers between devices: 1940 us -> 400 us
  local copies, waits for them, and re-layouts: 980 us -> 71.5 us
  blocking collectives: 443 us -> 0 us
  other arithmetic: 416 us -> 90.6 us
  matrix products: 382 us -> 248 us
  Pallas kernels: 0 us -> 99.2 us
  starting transfers between devices: 1.85 us -> 64.4 us
    unnamed x18 -> x9, waiting for transfers between devices: 1480 us -> 0.16 us
    gather x12 -> x7, local copies, waits for them, and re-layouts: 923 us -> 11 us  [the longest x2 7.63 us: shards(): jnp.take(own_columns, relative, axis=0).reshape(shard_count * tokens, -1)]
    all_gather x9 -> x0, blocking collectives: 356 us -> none  [the longest x6 157 us: combined_all(): everything = jax.tree.map(lambda part: lax.all_gather(part, axis), array)]
    reduce_sum x16 -> x6, other arithmetic: 268 us -> 18 us  [the longest x1 15.3 us: shards(): exp_total = jnp.sum(jnp.exp(logits - peak_value[:, None]), axis=-1)]
    psum x3 -> x0, waiting for transfers between devices: 234 us -> none  [the longest x2 213 us: shards(): lax.psum((precise_outer(moved_slabs[0], orthos[0]), precise_outer(moved_s...]
    reduce_scatter x4 -> x0, waiting for transfers between devices: 218 us -> none  [the longest x2 121 us: shards(): lax.psum_scatter(picked_rows, 'shard', scatter_dimension=0, tiled=True)]
    all_gather x9, waiting for transfers between devices: 2.55 us -> 209 us  [the longest x4 155 us: shards(): lax.all_gather(matrix.astype(BF16), ('rep', 'shard'), axis=0, tiled=True)]
    ppermute x0 -> x55, waiting for transfers between devices: none -> 191 us  [swap(): return lax.ppermute(array, axis, [(i, i ^ bit) for i in range(size)])]
  transfers between devices with their start and end apart: 17 -> 65, of which waited for: 9 -> 37; matrix products, arithmetic and copies ran while one was open for 21% -> 40% of each run, Pallas kernels for 0% -> 10%
where the time goes in v1:
time: 1000 us; the launch traced here: 996 us
  waiting for transfers between devices  400 us (40%)
  matrix products  248 us (25%)
  Pallas kernels  99.2 us (10%)
  other arithmetic  90.6 us (9%)
  local copies, waits for them, and re-layouts  71.5 us (7%)
  starting transfers between devices  64.4 us (6%)
  between operations  22.3 us (2%)
    dot_general x76, matrix products, dot_over(): lax.dot_general(left, right, (((left_dim,), (right_dim,)), ((), ())), pre...  248 us
    ppermute x55, waiting for transfers between devices, swap(): return lax.ppermute(array, axis, [(i, i ^ bit) for i in range(size)])  191 us
    all_gather x4, waiting for transfers between devices, shards(): lax.all_gather(matrix.astype(BF16), ('rep', 'shard'), axis=0, tiled=True)  155 us
    pallas_call x1, Pallas kernels, attend(): pl.pallas_call(functools.partial(attend_kernel, length), grid=(HEADS,), i...  69.4 us
    ppermute x55, starting transfers between devices, swap(): return lax.ppermute(array, axis, [(i, i ^ bit) for i in range(size)])  56.7 us
    pallas_call x1, Pallas kernels, attend_back(): pl.pallas_call(functools.partial(attend_back_kernel, length), grid=(HEADS...  29.8 us
    all_gather x1, waiting for transfers between devices, shards(): vocab = lax.all_gather(embed_table.astype(BF16), 'rep', axis=0, tiled=True)  29.2 us
    unnamed x343, local copies, waits for them, and re-layouts  28.3 us
  transfers between devices with their start and end apart: 65, of which 37 were waited for; matrix products, arithmetic and copies ran while one was open for 40% of the time, Pallas kernels for 10%

profile of v1, /device:TPU:0, one launch (start us, length us, event | category | flops | bytes accessed | tf_op | source)
XLA Modules:
  0.0 996.0 jit_solution(15356610949986902383)
XLA Ops:
  16.1 7.3 all-to-all-start
  41.9 29.2 %all-gather.10.cloned.1.call-done = bf16[4000,1024]{1,0:T(8,128)(2,1)} async-done(((bf16[1000,1024]{1,0:T(8,128)(2,1)}), bf16[4000,1024]{1,0:T(8,128)(2,1)}) %all-gather.10.cloned.1.call-update) | async-done | bytes 8192016 | tf_op jit(solution)/shard_map/all_gather | solution.py:369
  71.1 11.4 %fusion.21 = bf16[1024,1024]{1,0:T(8,128)(2,1)S(1)} fusion(bf16[4000,1024]{1,0:T(8,128)(2,1)} %all-gather.10.cloned.1.call-done, s32[1024]{0:T(1024)S(1)} %get-tuple-element.274), kind=kOutput, calls=%fused_computation.48 | convolution fusion | flops 8393752576 | bytes 10293248 | tf_op jit(solution)/shard_map/dot_general | solution.py:24
  91.2 10.6 %collective-permute-done.3 = bf16[4,128,512]{2,1,0:T(8,128)(2,1)S(1)} collective-permute-done((bf16[4,128,512]{2,1,0:T(8,128)(2,1)S(1)}, bf16[4,128,512]{2,1,0:T(8,128)(2,1)S(1)}, u32[]{:S(2)}, u32[]{:S(2)}) %collective-permute-start.3) | collective-permute-done | bytes 524320 | tf_op jit(solution)/shard_map/ppermute | solution.py:62
  129.6 20.5 %all-gather.12.cloned.1.call-done = bf16[1024,3072]{1,0:T(8,128)(2,1)} async-done(((bf16[32,3072]{1,0:T(8,128)(2,1)}), bf16[1024,3072]{1,0:T(8,128)(2,1)}) %all-gather.12.cloned.1.call-update) | async-done | bytes 6291472 | tf_op jit(solution)/shard_map/all_gather | solution.py:372
  154.0 69.4 %attend.1 = (bf16[128,1024]{1,0:T(8,128)(2,1)S(1)}, f32[128,1024]{1,0:T(8,128)S(1)}, f32[8,128,4096]{2,1,0:T(8,128)}) custom-call(bf16[128,3072]{1,0:T(8,128)(2,1)S(1)} %convolution_convert_fusion.queries_ref.keys_ref.values_ref, bf16[128,3072]{1,0:T(8,128)(2,1)S(1)} %convolution_convert_fusion.queries_ref.keys_ref.values_ref, ...), custom_call_target="tpu_custom_call" | custom-call | flops 2684354560 | bytes 33554432 | tf_op jit(solution)/shard_map/attend/pallas_call | solution.py:270
  227.0 62.2 %all-gather.16.cloned.1.call-done = bf16[1024,4096]{1,0:T(8,128)(2,1)} async-done(((bf16[32,4096]{1,0:T(8,128)(2,1)}), bf16[1024,4096]{1,0:T(8,128)(2,1)}) %all-gather.16.cloned.1.call-update) | async-done | bytes 8388624 | tf_op jit(solution)/shard_map/all_gather | solution.py:372
  289.1 6.6 multiply_convert_fusion.1
  295.7 72.8 %all-gather.18.cloned.1.call-done = bf16[4096,1024]{1,0:T(8,128)(2,1)} async-done(((bf16[128,1024]{1,0:T(8,128)(2,1)}), bf16[4096,1024]{1,0:T(8,128)(2,1)}) %all-gather.18.cloned.1.call-update) | async-done | bytes 8388624 | tf_op jit(solution)/shard_map/all_gather | solution.py:372
  409.6 13.2 %collective-permute-done.11 = bf16[4,128,512]{2,1,0:T(8,128)(2,1)S(1)} collective-permute-done((bf16[4,128,512]{2,1,0:T(8,128)(2,1)S(1)}, bf16[4,128,512]{2,1,0:T(8,128)(2,1)S(1)}, u32[]{:S(2)}, u32[]{:S(2)}) %collective-permute-start.11) | collective-permute-done | bytes 524320 | tf_op jit(solution)/shard_map/ppermute | solution.py:62
  425.5 13.2 %collective-permute-done.8 = bf16[4,128,512]{2,1,0:T(8,128)(2,1)S(1)} collective-permute-done((bf16[4,128,512]{2,1,0:T(8,128)(2,1)S(1)}, bf16[4,128,512]{2,1,0:T(8,128)(2,1)S(1)}, u32[]{:S(2)}, u32[]{:S(2)}) %collective-permute-start.8) | collective-permute-done | bytes 524320 | tf_op jit(solution)/shard_map/ppermute | solution.py:62
  443.9 11.9 %fusion.333 = (f32[1024]{0:T(1024)S(1)}, f32[1024,4000]{0,1:T(8,128)S(1)}) fusion(bf16[4000,1024]{1,0:T(8,128)(2,1)} %all-gather.10.cloned.1.call-done, bf16[1024,512]{1,0:T(8,128)(2,1)} %copy-done.97, bf16[1024,512]{1,0:T(8,128)(2,1)} %constant_dynamic-update-slice_fusion), kind=kOutput, calls=%fused_computation.795 | convolution fusion | flops 8396897280 | bytes 26677248 | tf_op jit(solution)/shard_map/dot_general | solution.py:24
  455.8 15.3 %exponential_reduce_fusion = (f32[1024]{0:T(1024)S(1)}, f32[1024]{0:T(1024)S(1)}) fusion(f32[1024,4000]{0,1:T(8,128)S(1)} %get-tuple-element.263, f32[1024]{0:T(1024)S(1)} %get-tuple-element.262, s32[1024]{0:T(1024)S(1)} %copy-done.83), kind=kLoop, calls=%fused_computation.14 | loop fusion | flops 20477952 | bytes 16400384 | tf_op jit(solution)/shard_map/reduce_sum | solution.py:426
  487.8 9.4 collective-permute-done.14
  503.2 14.2 %fusion.335 = f32[1024,1024]{1,0:T(8,128)S(1)} fusion(bf16[1024,4000]{0,1:T(8,128)(2,1)S(1)} %multiply_convert_fusion, bf16[4000,1024]{1,0:T(8,128)(2,1)} %all-gather.10.cloned.1.call-done), kind=kOutput, calls=%fused_computation.797 | convolution fusion | flops 8388608000 | bytes 20578304 | tf_op jit(solution)/shard_map/dot_general | solution.py:24
  521.8 19.5 %collective-permute-done.20 = f32[4,128,512]{2,1,0:T(8,128)S(1)} collective-permute-done((f32[4,128,512]{2,1,0:T(8,128)S(1)}, f32[4,128,512]{2,1,0:T(8,128)S(1)}, u32[]{:S(2)}, u32[]{:S(2)}) %collective-permute-start.20) | collective-permute-done | bytes 1048608 | tf_op jit(solution)/shard_map/ppermute | solution.py:62
  561.2 14.1 %collective-permute-done.22 = f32[1,128,512]{2,1,0:T(8,128)S(1)} collective-permute-done((f32[1,128,512]{2,1,0:T(8,128)S(1)}, f32[1,128,512]{2,1,0:T(8,128)S(1)}, u32[]{:S(2)}, u32[]{:S(2)}) %collective-permute-start.22) | collective-permute-done | bytes 262176 | tf_op jit(solution)/shard_map/ppermute | solution.py:62
  581.3 8.6 fusion.17
  589.9 7.4 multiply_reduce_fusion.1
  601.1 29.8 %attend_back.1 = (bf16[128,1024]{1,0:T(8,128)(2,1)S(1)}, bf16[128,1024]{1,0:T(8,128)(2,1)S(1)}, bf16[128,1024]{1,0:T(8,128)(2,1)S(1)}, f32[1,1024]{1,0:T(1,128)S(1)}) custom-call(bf16[128,3072]{1,0:T(8,128)(2,1)S(1)} %convolution_convert_fusion.queries_ref.keys_ref.values_ref, bf16[128,3072]{1,0:T(8,128)(2,1)S(1)} %convolution_convert_fusion.queries_ref.keys_ref.values_ref, ...), custom_call_target="tpu_custom_call" | custom-call | flops 2147483648 | bytes 33554432 | tf_op jit(solution)/shard_map/attend_back/pallas_call | solution.py:298
  667.9 17.2 %fusion.8 = f32[8,4000]{1,0:T(8,128)S(1)} fusion(f32[1024,8]{0,1:T(8,128)S(1)} %copy-done.58, f32[4000,1024]{1,0:T(8,128)} %bitcast.650, f32[24,4000]{1,0:T(8,128)S(1)} %fusion.1, f32[24,4000]{1,0:T(8,128)} %fusion.120), kind=kOutput, calls=%fused_computation.24 | convolution fusion | flops 393408000 | bytes 17312768 | tf_op jit(solution)/shard_map/dot_general | solution.py:24
  686.9 15.0 %collective-permute-done.34 = bf16[1,128,512]{2,1,0:T(8,128)(2,1)S(1)} collective-permute-done((bf16[1,128,512]{2,1,0:T(8,128)(2,1)S(1)}, bf16[1,128,512]{2,1,0:T(8,128)(2,1)S(1)}, u32[]{:S(2)}, u32[]{:S(2)}) %collective-permute-start.34) | collective-permute-done | bytes 131104 | tf_op jit(solution)/shard_map/ppermute | solution.py:62
  703.5 6.8 collective-permute-done.38
  716.0 9.7 collective-permute-done.32
  776.2 20.9 %fusion = f32[4000,1024]{1,0:T(8,128)} fusion(s32[1024]{0:T(1024)S(1)} %copy-done.117, bf16[1024,512]{1,0:T(8,128)(2,1)S(1)} %constant_dynamic-update-slice_fusion.68, bf16[1024,512]{1,0:T(8,128)(2,1)S(1)} %constant_dynamic-update-slice_fusion.60), kind=kOutput, calls=%fused_computation.7 | convolution fusion | flops 8396898304 | bytes 18485248 | tf_op jit(solution)/shard_map/dot_general | solution.py:24
  797.2 21.6 %add_add_fusion = f32[4000,1024]{1,0:T(8,128)} fusion(f32[4000,1024]{1,0:T(8,128)} %bitcast.651, f32[4000,1024]{1,0:T(8,128)} %fusion, bf16[1024,4000]{0,1:T(8,128)(2,1)S(1)} %bitcast.645, bf16[1024,512]{1,0:T(8,128)(2,1)} %copy-done.97, bf16[1024,512]{1,0:T(8,128)(2,1)} %constant_dynamic-update-slice_fusion), kind=kOutput, calls=%fused_computation.10 | convolution fusion | flops 8400994304 | bytes 59441152 | tf_op jit(solution)/shard_map/dot_general | solution.py:24
  818.9 11.3 %convolution_dynamic-update-slice_fusion = f32[8,11264]{1,0:T(8,128)S(1)} fusion(f32[8,11264]{1,0:T(8,128)S(1)} %copy-done.49, f32[8,4000]{1,0:T(8,128)S(1)} %fusion.90, f32[4000,1024]{1,0:T(8,128)} %add_add_fusion), kind=kOutput, calls=%fused_computation.58 | convolution fusion | flops 393216000 | bytes 16547840 | tf_op jit(solution)/shard_map/dot_general | solution.py:24
  865.9 9.9 collective-permute-done.46
  904.3 22.9 %fusion.334 = (f32[4000,1024]{1,0:T(8,128)}, f32[4000,1024]{1,0:T(8,128)}) fusion(f32[4000,1024]{1,0:T(8,128)} %add_add_fusion, f32[8,4000]{1,0:T(8,128)S(1)} %fusion.90, f32[8,11264]{1,0:T(8,128)S(1)} %bitcast.683), kind=kOutput, calls=%fused_computation.796 | convolution fusion | flops 397312000 | bytes 49315840 | tf_op jit(solution)/shard_map/dot_general | solution.py:24
  927.3 10.4 %multiply_subtract_fusion = (f32[1000,1024]{1,0:T(8,128)}, f32[1000,1024]{1,0:T(8,128)}) fusion(f32[1000,1024]{1,0:T(8,128)} %param.40, f32[4000,1024]{1,0:T(8,128)} %get-tuple-element.273, s32[]{:T(128)S(6)} %select_n.203, f32[]{:T(128)S(6)} %min.3, f32[1000,1024]{1,0:T(8,128)} %param.46), kind=kLoop, calls=%fused_computation.25 | loop fusion | flops 5120000 | bytes 20480008 | tf_op jit(solution)/shard_map/sub | solution.py:597
  956.9 24.3 %all-gather.24.cloned.1.call-done = bf16[1024,4096]{1,0:T(8,128)(2,1)} async-done(((bf16[128,4096]{1,0:T(8,128)(2,1)}), bf16[1024,4096]{1,0:T(8,128)(2,1)}) %all-gather.24.cloned.1.call-update) | async-done | bytes 8388624 | tf_op jit(solution)/shard_map/all_gather | solution.py:491
  981.2 6.7 fusion.6
  (782 shorter events, 350.3 us)
Async XLA Ops:
  7.2 63.9 %all-gather.10.cloned.1.call-start = ((), (), s32[]{:S(2)}) async-start(), calls=%async_computation.1 | async-start | bytes 10240000 | tf_op jit(solution)/shard_map/all_gather | solution.py:369
  11.1 138.9 %all-gather.12.cloned.1.call-start = ((), (), s32[]{:S(2)}) async-start(), calls=%async_computation.2 | async-start | bytes 6488064 | tf_op jit(solution)/shard_map/all_gather | solution.py:372
  12.7 210.7 %all-gather.14.cloned.1.call-start = ((), (), s32[]{:S(2)}) async-start(), calls=%async_computation.3 | async-start | bytes 2162688 | tf_op jit(solution)/shard_map/all_gather | solution.py:372
  13.5 275.6 %all-gather.16.cloned.1.call-start = ((), (), s32[]{:S(2)}) async-start(), calls=%async_computation.4 | async-start | bytes 8650752 | tf_op jit(solution)/shard_map/all_gather | solution.py:372
  14.3 354.2 %all-gather.18.cloned.1.call-start = ((), (), s32[]{:S(2)}) async-start(), calls=%async_computation.5 | async-start | bytes 8650752 | tf_op jit(solution)/shard_map/all_gather | solution.py:372
  16.1 23.9 %all-to-all-start = ((s32[8,3,128]{2,1,0:T(4,128)}), s32[8,3,128]{2,1,0:T(4,128)S(1)}, u32[]{:S(2)}, u32[]{:S(2)}) async-start(s32[8,3,128]{2,1,0:T(4,128)} %broadcast_in_dim.113), calls=%async_computation | async-start | bytes 32768 | tf_op jit(solution)/shard_map/all_to_all | solution.py:125
  23.3 918.8 %all-gather.22.cloned.1.call-start = ((), (), s32[]{:S(2)}) async-start(), calls=%async_computation.7 | async-start | bytes 2359296 | tf_op jit(solution)/shard_map/all_gather | solution.py:491
  84.1 17.7 %collective-permute-start.3 = (bf16[4,128,512]{2,1,0:T(8,128)(2,1)S(1)}, bf16[4,128,512]{2,1,0:T(8,128)(2,1)S(1)}, u32[]{:S(2)}, u32[]{:S(2)}) collective-permute-start(bf16[4,128,512]{2,1,0:T(8,128)(2,1)S(1)} %pad_maximum_fusion.8), channel_id=1, source_target_pairs={{0,2},{1,3},{2,0},{3,1},{4,6},{5,7},{6,4},{7,5},{8,10},{9,11},{10,... | collective-permute-start | bytes 1572872 | tf_op jit(solution)/shard_map/ppermute | solution.py:62
  88.2 17.2 %collective-permute-start.15 = (f32[8,128]{1,0:T(8,128)S(1)}, f32[8,128]{1,0:T(8,128)S(1)}, u32[]{:S(2)}, u32[]{:S(2)}) collective-permute-start(f32[8,128]{1,0:T(8,128)S(1)} %broadcast_in_dim.119), channel_id=1, source_target_pairs={{0,8},{8,0},{16,24},{24,16},{1,9},{9,1},{17,25},{25,17},{2,10},{10... | collective-permute-start | bytes 12296 | tf_op jit(solution)/shard_map/ppermute | solution.py:62
  106.6 270.4 %collective-permute-start.16 = (f32[8,128]{1,0:T(8,128)}, f32[8,128]{1,0:T(8,128)}, u32[]{:S(2)}, u32[]{:S(2)}) collective-permute-start(f32[8,128]{1,0:T(8,128)} %broadcast_add_fusion), channel_id=1, source_target_pairs={{0,16},{8,24},{16,0},{24,8},{1,17},{9,25},{17,1},{25,9},{2,18},{10... | collective-permute-start | bytes 12296 | tf_op jit(solution)/shard_map/ppermute | solution.py:62
  400.1 22.8 %collective-permute-start.11 = (bf16[4,128,512]{2,1,0:T(8,128)(2,1)S(1)}, bf16[4,128,512]{2,1,0:T(8,128)(2,1)S(1)}, u32[]{:S(2)}, u32[]{:S(2)}) collective-permute-start(bf16[4,128,512]{2,1,0:T(8,128)(2,1)S(1)} %pad_maximum_fusion.10), channel_id=1, source_target_pairs={{0,2},{1,3},{2,0},{3,1},{4,6},{5,7},{6,4},{7,5},{8,10},{9,11},{10,... | collective-permute-start | bytes 1572872 | tf_op jit(solution)/shard_map/ppermute | solution.py:62
  403.1 68.1 %collective-permute-start.48 = (bf16[128,896]{0,1:T(8,128)(2,1)}, bf16[128,896]{0,1:T(8,128)(2,1)}, u32[]{:S(2)}, u32[]{:S(2)}) collective-permute-start(bf16[128,896]{0,1:T(8,128)(2,1)} %get-tuple-element.123), channel_id=1, source_target_pairs={{0,1},{1,0},{2,3},{3,2},{4,5},{5,4},{6,7},{7,6},{8,9},{9,8},{10,11... | collective-permute-start | bytes 688136 | tf_op jit(solution)/shard_map/ppermute | solution.py:62
  403.9 73.1 %collective-permute-start.49 = (bf16[128,896]{0,1:T(8,128)(2,1)}, bf16[128,896]{0,1:T(8,128)(2,1)}, u32[]{:S(2)}, u32[]{:S(2)}) collective-permute-start(bf16[128,896]{0,1:T(8,128)(2,1)} %get-tuple-element.122), channel_id=1, source_target_pairs={{0,2},{1,3},{2,0},{3,1},{4,6},{5,7},{6,4},{7,5},{8,10},{9,11},{10,... | collective-permute-start | bytes 688136 | tf_op jit(solution)/shard_map/ppermute | solution.py:62
  405.1 81.6 %collective-permute-start.50 = (bf16[128,896]{0,1:T(8,128)(2,1)}, bf16[128,896]{0,1:T(8,128)(2,1)}, u32[]{:S(2)}, u32[]{:S(2)}) collective-permute-start(bf16[128,896]{0,1:T(8,128)(2,1)} %get-tuple-element.121), channel_id=1, source_target_pairs={{0,3},{1,2},{2,1},{3,0},{4,7},{5,6},{6,5},{7,4},{8,11},{9,10},{10,... | collective-permute-start | bytes 688136 | tf_op jit(solution)/shard_map/ppermute | solution.py:62
  406.7 111.2 %collective-permute-start.51 = (bf16[128,896]{0,1:T(8,128)(2,1)}, bf16[128,896]{0,1:T(8,128)(2,1)S(1)}, u32[]{:S(2)}, u32[]{:S(2)}) collective-permute-start(bf16[128,896]{0,1:T(8,128)(2,1)} %get-tuple-element.120), channel_id=1, source_target_pairs={{0,4},{1,5},{2,6},{3,7},{4,0},{5,1},{6,2},{7,3},{8,12},{9,13},{10,... | collective-permute-start | bytes 688136 | tf_op jit(solution)/shard_map/ppermute | solution.py:62
  422.8 15.8 %collective-permute-start.8 = (bf16[4,128,512]{2,1,0:T(8,128)(2,1)S(1)}, bf16[4,128,512]{2,1,0:T(8,128)(2,1)S(1)}, u32[]{:S(2)}, u32[]{:S(2)}) collective-permute-start(bf16[4,128,512]{2,1,0:T(8,128)(2,1)S(1)} %pad_maximum_fusion.9), channel_id=1, source_target_pairs={{0,1},{1,0},{2,3},{3,2},{4,5},{5,4},{6,7},{7,6},{8,9},{9,8},{10,11... | collective-permute-start | bytes 1572872 | tf_op jit(solution)/shard_map/ppermute | solution.py:62
  438.6 393.9 %collective-permute-start.52 = (bf16[128,896]{0,1:T(8,128)(2,1)}, bf16[128,896]{0,1:T(8,128)(2,1)}, u32[]{:S(2)}, u32[]{:S(2)}) collective-permute-start(bf16[128,896]{0,1:T(8,128)(2,1)} %get-tuple-element.119), channel_id=1, source_target_pairs={{0,5},{1,4},{2,7},{3,6},{4,1},{5,0},{6,3},{7,2},{8,13},{9,12},{10,... | collective-permute-start | bytes 688136 | tf_op jit(solution)/shard_map/ppermute | solution.py:62
  475.0 363.7 %collective-permute-start.53 = (bf16[128,896]{0,1:T(8,128)(2,1)}, bf16[128,896]{0,1:T(8,128)(2,1)}, u32[]{:S(2)}, u32[]{:S(2)}) collective-permute-start(bf16[128,896]{0,1:T(8,128)(2,1)} %get-tuple-element.118), channel_id=1, source_target_pairs={{0,6},{1,7},{2,4},{3,5},{4,2},{5,3},{6,0},{7,1},{8,14},{9,15},{10,... | collective-permute-start | bytes 688136 | tf_op jit(solution)/shard_map/ppermute | solution.py:62
  484.7 359.2 %collective-permute-start.54 = (bf16[128,896]{0,1:T(8,128)(2,1)}, bf16[128,896]{0,1:T(8,128)(2,1)}, u32[]{:S(2)}, u32[]{:S(2)}) collective-permute-start(bf16[128,896]{0,1:T(8,128)(2,1)} %get-tuple-element.117), channel_id=1, source_target_pairs={{0,7},{1,6},{2,5},{3,4},{4,3},{5,2},{6,1},{7,0},{8,15},{9,14},{10,... | collective-permute-start | bytes 688136 | tf_op jit(solution)/shard_map/ppermute | solution.py:62
  517.8 23.4 %collective-permute-start.20 = (f32[4,128,512]{2,1,0:T(8,128)S(1)}, f32[4,128,512]{2,1,0:T(8,128)S(1)}, u32[]{:S(2)}, u32[]{:S(2)}) collective-permute-start(f32[4,128,512]{2,1,0:T(8,128)S(1)} %pad_maximum_fusion.3), channel_id=1, source_target_pairs={{0,2},{1,3},{2,0},{3,1},{4,6},{5,7},{6,4},{7,5},{8,10},{9,11},{10,... | collective-permute-start | bytes 3145736 | tf_op jit(solution)/shard_map/ppermute | solution.py:62
  521.4 26.2 %collective-permute-start.17 = (f32[4,128,512]{2,1,0:T(8,128)S(1)}, f32[4,128,512]{2,1,0:T(8,128)S(1)}, u32[]{:S(2)}, u32[]{:S(2)}) collective-permute-start(f32[4,128,512]{2,1,0:T(8,128)S(1)} %pad_maximum_fusion.2), channel_id=1, source_target_pairs={{0,1},{1,0},{2,3},{3,2},{4,5},{5,4},{6,7},{7,6},{8,9},{9,8},{10,11... | collective-permute-start | bytes 3145736 | tf_op jit(solution)/shard_map/ppermute | solution.py:62
  556.2 19.2 %collective-permute-start.22 = (f32[1,128,512]{2,1,0:T(8,128)S(1)}, f32[1,128,512]{2,1,0:T(8,128)S(1)}, u32[]{:S(2)}, u32[]{:S(2)}) collective-permute-start(f32[1,128,512]{2,1,0:T(8,128)S(1)} %slice.1185), channel_id=1, source_target_pairs={{0,4},{1,5},{2,6},{3,7},{4,0},{5,1},{6,2},{7,3},{8,12},{9,13},{10,... | collective-permute-start | bytes 786440 | tf_op jit(solution)/shard_map/ppermute | solution.py:62
  557.7 21.8 %collective-permute-start.19 = (f32[1,128,512]{2,1,0:T(8,128)S(1)}, f32[1,128,512]{2,1,0:T(8,128)S(1)}, u32[]{:S(2)}, u32[]{:S(2)}) collective-permute-start(f32[1,128,512]{2,1,0:T(8,128)S(1)} %slice.1175), channel_id=1, source_target_pairs={{0,4},{1,5},{2,6},{3,7},{4,0},{5,1},{6,2},{7,3},{8,12},{9,13},{10,... | collective-permute-start | bytes 786440 | tf_op jit(solution)/shard_map/ppermute | solution.py:62
  598.5 346.7 %all-gather.26.cloned.1.call-start = ((), (), s32[]{:S(2)}) async-start(), calls=%async_computation.9 | async-start | bytes 2359296 | tf_op jit(solution)/shard_map/all_gather | solution.py:491
  641.4 309.6 %all-gather.20.cloned.1.call-start = ((), (), s32[]{:S(2)}) async-start(), calls=%async_computation.6 | async-start | bytes 7077888 | tf_op jit(solution)/shard_map/all_gather | solution.py:491
  652.8 328.4 %all-gather.24.cloned.1.call-start = ((), (), s32[]{:S(2)}) async-start(), calls=%async_computation.8 | async-start | bytes 9437184 | tf_op jit(solution)/shard_map/all_gather | solution.py:491
  655.3 31.4 %collective-permute-start.37 = (bf16[1,128,512]{2,1,0:T(8,128)(2,1)S(1)}, bf16[1,128,512]{2,1,0:T(8,128)(2,1)S(1)}, u32[]{:S(2)}, u32[]{:S(2)}) collective-permute-start(bf16[1,128,512]{2,1,0:T(8,128)(2,1)S(1)} %get-tuple-element.156), channel_id=1, source_target_pairs={{0,4},{1,5},{2,6},{3,7},{4,0},{5,1},{6,2},{7,3},{8,12},{9,13},{10,... | collective-permute-start | bytes 393224 | tf_op jit(solution)/shard_map/ppermute | solution.py:62
  664.5 20.6 %collective-permute-start.25 = (f32[1,8,896]{2,1,0:T(8,128)S(1)}, f32[1,8,896]{2,1,0:T(8,128)S(1)}, u32[]{:S(2)}, u32[]{:S(2)}) collective-permute-start(f32[1,8,896]{2,1,0:T(8,128)S(1)} %slice.1223), channel_id=1, source_target_pairs={{0,4},{1,5},{2,6},{3,7},{4,0},{5,1},{6,2},{7,3},{8,12},{9,13},{10,... | collective-permute-start | bytes 86024 | tf_op jit(solution)/shard_map/ppermute | solution.py:62
  686.7 16.2 %collective-permute-start.30 = (f32[8,4896]{1,0:T(8,128)S(1)}, f32[8,4896]{1,0:T(8,128)S(1)}, u32[]{:S(2)}, u32[]{:S(2)}) collective-permute-start(f32[8,4896]{1,0:T(8,128)S(1)} %fusion.301), channel_id=1, source_target_pairs={{0,16},{8,24},{16,0},{24,8},{1,17},{9,25},{17,1},{25,9},{2,18},{10... | collective-permute-start | bytes 470024 | tf_op jit(solution)/shard_map/ppermute | solution.py:62
  702.9 22.8 %collective-permute-start.35 = (bf16[2,128,512]{2,1,0:T(8,128)(2,1)S(1)}, bf16[2,128,512]{2,1,0:T(8,128)(2,1)S(1)}, u32[]{:S(2)}, u32[]{:S(2)}) collective-permute-start(bf16[2,128,512]{2,1,0:T(8,128)(2,1)S(1)} %pad_maximum_fusion.21), channel_id=1, source_target_pairs={{0,2},{1,3},{2,0},{3,1},{4,6},{5,7},{6,4},{7,5},{8,10},{9,11},{10,... | collective-permute-start | bytes 786440 | tf_op jit(solution)/shard_map/ppermute | solution.py:62
  725.6 42.7 %collective-permute-start.39 = (bf16[4,128,512]{2,1,0:T(8,128)(2,1)}, bf16[4,128,512]{2,1,0:T(8,128)(2,1)}, u32[]{:S(2)}, u32[]{:S(2)}) collective-permute-start(bf16[4,128,512]{2,1,0:T(8,128)(2,1)} %pad_maximum_fusion.15), channel_id=1, source_target_pairs={{0,2},{1,3},{2,0},{3,1},{4,6},{5,7},{6,4},{7,5},{8,10},{9,11},{10,... | collective-permute-start | bytes 1572872 | tf_op jit(solution)/shard_map/ppermute | solution.py:62
  732.2 40.2 %collective-permute-start.36 = (bf16[4,128,512]{2,1,0:T(8,128)(2,1)}, bf16[4,128,512]{2,1,0:T(8,128)(2,1)}, u32[]{:S(2)}, u32[]{:S(2)}) collective-permute-start(bf16[4,128,512]{2,1,0:T(8,128)(2,1)} %pad_maximum_fusion.14), channel_id=1, source_target_pairs={{0,1},{1,0},{2,3},{3,2},{4,5},{5,4},{6,7},{7,6},{8,9},{9,8},{10,11... | collective-permute-start | bytes 1572872 | tf_op jit(solution)/shard_map/ppermute | solution.py:62
  (167 other events, 1818.3 us)
Sparse Core Ops, SparseCore 0:
  11.2 59.8 all-gather.9
  74.6 75.3 all-gather.11
  153.6 55.7 all-gather.13
  212.8 76.2 all-gather.15
  292.5 75.9 all-gather.17
  598.6 47.4 all-gather.21
  648.3 54.8 all-gather.25
  705.4 109.4 all-gather.19
  856.6 124.5 all-gather.23

commit v2 on v1

v2 whole, which is shorter than its diff:
```python
import functools
import math

import jax
import jax.numpy as jnp
from jax import lax
from jax.experimental import pallas as pl
from jax.experimental.pallas import tpu as pltpu
from jax.sharding import PartitionSpec as P

HEADS = 8
RANK = 8
LANES = 128
EPSILON = 1e-06
MOMENTUM = 0.9
LEARN_RATE = 5000.0
CLIP_LEVEL = 0.02
F32 = jnp.float32
BF16 = jnp.bfloat16
FINE = lax.Precision.HIGHEST
FAIR = lax.Precision.HIGH
SMALL = pl.CostEstimate(flops=10**6, bytes_accessed=10**5, transcendentals=0)


def dot_over(left, right, left_dim, right_dim, precision=None):
    return lax.dot_general(
        left,
        right,
        (((left_dim,), (right_dim,)), ((), ())),
        precision=precision,
        preferred_element_type=F32,
    )


def matmul(left, right):
    return dot_over(left, right, 1, 0)


def matmul_back(left, right):
    return dot_over(left, right, 1, 1)


def matmul_outer(left, right):
    return dot_over(left, right, 0, 0)


def three_parts(values):
    first = lax.reduce_precision(values, 8, 7)
    rest = values - first
    second = lax.reduce_precision(rest, 8, 7)
    third = rest - second
    return [first.astype(BF16), second.astype(BF16), third.astype(BF16)]


def stacked_parts(rows):
    return jnp.concatenate(three_parts(rows), axis=0)


def unstack(wide):
    count = wide.shape[0] // 3
    return wide[:count] + (wide[count : 2 * count] + wide[2 * count :])


def rows_by_narrow(stacked, narrow, narrow_dim):
    return unstack(dot_over(stacked, narrow, 1, narrow_dim))


def outer_fine(left, right):
    a, b, c = three_parts(left)
    d, e, f = three_parts(right)
    return dot_over(
        jnp.concatenate([a, a, b, a, c, b], axis=0), jnp.concatenate([d, e, d, f, d, e], axis=0), 0, 0
    )


def swap(array, axis, bit):
    size = lax.axis_size(axis)
    return lax.ppermute(array, axis, [(i, i ^ bit) for i in range(size)])


def bits_of(axis):
    size = lax.axis_size(axis)
    return [1 << k for k in range(size.bit_length() - 1)]


def two_orders(axis):
    bits = bits_of(axis)
    return bits, ([bits[1], bits[0]] + bits[2:] if len(bits) > 1 else bits)


def scatter_sum(blocks, axis, order, sent=F32, later=None):
    bits = sorted(order, reverse=True)
    blocks = blocks.reshape((2,) * len(bits) + blocks.shape[1:])
    for bit in order:
        at = bits.index(bit)
        away = lax.index_in_dim(blocks, 1, at, False).astype(sent)
        if later is not None and bit == order[0]:
            away, later = lax.optimization_barrier((away, later))
        arrived = swap(away, axis, bit)
        blocks = lax.index_in_dim(blocks, 0, at, False) + arrived.astype(blocks.dtype)
        bits.remove(bit)
    return blocks if later is None else (blocks, later)


def scatter_sum_halves(blocks, axis, sent, later=None):
    half = blocks.shape[-1] // 2
    first, second = two_orders(axis)
    left = scatter_sum(blocks[..., :half], axis, first, sent, later)
    if later is not None:
        left, later = left
    right = scatter_sum(blocks[..., half:], axis, second, sent, later)
    if later is not None:
        right, later = right
    whole = jnp.concatenate([left, right], axis=-1)
    return whole if later is None else (whole, later)


def gather_blocks(block, axis, order):
    current, count = block[None], len(order)
    for bit in order:
        current = jnp.concatenate([current, swap(current, axis, bit)], axis=0)
    places = [count - 1 - order.index(bit) for bit in sorted(order, reverse=True)]
    current = current.reshape((2,) * count + block.shape)
    rest = list(range(count, current.ndim))
    return current.transpose(places + rest).reshape((1 << count,) + block.shape)


def gather_arrivals(block, axis):
    current, indices = block[None], [0]
    for bit in bits_of(axis)[::-1]:
        current = jnp.concatenate([current, swap(current, axis, bit)], axis=0)
        indices = indices + [j ^ bit for j in indices]
    return current, jnp.array(indices, jnp.int32)


def scatter_and_gather(blocks, block, axis, order):
    bits = sorted(order, reverse=True)
    tile = blocks.shape[-2:]
    blocks = blocks.reshape((2,) * len(bits) + blocks.shape[1:])
    current, indices = block[None], [0]
    for bit in order:
        at = bits.index(bit)
        away, kept = [lax.index_in_dim(blocks, k, at, False) for k in (1, 0)]
        sent = jnp.concatenate([away.reshape((-1,) + tile), current.reshape((-1,) + tile)], axis=0)
        arrived = swap(sent, axis, bit)
        count = math.prod(away.shape[:-2])
        blocks = kept + arrived[:count].reshape(kept.shape)
        current = jnp.concatenate([current, arrived[count:].reshape(current.shape)], axis=0)
        indices = indices + [j ^ bit for j in indices]
        bits.remove(bit)
    return blocks, current, jnp.array(indices, jnp.int32)


def to_tiles(rows):
    return rows.reshape(rows.shape[0], -1, LANES).transpose(1, 0, 2)


def from_tiles(tiles):
    return tiles.transpose(1, 0, 2).reshape(tiles.shape[1], -1)


def gather_halves(block, axis):
    half = block.shape[-1] // 2
    first, second = two_orders(axis)
    left = gather_blocks(block[..., :half], axis, first[::-1])
    right = gather_blocks(block[..., half:], axis, second[::-1])
    return jnp.concatenate([left, right], axis=-1).reshape(-1, block.shape[-1])


def in_order(blocks, relative):
    return blocks.at[relative].get(mode="promise_in_bounds")


def sum_over(array, axis):
    for bit in bits_of(axis):
        array = array + swap(array, axis, bit)
    return array


def spread_small(array, axis):
    size = lax.axis_size(axis)
    copies = jnp.broadcast_to(array[None], (size,) + array.shape)
    return lax.all_to_all(copies, axis, 0, 0, tiled=False)


def norm_rows(values, gain):
    inverse = lax.rsqrt(jnp.mean(values * values, axis=-1, keepdims=True) + EPSILON)
    return (values * inverse * gain, inverse)


def norm_back(values, inverse, gain, upstream):
    scaled = upstream * gain
    gain_part = jnp.sum(upstream * values * inverse, axis=0)
    result = inverse * scaled - values * inverse**3 * jnp.mean(
        scaled * values, axis=-1, keepdims=True
    )
    return (result, gain_part)


def local_probs(queries, keys, length, scale):
    rows = queries.shape[0]
    scores = matmul_back(queries, keys) * scale
    row = lax.broadcasted_iota(jnp.int32, (rows, rows), 0)
    column = lax.broadcasted_iota(jnp.int32, (rows, rows), 1)
    allowed = (row >= column) & (row // length == column // length)
    scores = jnp.where(allowed, scores, -1e30)
    powers = jnp.exp(scores - jnp.max(scores, axis=-1, keepdims=True))
    return powers / jnp.sum(powers, axis=-1, keepdims=True)


def attend_kernel(
    length,
    queries_ref,
    keys_ref,
    values_ref,
    mem_keys_ref,
    mem_values_ref,
    block_ref,
    lane_ref,
    opening_ref,
    attended_ref,
    difference_ref,
    weights_ref,
    scores_ref,
    rounded_ref,
):
    queries = queries_ref[...]
    tokens, width = queries.shape
    slots = mem_keys_ref.shape[2]
    lane_blocks = slots // LANES
    scale = width ** (-0.5)
    picks = block_ref.shape[2]
    block_at = lax.broadcasted_iota(jnp.int32, (lane_blocks * 8, picks), 0).astype(F32).astype(BF16)
    lane_at = lax.broadcasted_iota(jnp.int32, (LANES, picks), 0).astype(F32).astype(BF16)
    one, zero = jnp.ones((), BF16), jnp.zeros((), BF16)
    scores_ref[...] = matmul_back(queries, mem_keys_ref[0, 0]) * scale

    def group(at, carry):
        rows = pl.ds(pl.multiple_of(at * 8, 8), 8)
        block_hot = jnp.where(block_at == block_ref[0, pl.ds(at, 1), :], one, zero)
        lane_hot = jnp.where(lane_at == lane_ref[0, pl.ds(at, 1), :], one, zero)
        counts = matmul_back(block_hot, lane_hot)
        counts = jnp.concatenate([counts[k * 8 : k * 8 + 8] for k in range(lane_blocks)], axis=1)
        scores = jnp.where(counts > 0.0, scores_ref[rows, :], -1e30)
        powers = jnp.exp(scores - jnp.max(scores, axis=-1, keepdims=True))
        total = jnp.sum(powers * counts, axis=-1, keepdims=True)
        probs = powers * (1.0 / total)
        weights_ref[0, rows, :] = probs * counts
        rounded_ref[rows, :] = probs.astype(BF16).astype(F32) * counts
        return carry

    lax.fori_loop(0, tokens // 8, group, 0, unroll=True)
    memory_out = matmul(rounded_ref[...].astype(BF16), mem_values_ref[0, 0])
    probs = local_probs(queries, keys_ref[...], length, scale)
    local_out = matmul(probs.astype(BF16), values_ref[...])
    opening = opening_ref[...]
    attended_ref[...] = (opening * memory_out + (1.0 - opening) * local_out).astype(BF16)
    difference_ref[...] = memory_out - local_out


def attend_back_kernel(
    length,
    queries_ref,
    keys_ref,
    values_ref,
    mem_keys_ref,
    mem_values_ref,
    weights_ref,
    upstream_ref,
    difference_ref,
    opening_ref,
    query_ref,
    key_ref,
    value_ref,
    parts_ref,
    gate_ref,
    slope_ref,
):
    queries, keys, values = queries_ref[...], keys_ref[...], values_ref[...]
    tokens, width = queries.shape
    scale = width ** (-0.5)
    opening = opening_ref[...]
    upstream = upstream_ref[...]
    gate_ref[...] = jnp.sum(upstream * difference_ref[...], axis=0, keepdims=True)
    memory_up = (opening * upstream).astype(BF16)
    local_up = ((1.0 - opening) * upstream).astype(BF16)
    slope_ref[...] = matmul_back(memory_up, mem_values_ref[0, 0])

    def group(at, carry):
        rows = pl.ds(pl.multiple_of(at * 8, 8), 8)
        weights, slope = weights_ref[0, rows, :], slope_ref[rows, :]
        middle = jnp.sum(weights * slope, axis=-1, keepdims=True)
        slope_ref[rows, :] = weights * (slope - middle)
        return carry

    lax.fori_loop(0, tokens // 8, group, 0, unroll=True)
    memory_part = matmul(slope_ref[...].astype(BF16), mem_keys_ref[0, 0])
    probs = local_probs(queries, keys, length, scale)
    slope = matmul_back(local_up, values)
    slope = (probs * (slope - jnp.sum(probs * slope, axis=-1, keepdims=True))).astype(BF16)
    query_ref[...] = ((matmul(slope, keys) + memory_part) * scale).astype(BF16)
    key_ref[...] = (matmul_outer(slope, queries) * scale).astype(BF16)
    value_ref[...] = matmul_outer(probs.astype(BF16), local_up).astype(BF16)
    parts_ref[0] = jnp.concatenate([query_ref[...], key_ref[...], value_ref[...]], axis=1)


def head_specs(tokens, width, slots):
    column = [
        pl.BlockSpec((tokens, width), functools.partial(lambda part, h: (0, part * HEADS + h), part))
        for part in range(3)
    ]
    store = [
        pl.BlockSpec((1, 1, slots, width), functools.partial(lambda part, h: (part, h, 0, 0), part))
        for part in range(2)
    ]
    return column, store


def attend(projected, memory, block_codes, lane_codes, opening_row, length):
    tokens = projected.shape[0]
    width = memory.shape[3]
    slots = memory.shape[2]
    column, store = head_specs(tokens, width, slots)
    codes = pl.BlockSpec((1,) + block_codes.shape[1:], lambda h: (h, 0, 0))
    head = pl.BlockSpec((tokens, width), lambda h: (0, h))
    return pl.pallas_call(
        functools.partial(attend_kernel, length),
        grid=(HEADS,),
        in_specs=column + store + [codes, codes, pl.BlockSpec((1, width), lambda h: (0, h))],
        out_specs=[head, head, pl.BlockSpec((1, tokens, slots), lambda h: (h, 0, 0))],
        out_shape=[
            jax.ShapeDtypeStruct((tokens, HEADS * width), BF16),
            jax.ShapeDtypeStruct((tokens, HEADS * width), F32),
            jax.ShapeDtypeStruct((HEADS, tokens, slots), F32),
        ],
        scratch_shapes=[pltpu.VMEM((tokens, slots), F32), pltpu.VMEM((tokens, slots), F32)],
        compiler_params=pltpu.CompilerParams(vmem_limit_bytes=40 * 2**20),
        cost_estimate=SMALL,
        name="attend",
    )(projected, projected, projected, memory, memory, block_codes, lane_codes, opening_row)


def attend_back(projected, memory, weights, upstream, difference, opening_row, length):
    tokens = projected.shape[0]
    width = memory.shape[3]
    slots = memory.shape[2]
    column, store = head_specs(tokens, width, slots)
    head = pl.BlockSpec((tokens, width), lambda h: (0, h))
    row = pl.BlockSpec((1, width), lambda h: (0, h))
    return pl.pallas_call(
        functools.partial(attend_back_kernel, length),
        grid=(HEADS,),
        in_specs=column
        + store
        + [pl.BlockSpec((1, tokens, slots), lambda h: (h, 0, 0)), head, head, row],
        out_specs=[head, head, head, pl.BlockSpec((1, tokens, 3 * width), lambda h: (h, 0, 0)), row],
        out_shape=[jax.ShapeDtypeStruct((tokens, HEADS * width), BF16)] * 3
        + [jax.ShapeDtypeStruct((HEADS, tokens, 3 * width), BF16)]
        + [jax.ShapeDtypeStruct((1, HEADS * width), F32)],
        scratch_shapes=[pltpu.VMEM((tokens, slots), F32)],
        compiler_params=pltpu.CompilerParams(vmem_limit_bytes=40 * 2**20),
        cost_estimate=SMALL,
        name="attend_back",
    )(projected, projected, projected, memory, memory, weights, upstream, difference, opening_row)


HEAD_ROWS = 400


def head_rows(total, shape):
    row = pl.program_id(0) * shape[0] + lax.broadcasted_iota(jnp.int32, shape, 0)
    return row, (row < total if total % shape[0] else None)


def logits_kernel(total, vocab_ref, final_ref, target_ref, logits_ref, stats_ref):
    logits = matmul_back(vocab_ref[...], final_ref[...])
    row, exists = head_rows(total, logits.shape)
    if exists is not None:
        logits = jnp.where(exists, logits, -1e30)
    logits_ref[...] = logits
    picked = jnp.sum(jnp.where(row == target_ref[...], logits, 0.0), axis=0, keepdims=True)
    peak = jnp.max(logits, axis=0, keepdims=True)

    @pl.when(pl.program_id(0) == 0)
    def _():
        stats_ref[0:1] = peak
        stats_ref[1:2] = jnp.sum(jnp.exp(logits - peak), axis=0, keepdims=True)
        stats_ref[2:3] = picked

    @pl.when(pl.program_id(0) > 0)
    def _():
        before = stats_ref[0:1]
        new_peak = jnp.maximum(before, peak)
        here = jnp.sum(jnp.exp(logits - new_peak), axis=0, keepdims=True)
        stats_ref[1:2] = stats_ref[1:2] * jnp.exp(before - new_peak) + here
        stats_ref[0:1] = new_peak
        stats_ref[2:3] += picked


def logits_and_stats(vocab, final_all, targets):
    total, width = vocab.shape
    tokens = final_all.shape[0]
    return pl.pallas_call(
        functools.partial(logits_kernel, total),
        grid=(pl.cdiv(total, HEAD_ROWS),),
        in_specs=[
            pl.BlockSpec((HEAD_ROWS, width), lambda i: (i, 0)),
            pl.BlockSpec((tokens, width), lambda i: (0, 0)),
            pl.BlockSpec((1, tokens), lambda i: (0, 0)),
        ],
        out_specs=[
            pl.BlockSpec((HEAD_ROWS, tokens), lambda i: (i, 0)),
            pl.BlockSpec((3, tokens), lambda i: (0, 0)),
        ],
        out_shape=[
            jax.ShapeDtypeStruct((total, tokens), F32),
            jax.ShapeDtypeStruct((3, tokens), F32),
        ],
        compiler_params=pltpu.CompilerParams(vmem_limit_bytes=52 * 2**20),
        cost_estimate=SMALL,
        name="logits",
    )(vocab, final_all, targets)


def logits_back_kernel(total, logits_ref, vocab_ref, log_ref, scale_ref, target_ref, grad_ref, final_ref):
    logits, vocab = logits_ref[...], vocab_ref[...]
    row, exists = head_rows(total, logits.shape)
    probs = jnp.exp(logits - log_ref[...])
    grad = jnp.where(row == target_ref[...], probs - 1.0, probs) * scale_ref[...]
    if exists is not None:
        grad = jnp.where(exists, grad, 0.0)
        vocab = jnp.where(exists[:, :1], vocab, 0.0).astype(BF16)
    grad = grad.astype(BF16)
    grad_ref[...] = grad
    part = matmul_outer(grad, vocab)

    @pl.when(pl.program_id(0) == 0)
    def _():
        final_ref[...] = part

    @pl.when(pl.program_id(0) > 0)
    def _():
        final_ref[...] += part


def logits_back(logits, vocab, log_total, scale, targets):
    total, width = vocab.shape
    tokens = logits.shape[1]
    row = pl.BlockSpec((1, tokens), lambda i: (0, 0))
    return pl.pallas_call(
        functools.partial(logits_back_kernel, total),
        grid=(pl.cdiv(total, HEAD_ROWS),),
        in_specs=[
            pl.BlockSpec((HEAD_ROWS, tokens), lambda i: (i, 0)),
            pl.BlockSpec((HEAD_ROWS, width), lambda i: (i, 0)),
            row,
            row,
            row,
        ],
        out_specs=[
            pl.BlockSpec((HEAD_ROWS, tokens), lambda i: (i, 0)),
            pl.BlockSpec((tokens, width), lambda i: (0, 0)),
        ],
        out_shape=[
            jax.ShapeDtypeStruct((total, tokens), BF16),
            jax.ShapeDtypeStruct((tokens, width), F32),
        ],
        compiler_params=pltpu.CompilerParams(vmem_limit_bytes=56 * 2**20),
        cost_estimate=SMALL,
        name="logits_back",
    )(logits, vocab, log_total, scale, targets)


def table_gradient_kernel(grad_ref, final_ref, error_ref, out_ref):
    out_ref[...] = matmul(grad_ref[...], final_ref[...]) + error_ref[...]


def table_gradient(logit_grad, final_all, error):
    total, tokens = logit_grad.shape
    width = final_all.shape[1]
    return pl.pallas_call(
        table_gradient_kernel,
        grid=(pl.cdiv(total, 2 * HEAD_ROWS),),
        in_specs=[
            pl.BlockSpec((2 * HEAD_ROWS, tokens), lambda i: (i, 0)),
            pl.BlockSpec((tokens, width), lambda i: (0, 0)),
            pl.BlockSpec((2 * HEAD_ROWS, width), lambda i: (i, 0)),
        ],
        out_specs=pl.BlockSpec((2 * HEAD_ROWS, width), lambda i: (i, 0)),
        out_shape=jax.ShapeDtypeStruct((total, width), F32),
        compiler_params=pltpu.CompilerParams(vmem_limit_bytes=52 * 2**20),
        cost_estimate=SMALL,
        name="table_gradient",
    )(logit_grad, final_all, error)


def split_rows(rows):
    first = rows.astype(BF16).astype(F32)
    second = (rows - first).astype(BF16).astype(F32)
    return jnp.concatenate([first, second, rows - first - second], axis=0).astype(BF16)


def pair_rows(left, right):
    a = left.astype(BF16).astype(F32)
    b = (left - a).astype(BF16).astype(F32)
    d = right.astype(BF16).astype(F32)
    e = (right - d).astype(BF16).astype(F32)
    c, f = left - a - b, right - d - e
    return (
        jnp.concatenate([a, a, b, a, c, b], axis=0).astype(BF16),
        jnp.concatenate([d, e, d, f, d, e], axis=0).astype(BF16),
    )


def left_kernel(
    relative_ref, base_ref, table_factor_ref, start_ref, *refs
):
    factors, rights, lefts = refs[:4], refs[4:8], refs[8:12]
    pieces_ref, narrow_ref, whole_ref = refs[12:]
    whole_ref[...] = base_ref[...]
    start = 0
    for factor, right, left in zip(factors, rights, lefts):
        narrowed = unstack(matmul_back(factor[...], right[...]))
        part = unstack(matmul(split_rows(narrowed), left[...]))
        columns = slice(start, start + left.shape[1])
        whole_ref[:, columns] += part
        start += left.shape[1]
    narrow_ref[...] = dot_over(table_factor_ref[...], start_ref[...], 1, 1, FINE)
    tiles = pieces_ref.shape[1]
    for j in range(pieces_ref.shape[0]):
        for k in range(tiles):
            first = pl.multiple_of((relative_ref[j] * tiles + k) * LANES, LANES)
            pieces_ref[j, k] = whole_ref[:, pl.ds(first, LANES)]


def left_pieces(relative, base, table_factor, start_grad, factor_parts, rights, lefts):
    count, width = relative.shape[0], base.shape[1]
    tokens = start_grad.shape[0]
    return pl.pallas_call(
        left_kernel,
        in_specs=[pl.BlockSpec(memory_space=pltpu.SMEM)] + [pl.BlockSpec(memory_space=pltpu.VMEM)] * 15,
        out_shape=[
            jax.ShapeDtypeStruct((count, width // count // LANES, RANK, LANES), F32),
            jax.ShapeDtypeStruct((RANK, tokens), F32),
        ],
        scratch_shapes=[pltpu.VMEM((RANK, width), F32)],
        compiler_params=pltpu.CompilerParams(vmem_limit_bytes=32 * 2**20),
        cost_estimate=SMALL,
        name="left_pieces",
    )(relative, base, table_factor, start_grad, *factor_parts, *rights, *lefts)


def inverse_of_cholesky(gram):
    size = gram.shape[0]
    row = lax.broadcasted_iota(jnp.int32, (size, size), 0)
    column = lax.broadcasted_iota(jnp.int32, (size, size), 1)
    left, right = gram, jnp.where(row == column, 1.0, 0.0)
    for k in range(size):
        scale = 1.0 / jnp.sqrt(left[k : k + 1, k : k + 1])
        pivot_left, pivot_right = left[k : k + 1] * scale, right[k : k + 1] * scale
        weight = left[:, k : k + 1] * scale
        below, here = row > k, row == k
        left = jnp.where(below, left - weight * pivot_left, jnp.where(here, pivot_left, left))
        right = jnp.where(below, right - weight * pivot_right, jnp.where(here, pivot_right, right))
    return right


def right_kernel(widths, relative_ref, pieces_ref, table_left_ref, token_ref, start_ref, *refs):
    rights, lefts = refs[:4], refs[4:8]
    ortho_ref, table_ortho_ref, right_ref, token_right_ref, squares_ref, whole_ref = refs[8:]
    tiles = pieces_ref.shape[1] - 1
    table_gram = jnp.zeros((RANK, LANES), F32)
    for j in range(pieces_ref.shape[0]):
        for k in range(tiles):
            first = pl.multiple_of((relative_ref[j] * tiles + k) * LANES, LANES)
            whole_ref[:, pl.ds(first, LANES)] = pieces_ref[j, k]
        table_gram = table_gram + pieces_ref[j, tiles]
    starts = [sum(widths[:k]) for k in range(5)]
    sums = [whole_ref[:, starts[k] : starts[k + 1]] for k in range(4)]
    grams = [dot_over(part, part, 1, 1, FINE) for part in sums] + [table_gram[:, :RANK]]
    inverses = [inverse_of_cholesky(gram) for gram in grams]
    start = 0
    for k in range(4):
        ortho = dot_over(inverses[k], sums[k], 1, 0, FINE)
        ortho_ref[:, starts[k] : starts[k + 1]] = ortho
        squares_ref[k] = dot_over(ortho, ortho, 1, 1, FINE)
        narrowed = unstack(matmul_back(split_rows(ortho), lefts[k][...]))
        wide = unstack(matmul(split_rows(narrowed), rights[k][...]))
        right_ref[:, start : start + wide.shape[1]] = wide
        start += wide.shape[1]
    ortho = dot_over(inverses[4], table_left_ref[...], 1, 0, FINE)
    table_ortho_ref[...] = ortho
    squares_ref[4] = dot_over(ortho, ortho, 1, 1, FINE)
    token_ortho = dot_over(inverses[4], token_ref[...], 1, 0, FINE)
    token_right_ref[...] = dot_over(token_ortho, start_ref[...], 1, 0, FINE)


def right_pieces(relative, pieces, table_left, token_left, start_grad, rights, lefts):
    count, tiles = pieces.shape[:2]
    piece = (tiles - 1) * LANES
    widths = [left.shape[1] for left in lefts]
    right_width = sum(right.shape[1] for right in rights)
    return pl.pallas_call(
        functools.partial(right_kernel, widths),
        in_specs=[pl.BlockSpec(memory_space=pltpu.SMEM)] + [pl.BlockSpec(memory_space=pltpu.VMEM)] * 12,
        out_shape=[
            jax.ShapeDtypeStruct((RANK, sum(widths)), F32),
            jax.ShapeDtypeStruct(table_left.shape, F32),
            jax.ShapeDtypeStruct((RANK, right_width), F32),
            jax.ShapeDtypeStruct((RANK, start_grad.shape[1]), F32),
            jax.ShapeDtypeStruct((5, RANK, RANK), F32),
        ],
        scratch_shapes=[pltpu.VMEM((RANK, count * piece), F32)],
        compiler_params=pltpu.CompilerParams(vmem_limit_bytes=32 * 2**20),
        cost_estimate=SMALL,
        name="right_pieces",
    )(relative, pieces, table_left, token_left, start_grad, *rights, *lefts)


def whole_kernel(widths, relative_ref, pieces_ref, whole_ref, grams_ref):
    piece = pieces_ref.shape[2]
    for j in range(pieces_ref.shape[0]):
        whole_ref[:, pl.ds(pl.multiple_of(relative_ref[j] * piece, LANES), piece)] = pieces_ref[j]
    start = 0
    for k, width in enumerate(widths):
        right = whole_ref[:, start : start + width]
        grams_ref[k] = dot_over(right, right, 1, 1, FINE)
        start += width


def whole_and_grams(relative, pieces, widths):
    count, unused_rank, piece = pieces.shape
    return pl.pallas_call(
        functools.partial(whole_kernel, widths),
        in_specs=[pl.BlockSpec(memory_space=pltpu.SMEM), pl.BlockSpec(memory_space=pltpu.VMEM)],
        out_shape=[
            jax.ShapeDtypeStruct((RANK, count * piece), F32),
            jax.ShapeDtypeStruct((len(widths), RANK, RANK), F32),
        ],
        cost_estimate=SMALL,
        name="whole_and_grams",
    )(relative, pieces)


def table_error_kernel(moved_ref, ids_ref, start_ref, ortho_ref, right_ref, out_ref):
    rows = moved_ref.shape[0]
    at = pl.program_id(0) * rows + lax.broadcasted_iota(jnp.int32, (rows, ids_ref.shape[1]), 0)
    hot = jnp.where(at == ids_ref[...], 1.0, 0.0).astype(BF16)
    ortho, right = pair_rows(-ortho_ref[...], right_ref[...])
    out_ref[...] = moved_ref[...] + matmul(hot, start_ref[...]) + matmul_outer(ortho, right)


def table_error(moved, ids, start_all, ortho, right):
    height, width = moved.shape
    rows = 512
    return pl.pallas_call(
        table_error_kernel,
        grid=(pl.cdiv(height, rows),),
        in_specs=[
            pl.BlockSpec((rows, width), lambda i: (i, 0)),
            pl.BlockSpec(ids.shape, lambda i: (0, 0)),
            pl.BlockSpec(start_all.shape, lambda i: (0, 0)),
            pl.BlockSpec((RANK, rows), lambda i: (0, i)),
            pl.BlockSpec((RANK, width), lambda i: (0, 0)),
        ],
        out_specs=pl.BlockSpec((rows, width), lambda i: (i, 0)),
        out_shape=jax.ShapeDtypeStruct((height, width), F32),
        compiler_params=pltpu.CompilerParams(vmem_limit_bytes=40 * 2**20),
        cost_estimate=SMALL,
        name="table_error",
    )(moved, ids, start_all, ortho, right)


def pack(matrices, width):
    pieces = []
    for matrix in matrices:
        matrix = matrix.astype(BF16)
        pieces += [matrix[:, k : k + width] for k in range(0, matrix.shape[1], width)]
    return jnp.concatenate(pieces, axis=0)


def unpack(packed, first, count, height):
    devices, unused_rows, width = packed.shape
    part = packed[:, first * height : (first + count) * height].reshape(devices, count, height, width)
    return part.transpose(0, 2, 1, 3).reshape(devices * height, count * width)


def columns_kernel(x_ref, w_ref, out_ref):
    weights = w_ref[...].reshape(-1, w_ref.shape[2])
    out_ref[...] = matmul(x_ref[...], weights).astype(out_ref.dtype)


def columns_back_kernel(x_ref, w_ref, out_ref):
    part = matmul_back(x_ref[...], w_ref[...].reshape(-1, w_ref.shape[2]))
    first = pl.program_id(0) == 0

    @pl.when(first)
    def _():
        out_ref[...] = part

    @pl.when(jnp.logical_not(first))
    def _():
        out_ref[...] += part


def rows_kernel(x_ref, w_ref, out_ref):
    part = matmul(x_ref[...], w_ref[...].reshape(-1, w_ref.shape[2]))
    first = pl.program_id(0) == 0

    @pl.when(first)
    def _():
        out_ref[...] = part

    @pl.when(jnp.logical_not(first))
    def _():
        out_ref[...] += part


def rows_back_kernel(x_ref, w_ref, out_ref):
    out_ref[...] = matmul_back(x_ref[...], w_ref[...].reshape(-1, w_ref.shape[2]))


def packed_call(kernel, x, packed, block, index, steps, x_step, out_width, out_step, dtype):
    tokens = x.shape[0]
    rows = x_step if x_step else x.shape[1]
    columns = out_step if out_step else out_width
    return pl.pallas_call(
        kernel,
        grid=(steps,),
        in_specs=[
            pl.BlockSpec((tokens, rows), (lambda j: (0, j)) if x_step else (lambda j: (0, 0))),
            pl.BlockSpec(block, index),
        ],
        out_specs=pl.BlockSpec((tokens, columns), (lambda j: (0, j)) if out_step else (lambda j: (0, 0))),
        out_shape=jax.ShapeDtypeStruct((tokens, out_width), dtype),
        compiler_params=pltpu.CompilerParams(vmem_limit_bytes=32 * 2**20),
        cost_estimate=SMALL,
        name=kernel.__name__,
    )(x, packed)


class Packed:
    def __init__(self, packed, height):
        self.packed, self.height = packed, height
        self.devices, self.rows, self.width = packed.shape
        self.plain = height % 16 != 0

    def columns(self, x, first, count, dtype=F32):
        if self.plain:
            return matmul(x, unpack(self.packed, first, count, self.height)).astype(dtype)
        block = (self.devices, self.height, self.width)
        return packed_call(
            columns_kernel, x, self.packed, block, lambda j: (0, first + j, 0), count, 0,
            count * self.width, self.width, dtype,
        )

    def columns_back(self, x, first, count):
        if self.plain:
            return matmul_back(x, unpack(self.packed, first, count, self.height))
        block = (self.devices, self.height, self.width)
        return packed_call(
            columns_back_kernel, x, self.packed, block, lambda j: (0, first + j, 0), count,
            self.width, self.devices * self.height, 0, F32,
        )

    def down_rows(self, height):
        return self.packed[:, self.rows - height :].reshape(-1, self.width)

    def rows_of(self, x, height):
        if self.plain:
            return matmul(x, self.down_rows(height))
        group = self.width // height
        block, at = (group, height, self.width), self.rows // height - 1
        return packed_call(
            rows_kernel, x, self.packed, block, lambda j: (j, at, 0), self.devices // group,
            group * height, self.width, 0, F32,
        )

    def rows_back(self, x, height):
        if self.plain:
            return matmul_back(x, self.down_rows(height))
        group = self.width // height
        block, at = (group, height, self.width), self.rows // height - 1
        return packed_call(
            rows_back_kernel, x, self.packed, block, lambda j: (j, at, 0), self.devices // group,
            0, self.devices * height, group * height, F32,
        )


def write_rows(grad, send_ref, rep_count, height):
    shard_count = send_ref.shape[0]
    for d in range(shard_count):
        for a in range(rep_count):
            first = (a * shard_count + d) * height
            send_ref[d, a * height : (a + 1) * height] = grad[first : first + height].astype(BF16)


def gelu_and_slope(x):
    root = math.sqrt(2.0 / math.pi)
    t = jnp.tanh(root * (x + 0.044715 * (x * x * x)))
    slope = 0.5 * (1.0 + t) + 0.5 * x * (1.0 - t * t) * root * (1.0 + 3 * 0.044715 * (x * x))
    return x * (0.5 * (1.0 + t)), slope


def mlp_part_kernel(height, at_ref, two_ref, down_in_ref, up_ref, down_ref, send_ref, grad_ref):
    two, down_in = two_ref[...], down_in_ref[...]
    up_value = matmul(two, up_ref[...].reshape(two.shape[1], -1))
    activated, slope = gelu_and_slope(up_value)
    up_in = (matmul_back(down_in, down_ref[0]) * slope).astype(BF16)
    grad_ref[...] = matmul_outer(activated.astype(BF16), down_in)
    write_rows(matmul_outer(two, up_in), send_ref, pl.num_programs(0), height)


def mlp_part(shard_at, two_all, down_all, packed, height, down_height, shard_count, rep_count):
    rows, width = two_all.shape
    devices = packed.shape[0]
    last = packed.shape[1] // down_height - 1
    whole = pl.BlockSpec((rows, width), lambda a, at: (0, 0))
    return pl.pallas_call(
        functools.partial(mlp_part_kernel, height),
        grid_spec=pltpu.PrefetchScalarGridSpec(
            num_scalar_prefetch=1,
            grid=(rep_count,),
            in_specs=[
                whole,
                whole,
                pl.BlockSpec((devices, height, down_height), lambda a, at: (0, 4 + a, at[0])),
                pl.BlockSpec(
                    (1, down_height, width), lambda a, at: (a * shard_count + at[0], last, 0)
                ),
            ],
            out_specs=[
                pl.BlockSpec((shard_count, rep_count * height, down_height), lambda a, at: (0, 0, a)),
                pl.BlockSpec((down_height, width), lambda a, at: (a, 0)),
            ],
        ),
        out_shape=[
            jax.ShapeDtypeStruct(
                (shard_count, rep_count * height, rep_count * down_height), BF16
            ),
            jax.ShapeDtypeStruct((rep_count * down_height, width), F32),
        ],
        compiler_params=pltpu.CompilerParams(vmem_limit_bytes=40 * 2**20),
        cost_estimate=SMALL,
        name="mlp_part",
    )(shard_at.reshape(1), two_all, down_all, packed, packed)


def qkv_part_kernel(rep_count, height, one_ref, part_ref, send_ref):
    write_rows(matmul_outer(one_ref[...], part_ref[...]), send_ref, rep_count, height)


def qkv_part(one_all, part, height, shard_count, rep_count):
    return pl.pallas_call(
        functools.partial(qkv_part_kernel, rep_count, height),
        out_shape=jax.ShapeDtypeStruct((shard_count, rep_count * height, part.shape[1]), BF16),
        compiler_params=pltpu.CompilerParams(vmem_limit_bytes=32 * 2**20),
        cost_estimate=SMALL,
        name="qkv_part",
    )(one_all, part)


def out_part_kernel(rep_count, shard_count, at_ref, left_ref, right_ref, out_ref, whole_ref):
    whole_ref[...] = matmul_outer(left_ref[...], right_ref[...])
    height = out_ref.shape[0] // rep_count
    for a in range(rep_count):
        first = pl.multiple_of((a * shard_count + at_ref[0]) * height, height)
        out_ref[a * height : (a + 1) * height] = whole_ref[pl.ds(first, height)]


def out_part(shard_at, left, right, shard_count, rep_count):
    rows, width = left.shape
    columns = 512
    return pl.pallas_call(
        functools.partial(out_part_kernel, rep_count, shard_count),
        grid=(right.shape[1] // columns,),
        in_specs=[
            pl.BlockSpec(memory_space=pltpu.SMEM),
            pl.BlockSpec((rows, width), lambda j: (0, 0)),
            pl.BlockSpec((rows, columns), lambda j: (0, j)),
        ],
        out_specs=pl.BlockSpec((width // shard_count, columns), lambda j: (0, j)),
        out_shape=jax.ShapeDtypeStruct((width // shard_count, right.shape[1]), F32),
        scratch_shapes=[pltpu.VMEM((width, columns), F32)],
        compiler_params=pltpu.CompilerParams(vmem_limit_bytes=32 * 2**20),
        cost_estimate=SMALL,
        name="out_part",
    )(shard_at.reshape(1), left, right)


def finish_kernel(shrink_ref, *refs):
    ortho_ref, own_ref, right_ref, grad_ref, error_ref, moment_ref, master_ref = refs[:7]
    new_error_ref, new_moment_ref, new_master_ref = refs[7:]
    grad = grad_ref[...]
    if len(grad.shape) == 3:
        grad = jnp.concatenate([grad[k] for k in range(grad.shape[0])], axis=1).astype(F32)
    minus, right = pair_rows(-ortho_ref[...], right_ref[...])
    new_error_ref[...] = grad + error_ref[...] + matmul_outer(minus, right)
    update(shrink_ref, own_ref, right_ref, moment_ref, master_ref, new_moment_ref, new_master_ref)


def update(shrink_ref, own_ref, right_ref, moment_ref, master_ref, new_moment_ref, new_master_ref):
    own, right = pair_rows(own_ref[...], right_ref[...])
    moment = MOMENTUM * moment_ref[...] + shrink_ref[0] * matmul_outer(own, right)
    new_moment_ref[...] = moment
    new_master_ref[...] = master_ref[...] - LEARN_RATE * moment


def finish(shrink, ortho, own_ortho, right_all, first, grad, error, moment, master, step):
    height, width = error.shape
    own = moment.shape[0]
    row, own_row = pl.BlockSpec((height, step), lambda j: (0, j)), pl.BlockSpec((own, step), lambda j: (0, j))
    if grad.ndim == 3:
        grad_spec = pl.BlockSpec(
            (grad.shape[0], height, step // grad.shape[0]), lambda j: (0, 0, j)
        )
    else:
        grad_spec = row
    return pl.pallas_call(
        finish_kernel,
        grid=(width // step,),
        in_specs=[
            pl.BlockSpec(memory_space=pltpu.SMEM),
            pl.BlockSpec((RANK, height), lambda j: (0, 0)),
            pl.BlockSpec((RANK, own), lambda j: (0, 0)),
            pl.BlockSpec((RANK, step), lambda j: (0, first // step + j)),
            grad_spec,
            row,
            own_row,
            own_row,
        ],
        out_specs=[row, own_row, own_row],
        out_shape=[
            jax.ShapeDtypeStruct((height, width), F32),
            jax.ShapeDtypeStruct((own, width), F32),
            jax.ShapeDtypeStruct((own, width), F32),
        ],
        compiler_params=pltpu.CompilerParams(vmem_limit_bytes=32 * 2**20),
        cost_estimate=SMALL,
        name="finish",
    )(shrink, ortho, own_ortho, right_all, grad, error, moment, master)


def finish_table(shrink, own_ortho, right_all, first, moment, master, step):
    own, width = moment.shape
    own_row = pl.BlockSpec((own, step), lambda j: (0, j))
    return pl.pallas_call(
        update,
        grid=(width // step,),
        in_specs=[
            pl.BlockSpec(memory_space=pltpu.SMEM),
            pl.BlockSpec((RANK, own), lambda j: (0, 0)),
            pl.BlockSpec((RANK, step), lambda j: (0, first // step + j)),
            own_row,
            own_row,
        ],
        out_specs=[own_row, own_row],
        out_shape=[jax.ShapeDtypeStruct((own, width), F32)] * 2,
        compiler_params=pltpu.CompilerParams(vmem_limit_bytes=32 * 2**20),
        cost_estimate=SMALL,
        name="finish_table",
    )(shrink, own_ortho, right_all, moment, master)


def shards(
    token_ids,
    targets,
    valid_mask,
    mem_index,
    memory,
    w_qkv,
    w_out,
    w_up,
    w_down,
    embed_table,
    gain_vector,
    mom_qkv,
    mom_out,
    mom_up,
    mom_down,
    mom_table,
    mom_gains,
    err_qkv,
    err_out,
    err_up,
    err_down,
    err_table,
    fac_qkv,
    fac_out,
    fac_up,
    fac_down,
    fac_table,
):
    rep_count = lax.axis_size("rep")
    shard_count = lax.axis_size("shard")
    rep_at = lax.axis_index("rep")
    shard_at = lax.axis_index("shard")
    micro_count, length = token_ids.shape[1:]
    tokens = micro_count * length
    model_width = w_out.shape[1]
    block_rows = embed_table.shape[0]
    masters = (w_qkv, w_out, w_up, w_down, embed_table, gain_vector)
    errors = (err_qkv, err_out, err_up, err_down, err_table)
    factors = (fac_qkv, fac_out, fac_up, fac_down, fac_table)
    relative = shard_at ^ jnp.arange(shard_count)

    own_rows = jnp.stack(
        [token_ids.reshape(tokens), targets.reshape(tokens), valid_mask.reshape(tokens)]
    )
    group_rows = in_order(spread_small(own_rows, "shard"), relative)
    group_ids = group_rows[:, 0].reshape(-1)
    group_targets = group_rows[:, 1].reshape(-1)
    group_valid = group_rows[:, 2].reshape(-1).astype(F32)
    valid_count = sum_over(jnp.full((8, LANES), jnp.sum(group_valid)), "rep")[0, 0]

    blocks = {0: embed_table.astype(BF16)}
    for bit in bits_of("rep")[::-1]:
        blocks.update({j ^ bit: swap(block, "rep", bit) for j, block in list(blocks.items())})
    vocab = jnp.zeros((rep_count, block_rows, model_width), BF16)
    for j, block in blocks.items():
        vocab = lax.dynamic_update_index_in_dim(vocab, block, rep_at ^ j, 0)
    vocab = vocab.reshape(-1, model_width)
    vocab_rows = vocab.shape[0]
    packed = lax.all_gather(pack(masters[:4], model_width), ("rep", "shard"), axis=0, tiled=False)
    qkv_height, down_height = w_qkv.shape[0], w_down.shape[0]
    ff_blocks = w_up.shape[1] // model_width

    flat_errors = [error.reshape(-1, error.shape[-1]) for error in errors]
    error_left = [
        dot_over(factor, error, 0, 1, FINE) for factor, error in zip(factors, flat_errors)
    ]
    factor_parts = [stacked_parts(factor.T) for factor in factors]
    left_width = rep_count * shard_count * sum(matrix.shape[0] for matrix in masters[:4])
    left_width = -(-left_width // (shard_count * LANES)) * shard_count * LANES
    left_base = []
    for part, matrix in zip(error_left[:4], masters[:4]):
        spread = jnp.zeros((RANK, rep_count, shard_count, matrix.shape[0]), F32)
        part = part.reshape(RANK, rep_count, 1, matrix.shape[0])
        spread = lax.dynamic_update_slice_in_dim(spread, part, shard_at, 2)
        left_base.append(spread.reshape(RANK, -1))
    left_base = jnp.concatenate(left_base, axis=1)
    left_base = jnp.pad(left_base, ((0, 0), (0, left_width - left_base.shape[1])))
    vocab, table_left, left_base, factor_parts = lax.optimization_barrier(
        (vocab, error_left[4], left_base, factor_parts)
    )
    weights = Packed(packed, qkv_height)

    vocab_slots = jnp.arange(vocab_rows)

    def places(id_values):
        block_index = id_values // block_rows
        column = block_index // shard_count * block_rows + id_values % block_rows
        return jnp.where(block_index % shard_count == shard_at, column, -1)

    def hits(id_values):
        return places(id_values)[:, None] == vocab_slots[None, :]

    token_hot = hits(group_ids).astype(BF16)
    embed_scale = math.sqrt(model_width)
    picked_rows = matmul(token_hot, vocab).astype(BF16)
    start_rows = embed_scale * scatter_sum_halves(
        picked_rows.reshape(shard_count, tokens, model_width), "shard", BF16
    ).astype(F32)

    gain_attn = gain_vector[:model_width]
    gain_mlp = gain_vector[model_width : 2 * model_width]
    gain_final = gain_vector[2 * model_width : 3 * model_width]
    opening = jax.nn.sigmoid(gain_vector[3 * model_width :])
    head_width = model_width // HEADS
    opening_row = jnp.repeat(opening, head_width)[None]
    picks = jnp.transpose(mem_index.reshape(tokens, HEADS, -1), (1, 0, 2))
    picks = picks.reshape(HEADS, tokens // 8, -1)
    token_of_pick = jnp.arange(picks.shape[2]) // mem_index.shape[-1]
    block_codes = picks // LANES * 8 + token_of_pick
    block_codes = block_codes.astype(BF16)
    lane_codes = (picks % LANES).astype(BF16)

    normed_one, inverse_one = norm_rows(start_rows, gain_attn)
    hidden_one = normed_one.astype(BF16)
    projected = weights.columns(hidden_one, 0, 3, BF16)
    attended, difference, mem_weights = attend(
        projected, memory, block_codes, lane_codes, opening_row, length
    )
    after_attn = start_rows + weights.columns(attended, 3, 1)
    normed_two, inverse_two = norm_rows(after_attn, gain_mlp)
    hidden_two = normed_two.astype(BF16)
    up_value = weights.columns(hidden_two, 4, ff_blocks)
    activated = jax.nn.gelu(up_value).astype(BF16)
    after_mlp = after_attn + weights.rows_of(activated, down_height)
    final_norm, final_inverse = norm_rows(after_mlp, gain_final)

    final_all = gather_halves(final_norm.astype(BF16), "shard")
    target_rows = places(group_targets)[None]
    logits, stats = logits_and_stats(vocab, final_all, target_rows)
    peak_value, exp_total, picked_logit = stats[0], stats[1], stats[2]
    for bit in bits_of("shard"):
        mine = jnp.stack([peak_value, exp_total, picked_logit])
        theirs = swap(mine, "shard", bit).reshape((3, shard_count // (2 * bit), 2, bit, tokens))
        theirs = jnp.flip(theirs, 2).reshape(3, -1)
        new_peak = jnp.maximum(peak_value, theirs[0])
        exp_total = exp_total * jnp.exp(peak_value - new_peak) + theirs[1] * jnp.exp(
            theirs[0] - new_peak
        )
        peak_value, picked_logit = new_peak, picked_logit + theirs[2]
    log_total = peak_value + jnp.log(exp_total)
    loss_own = jnp.sum((group_valid * (log_total - picked_logit))[:tokens])
    logit_grad, final_part = logits_back(
        logits, vocab, log_total[None], (group_valid / valid_count)[None], target_rows
    )
    final_part = final_part.reshape(shard_count, tokens, model_width)
    final_grad, logit_grad = scatter_sum_halves(final_part, "shard", BF16, logit_grad)
    moved_table = table_gradient(logit_grad, final_all, flat_errors[4])
    final_narrow = rows_by_narrow(factor_parts[4], final_all, 1)
    table_left = table_left + rows_by_narrow(stacked_parts(final_narrow), logit_grad, 1)
    one_all, attended_all, two_all = [
        lax.all_gather(left, "shard", axis=0, tiled=True)
        for left in (hidden_one, attended, hidden_two)
    ]
    final_grad, moved_table, table_left, one_all, attended_all, two_all = lax.optimization_barrier(
        (final_grad, moved_table, table_left, one_all, attended_all, two_all)
    )

    mlp_grad, gain_final_grad = norm_back(after_mlp, final_inverse, gain_final, final_grad)
    down_in = mlp_grad.astype(BF16)
    act_grad = weights.rows_back(down_in, down_height)
    unused_value, gelu_pull = jax.vjp(jax.nn.gelu, up_value)
    up_in = gelu_pull(act_grad)[0].astype(BF16)
    norm_two_grad, gain_mlp_grad = norm_back(
        after_attn, inverse_two, gain_mlp, weights.columns_back(up_in, 4, ff_blocks)
    )
    attn_grad = mlp_grad + norm_two_grad
    out_in = attn_grad.astype(BF16)
    mixture_grad = weights.columns_back(out_in, 3, 1)
    query_in, key_in, value_in, qkv_parts, gate_row = attend_back(
        projected, memory, mem_weights, mixture_grad, difference, opening_row, length
    )
    gate_grad = jnp.sum(gate_row.reshape(HEADS, head_width), axis=1) * opening * (1.0 - opening)
    qkv_in = jnp.concatenate([query_in, key_in, value_in], axis=1)
    norm_one_grad, gain_attn_grad = norm_back(
        start_rows, inverse_one, gain_attn, weights.columns_back(qkv_in, 0, 3)
    )
    start_grad = embed_scale * (attn_grad + norm_one_grad)
    gain_grad = jnp.concatenate([gain_attn_grad, gain_mlp_grad, gain_final_grad, gate_grad])

    lefts = (hidden_one, attended, hidden_two, activated)
    rights = (qkv_in, out_in, up_in, down_in)

    def everyone_of(array):
        return lax.all_gather(array, "shard", axis=0, tiled=True)

    def exchange(array):
        return lax.all_to_all(array, "shard", 0, 0, tiled=False)

    def columns_to_rows(grad):
        width, parts, each = grad.shape
        height = width // (rep_count * shard_count)
        grad = grad.astype(BF16).reshape(rep_count, shard_count, height * parts * each)
        grad = exchange(grad.transpose(1, 0, 2))
        grad = grad.reshape(shard_count, rep_count * height, parts, each).transpose(1, 2, 0, 3)
        return grad.reshape(rep_count * height, -1)

    heights = [left.shape[1] // (rep_count * shard_count) for left in lefts]
    slab_widths = [rep_count * height for height in heights]
    starts = [sum(slab_widths[:k]) for k in range(5)]
    down_all, out_all = everyone_of(down_in), everyone_of(out_in)
    qkv_in_part = exchange(
        qkv_parts.reshape(HEADS, tokens, 3, shard_count // HEADS, -1)
        .transpose(0, 3, 1, 2, 4)
        .reshape(shard_count, tokens, -1)
    ).reshape(shard_count * tokens, -1)
    if weights.plain:
        up_slices = [
            lax.dynamic_slice_in_dim(
                packed[:, (4 + k) * qkv_height : (5 + k) * qkv_height],
                shard_at * down_height,
                down_height,
                2,
            ).reshape(model_width, down_height)
            for k in range(rep_count)
        ]
        down_slab = jnp.concatenate(
            [
                lax.dynamic_index_in_dim(packed, k * shard_count + shard_at, 0, False)[-down_height:]
                for k in range(rep_count)
            ],
            axis=0,
        )
        up_part = matmul(two_all, jnp.concatenate(up_slices, axis=1))
        act_part, part_pull = jax.vjp(jax.nn.gelu, up_part)
        up_in_part = part_pull(matmul_back(down_all, down_slab))[0].astype(BF16)
        attended_part = lax.dynamic_index_in_dim(
            attended_all.reshape(-1, rep_count, shard_count, heights[1]), shard_at, 2, False
        ).reshape(-1, slab_widths[1])
        slab_grads = [
            columns_to_rows(matmul_outer(one_all, qkv_in_part).reshape(model_width, 3, -1)),
            matmul_outer(attended_part, out_all),
            columns_to_rows(matmul_outer(two_all, up_in_part).reshape(model_width, rep_count, -1)),
            matmul_outer(act_part.astype(BF16), down_all),
        ]
    else:
        up_send, down_grad = mlp_part(
            shard_at, two_all, down_all, packed, qkv_height, down_height, shard_count, rep_count
        )

    start_grad, down_all = lax.optimization_barrier((start_grad, down_all))
    left_blocks, start_narrow = left_pieces(
        relative, left_base, fac_table.T, start_grad, factor_parts[:4], rights, lefts
    )
    own_left, start_narrow, unused_arrival = scatter_and_gather(
        left_blocks, start_narrow[None], "shard", bits_of("shard")
    )
    start_narrow = start_narrow[:, 0].transpose(1, 0, 2).reshape(RANK, -1)
    table_left = table_left + rows_by_narrow(stacked_parts(start_narrow), token_hot, 0)
    tiles = own_left.shape[0]
    table_pad = -vocab_rows % LANES
    left_sum = jnp.concatenate(
        [own_left, to_tiles(jnp.pad(table_left, ((0, 0), (0, table_pad))))], axis=0
    )
    left_sum = sum_over(left_sum, "rep")
    own_left, table_tiles = left_sum[:tiles], left_sum[tiles:]
    table_left = from_tiles(table_tiles)[:, :vocab_rows]
    table_gram = lax.dot_general(
        table_tiles,
        table_tiles,
        (((0, 2), (0, 2)), ((), ())),
        precision=FINE,
        preferred_element_type=F32,
    )
    table_gram = jnp.pad(table_gram, ((0, 0), (0, LANES - RANK)))[None]
    token_left = rows_by_narrow(stacked_parts(table_left), token_hot, 1)
    token_left = token_left.reshape(RANK, shard_count, tokens).transpose(1, 0, 2)
    token_left, payloads, arrival = scatter_and_gather(
        token_left[:, None],
        jnp.concatenate([own_left, table_gram], axis=0),
        "shard",
        bits_of("shard")[::-1],
    )
    arrival = shard_at ^ arrival

    if not weights.plain:
        payloads, up_send, down_grad = lax.optimization_barrier((payloads, up_send, down_grad))
    ortho, table_ortho, right_part, token_right, squares = right_pieces(
        arrival, payloads, table_left, token_left[0], start_grad, rights, lefts
    )
    slab_orthos, first = [], 0
    for left, height in zip(lefts, heights):
        full = ortho[:, first : first + left.shape[1]]
        first += left.shape[1]
        full = full.reshape(RANK, rep_count, shard_count, height)
        slab_orthos.append(
            lax.dynamic_index_in_dim(full, shard_at, 2, False).reshape(RANK, rep_count * height)
        )
    slab_orthos.append(table_ortho)
    error_right = [
        dot_over(slab, error, 1, 0, FAIR) for slab, error in zip(slab_orthos, flat_errors[:4])
    ]
    table_right = dot_over(table_ortho, moved_table, 1, 0, FAIR)
    table_right = table_right + token_right
    widths = [right.shape[1] for right in rights] + [model_width]
    extra = jnp.concatenate([gain_grad, loss_own[None], squares[4].reshape(-1)])
    total_width = sum(widths) + -(-extra.shape[0] // RANK)
    piece = -(-total_width // (shard_count * LANES)) * LANES
    extra_width = piece * shard_count - sum(widths)
    extra = jnp.pad(extra, (0, extra_width * RANK - extra.shape[0])).reshape(RANK, extra_width)
    pieces = jnp.concatenate(
        [right_part + jnp.concatenate(error_right, axis=1), table_right, extra], axis=1
    )
    pieces = in_order(pieces.reshape(RANK, shard_count, piece).transpose(1, 0, 2), relative)
    pieces, qkv_in_part = lax.optimization_barrier((pieces, qkv_in_part))
    own_piece = scatter_sum(pieces, "shard", bits_of("shard"))
    start_all = everyone_of(start_grad.astype(BF16))
    if not weights.plain:
        qkv_send = qkv_part(one_all, qkv_in_part, qkv_height, shard_count, rep_count)
        out_grad = out_part(shard_at, attended_all, out_all, shard_count, rep_count)
        slab_grads = [exchange(qkv_send), out_grad, exchange(up_send), down_grad]
    own_piece = sum_over(own_piece, "rep")
    pieces, unused_arrival = gather_arrivals(own_piece, "shard")
    gain_count = gain_grad.shape[0]
    right_all, right_grams = whole_and_grams(arrival, pieces, widths)
    extra = right_all[:, sum(widths) :].reshape(-1)
    gain_sum, loss_sum = extra[:gain_count], extra[gain_count]
    table_square = extra[gain_count + 1 : gain_count + 1 + RANK * RANK].reshape(RANK, RANK)
    squares = jnp.concatenate([squares[:4], table_square[None] / rep_count], axis=0)
    right_sums = [right_all[:, sum(widths[:k]) : sum(widths[: k + 1])] for k in range(5)]
    clip_norm = jnp.sqrt(jnp.sum(gain_sum * gain_sum) + jnp.sum(squares * right_grams))
    shrink = jnp.minimum(1.0, CLIP_LEVEL / clip_norm).reshape(1)

    ids_in_order = in_order(places(group_ids).reshape(shard_count, tokens), relative)
    moments = (mom_qkv, mom_out, mom_up, mom_down, mom_table, mom_gains)
    new_errors, new_moments, new_weights = [], [], []
    for k in range(5):
        height = flat_errors[k].shape[0] // rep_count
        own_ortho = lax.dynamic_slice_in_dim(slab_orthos[k], rep_at * height, height, 1)
        first = sum(widths[:k])
        if k < 4:
            new_error, new_moment, new_weight = finish(
                shrink, slab_orthos[k], own_ortho, right_all, first, slab_grads[k], flat_errors[k],
                moments[k], masters[k], model_width,
            )
        else:
            new_moment, new_weight = finish_table(
                shrink, own_ortho, right_all, first, moments[k], masters[k], model_width // 4
            )
            new_error = table_error(
                moved_table, ids_in_order.reshape(1, -1), start_all, table_ortho, right_sums[4]
            )
        new_errors.append(new_error.reshape(errors[k].shape))
        new_moments.append(new_moment)
        new_weights.append(new_weight)
    new_moments.append(MOMENTUM * mom_gains + shrink * gain_sum)
    new_weights.append(gain_vector - LEARN_RATE * new_moments[5])
    return (
        loss_sum,
        valid_count,
        clip_norm,
        *new_moments,
        *new_weights,
        *new_errors,
        *[right.T for right in right_sums],
    )


def solution(mesh):
    everyone = P(("rep", "shard"), None)
    group = P("rep", None, "shard")
    buffer = P("rep", "shard", None, None, None)
    return jax.shard_map(
        shards,
        mesh=mesh,
        in_specs=(group,) * 3
        + (P("rep", None, "shard", None, None), P())
        + (everyone,) * 5
        + (P(),)
        + (everyone,) * 5
        + (P(),)
        + (buffer,) * 5
        + (P(),) * 5,
        out_specs=(P(),) * 3
        + (everyone,) * 5
        + (P(),)
        + (everyone,) * 5
        + (P(),)
        + (buffer,) * 5
        + (P(),) * 5,
        check_vma=False,
    )
```

time: 1000 us -> 713 us (0.71)
  matrix products: 248 us -> 60.3 us
  waiting for transfers between devices: 400 us -> 238 us
  Pallas kernels: 99.2 us -> 202 us
  other arithmetic: 90.6 us -> 48.8 us
    all_gather x9 -> x7, waiting for transfers between devices: 209 us -> 14.8 us  [the longest x1 10.5 us: shards(): lax.all_gather(pack(masters[:4], model_width), ('rep', 'shard'), axis=0,...]
    dot_general x76 -> x15, matrix products: 248 us -> 59.9 us  [dot_over(): lax.dot_general(left, right, (((left_dim,), (right_dim,)), ((), ())), pre...]
    pallas_call x0 -> x23, Pallas kernels: none -> 163 us  [the longest x8 37.7 us: packed_call(): pl.pallas_call(kernel, grid=(steps,), in_specs=[pl.BlockSpec((tokens, row...]
    pallas_call x1, Pallas kernels: 69.4 us -> 21.6 us  [attend(): pl.pallas_call(functools.partial(attend_kernel, length), grid=(HEADS,), i...]
    ppermute x55 -> x42, waiting for transfers between devices: 191 us -> 221 us  [swap(): return lax.ppermute(array, axis, [(i, i ^ bit) for i in range(size)])]
    sub x6 -> x1, other arithmetic: 17.1 us -> 0.62 us  [shards(): new_weights.append(gain_vector - LEARN_RATE * new_moments[5])]
    all_to_all x0 -> x3, starting transfers between devices: none -> 13.8 us  [exchange(): return lax.all_to_all(array, 'shard', 0, 0, tiled=False)]
    reduce_sum x3, other arithmetic: 16 us -> 2.69 us  [the longest x1 1.35 us: shards(): jnp.sum(squares * right_grams)]
  transfers between devices with their start and end apart: 65 -> 53, of which waited for: 37 -> 33; matrix products, arithmetic and copies ran while one was open for 40% -> 18% of each run, Pallas kernels for 10% -> 26%
where the time goes in v2:
time: 713 us; the launch traced here: 704 us
  waiting for transfers between devices  238 us (33%)
  Pallas kernels  202 us (28%)
  starting transfers between devices  73.6 us (10%)
  local copies, waits for them, and re-layouts  61.8 us (9%)
  matrix products  60.3 us (8%)
  other arithmetic  48.8 us (7%)
  between operations  19.4 us (3%)
    ppermute x42, waiting for transfers between devices, swap(): return lax.ppermute(array, axis, [(i, i ^ bit) for i in range(size)])  221 us
    dot_general x15, matrix products, dot_over(): lax.dot_general(left, right, (((left_dim,), (right_dim,)), ((), ())), pre...  59.9 us
    ppermute x42, starting transfers between devices, swap(): return lax.ppermute(array, axis, [(i, i ^ bit) for i in range(size)])  53.7 us
    pallas_call x8, Pallas kernels, packed_call(): pl.pallas_call(kernel, grid=(steps,), in_specs=[pl.BlockSpec((tokens, row...  37.7 us
    unnamed x324, local copies, waits for them, and re-layouts  32.5 us
    pallas_call x1, Pallas kernels, logits_back(): pl.pallas_call(functools.partial(logits_back_kernel, total), grid=(pl.cdi...  22.4 us
    pallas_call x1, Pallas kernels, attend(): pl.pallas_call(functools.partial(attend_kernel, length), grid=(HEADS,), i...  21.6 us
    pallas_call x1, Pallas kernels, table_gradient(): pl.pallas_call(table_gradient_kernel, grid=(pl.cdiv(total, 2 * HEAD_ROWS)...  20.7 us
  transfers between devices with their start and end apart: 53, of which 33 were waited for; matrix products, arithmetic and copies ran while one was open for 18% of the time, Pallas kernels for 26%

profile of v2, /device:TPU:0, one launch (start us, length us, event | category | flops | bytes accessed | tf_op | source)
XLA Modules:
  0.0 703.7 jit_solution(38261620368833055)
XLA Ops:
  22.4 5.8 all-to-all-start
  30.7 4.6 fusion.20
  40.3 17.7 %fusion.163 = f32[8,4000]{1,0:T(8,128)} fusion(f32[1024,8]{0,1:T(8,128)S(1)} %copy-done.59, f32[4000,1024]{1,0:T(8,128)} %bitcast.469), kind=kOutput, calls=%fused_computation.406 | convolution fusion | flops 393216000 | bytes 16544768 | tf_op jit(solution)/shard_map/dot_general | solution.py:26
  59.8 31.9 %collective-permute-done = bf16[1000,1024]{1,0:T(8,128)(2,1)} collective-permute-done((bf16[1000,1024]{1,0:T(8,128)(2,1)}, bf16[1000,1024]{1,0:T(8,128)(2,1)}, u32[]{:S(2)}, u32[]{:S(2)}) %collective-permute-start) | collective-permute-done | bytes 2048032 | tf_op jit(solution)/shard_map/ppermute | solution.py:78
  102.7 11.6 %fusion.17 = bf16[1024,1024]{1,0:T(8,128)(2,1)S(1)} fusion(bf16[4000,1024]{1,0:T(8,128)(2,1)} %bitcast.466, s32[1024]{0:T(1024)S(1)} %fusion.118), kind=kOutput, calls=%fused_computation.29 | convolution fusion | flops 8393752576 | bytes 10293248 | tf_op jit(solution)/shard_map/dot_general | solution.py:26
  118.0 22.3 %collective-permute-done.3 = bf16[2,2,128,512]{3,2,0,1:T(8,128)(2,1)S(1)} collective-permute-done((bf16[2,2,128,512]{3,2,0,1:T(8,128)(2,1)S(1)}, bf16[2,2,128,512]{3,2,0,1:T(8,128)(2,1)S(1)}, u32[]{:S(2)}, u32[]{:S(2)}) %collective-permute-start.3) | collective-permute-done | bytes 524320 | tf_op jit(solution)/shard_map/ppermute | solution.py:78
  141.9 19.1 %collective-permute-done.6 = bf16[2,2,128,512]{3,2,0,1:T(8,128)(2,1)S(1)} collective-permute-done((bf16[2,2,128,512]{3,2,0,1:T(8,128)(2,1)S(1)}, bf16[2,2,128,512]{3,2,0,1:T(8,128)(2,1)S(1)}, u32[]{:S(2)}, u32[]{:S(2)}) %collective-permute-start.6) | collective-permute-done | bytes 524320 | tf_op jit(solution)/shard_map/ppermute | solution.py:78
  161.7 13.1 %collective-permute-done.4 = bf16[2,128,512]{2,1,0:T(8,128)(2,1)S(1)} collective-permute-done((bf16[2,128,512]{2,1,0:T(8,128)(2,1)S(1)}, bf16[2,128,512]{2,1,0:T(8,128)(2,1)S(1)}, u32[]{:S(2)}, u32[]{:S(2)}) %collective-permute-start.4) | collective-permute-done | bytes 262176 | tf_op jit(solution)/shard_map/ppermute | solution.py:78
  178.0 14.1 %collective-permute-done.5 = bf16[128,512]{1,0:T(8,128)(2,1)S(1)} collective-permute-done((bf16[128,512]{1,0:T(8,128)(2,1)S(1)}, bf16[128,512]{1,0:T(8,128)(2,1)S(1)}, u32[]{:S(2)}, u32[]{:S(2)}) %collective-permute-start.5) | collective-permute-done | bytes 131104 | tf_op jit(solution)/shard_map/ppermute | solution.py:78
  192.1 9.9 %collective-permute-done.8 = bf16[128,512]{1,0:T(8,128)(2,1)S(1)} collective-permute-done((bf16[128,512]{1,0:T(8,128)(2,1)S(1)}, bf16[128,512]{1,0:T(8,128)(2,1)S(1)}, u32[]{:S(2)}, u32[]{:S(2)}) %collective-permute-start.8) | collective-permute-done | bytes 131104 | tf_op jit(solution)/shard_map/ppermute | solution.py:78
  204.6 10.5 %all-gather.21.cloned.1.call-done = bf16[12288,1024]{1,0:T(8,128)(2,1)} async-done(((bf16[384,1024]{1,0:T(8,128)(2,1)}), bf16[12288,1024]{1,0:T(8,128)(2,1)}) %all-gather.21.cloned.1.call-update) | async-done | bytes 25165840 | tf_op jit(solution)/shard_map/all_gather | solution.py:1024
  219.5 21.6 %attend.1 = (bf16[128,1024]{1,0:T(8,128)(2,1)}, f32[128,1024]{1,0:T(8,128)S(1)}, f32[8,128,4096]{2,1,0:T(8,128)}) custom-call(bf16[128,3072]{1,0:T(8,128)(2,1)S(1)} %columns_kernel.3.queries_ref.keys_ref.values_ref, bf16[128,3072]{1,0:T(8,128)(2,1)S(1)} %columns_kernel.3.queries_ref.keys_ref.values_ref, ...), custom_call_target="tpu_custom_call" | custom-call | flops 1000000 | bytes 100000 | tf_op jit(solution)/shard_map/attend/pallas_call | solution.py:326
  246.6 5.2 columns_kernel.5
  252.4 5.5 rows_kernel.1
  263.3 13.1 %collective-permute-done.9 = bf16[1,128,512]{2,1,0:T(8,128)(2,1)S(1)} collective-permute-done((bf16[1,128,512]{2,1,0:T(8,128)(2,1)S(1)}, bf16[1,128,512]{2,1,0:T(8,128)(2,1)S(1)}, u32[]{:S(2)}, u32[]{:S(2)}) %collective-permute-start.9) | collective-permute-done | bytes 131104 | tf_op jit(solution)/shard_map/ppermute | solution.py:78
  290.8 10.8 %collective-permute-done.11 = bf16[4,128,512]{2,1,0:T(8,128)(2,1)} collective-permute-done((bf16[4,128,512]{2,1,0:T(8,128)(2,1)}, bf16[4,128,512]{2,1,0:T(8,128)(2,1)}, u32[]{:S(2)}, u32[]{:S(2)}) %collective-permute-start.11) | collective-permute-done | bytes 524320 | tf_op jit(solution)/shard_map/ppermute | solution.py:78
  310.3 18.5 %logits.1 = (f32[4000,1024]{1,0:T(8,128)}, f32[3,1024]{1,0:T(4,128)S(1)}) custom-call(bf16[4000,1024]{1,0:T(8,128)(2,1)} %bitcast.467, bf16[1024,1024]{1,0:T(8,128)(2,1)} %pad_maximum_fusion.final_ref, s32[1,1024]{1,0:T(1,128)S(1)} %compare_select_fusion.target_ref), custom_call_target="tpu_custom_call" | custom-call | flops 1000000 | bytes 100000 | tf_op jit(solution)/shard_map/logits/pallas_call | solution.py:403
  343.4 22.4 %logits_back.1 = (bf16[4000,1024]{1,0:T(8,128)(2,1)}, f32[1024,1024]{1,0:T(8,128)}) custom-call(f32[4000,1024]{1,0:T(8,128)} %get-tuple-element.89.logits_ref, bf16[4000,1024]{1,0:T(8,128)(2,1)} %bitcast.468, f32[1,1024]{1,0:T(1,128)} %log_add_fusion.log_ref, f32[1,1024]{1,0:T(1,128)} %divide_bitcast_fusion.scale_ref, s32[1,1024]{1,0:T(1,128)} %copy-done.66), custom_call_target="tpu_custom_call" | custom-call | flops 1000000 | bytes 100000 | tf_op jit(solution)/shard_map/logits_back/pallas_call | solution.py:450
  375.5 20.7 %table_gradient.1.moved_ref = f32[4000,1024]{1,0:T(8,128)} custom-call(bf16[4000,1024]{1,0:T(8,128)(2,1)} %get-tuple-element.96.grad_ref, bf16[1024,1024]{1,0:T(8,128)(2,1)} %pad_maximum_fusion.final_ref, f32[4000,1024]{1,0:T(8,128)} %bitcast.470), custom_call_target="tpu_custom_call" | custom-call | flops 1000000 | bytes 100000 | tf_op jit(solution)/shard_map/table_gradient/pallas_call | solution.py:481
  401.6 4.5 collective-permute-done.21
  423.6 6.3 rows_back_kernel.1
  431.4 6.5 columns_back_kernel.3
  442.3 17.0 %attend_back.1 = (bf16[128,1024]{1,0:T(8,128)(2,1)S(1)}, bf16[128,1024]{1,0:T(8,128)(2,1)S(1)}, bf16[128,1024]{1,0:T(8,128)(2,1)S(1)}, bf16[8,128,384]{2,1,0:T(8,128)(2,1)S(1)}, f32[1,1024]{1,0:T(1,128)S(1)}) custom-call(bf16[128,3072]{1,0:T(8,128)(2,1)S(1)} %columns_kernel.3.queries_ref.keys_ref.values_ref, ...), custom_call_target="tpu_custom_call" | custom-call | flops 1000000 | bytes 100000 | tf_op jit(solution)/shard_map/attend_back/pallas_call | solution.py:350
  460.0 5.4 columns_back_kernel.5
  528.9 12.7 %mlp_part.1 = (bf16[8,128,512]{2,1,0:T(8,128)(2,1)S(1)}, f32[512,1024]{1,0:T(8,128)S(1)}) custom-call(s32[1]{0:T(128)} %bitcast.129.at_ref, bf16[1024,1024]{1,0:T(8,128)(2,1)S(1)} %copy-done.34, bf16[1024,1024]{1,0:T(8,128)(2,1)S(1)} %copy-done.35, bf16[32,384,1024]{2,1,0:T(8,128)(2,1)} %bitcast.464, bf16[32,384,1024]{2,1,0:T(8,128)(2,1)} %bitcast.465), custom_call_target="tpu_custom_call" | custom-call | flops 1000000 | bytes 100000 | tf_op jit(solution)/shard_map/mlp_part/pallas_call | solution.py:819
  541.9 6.4 right_pieces.1
  553.7 7.9 %fusion.162 = f32[8,1024]{1,0:T(8,128)S(1)} fusion(f32[8,1024]{1,0:T(8,128)S(1)} %copy-done.68, f32[8,4000]{1,0:T(8,128)S(1)} %get-tuple-element.119.ortho_ref, f32[4000,1024]{1,0:T(8,128)} %table_gradient.1.moved_ref), kind=kOutput, calls=%fused_computation.405 | convolution fusion | flops 196616192 | bytes 16577536 | tf_op jit(solution)/shard_map/dot_general | solution.py:26
  568.2 5.1 collective-permute-done.34
  609.3 16.5 %collective-permute-done.40 = f32[2,8,1408]{2,1,0:T(8,128)S(1)} collective-permute-done((f32[2,8,1408]{2,1,0:T(8,128)S(1)}, f32[2,8,1408]{2,1,0:T(8,128)S(1)}, u32[]{:S(2)}, u32[]{:S(2)}) %collective-permute-start.40) | collective-permute-done | bytes 90144 | tf_op jit(solution)/shard_map/ppermute | solution.py:78
  627.9 8.0 %collective-permute-done.41 = f32[4,8,1408]{2,1,0:T(8,128)S(1)} collective-permute-done((f32[4,8,1408]{2,1,0:T(8,128)S(1)}, f32[4,8,1408]{2,1,0:T(8,128)S(1)}, u32[]{:S(2)}, u32[]{:S(2)}) %collective-permute-start.41) | collective-permute-done | bytes 180256 | tf_op jit(solution)/shard_map/ppermute | solution.py:78
  642.2 5.4 all-to-all-start.3
  677.7 17.8 %table_error.1 = f32[4000,1024]{1,0:T(8,128)} custom-call(f32[4000,1024]{1,0:T(8,128)} %table_gradient.1.moved_ref, s32[1,1024]{1,0:T(1,128)S(1)} %bitcast.454, bf16[1024,1024]{1,0:T(8,128)(2,1)S(1)} %copy-done.46, f32[8,4000]{1,0:T(8,128)S(1)} %get-tuple-element.119.ortho_ref, f32[8,1024]{1,0:T(8,128)S(1)} %get-tuple-element.182.right_ref), custom_call_target="tpu_custom_call" | custom-call | flops 1000000 | bytes 100000 | tf_op jit(solution)/shard_map/table_error/pallas_call | solution.py:656
  (683 shorter events, 286.6 us)
Async XLA Ops:
  7.2 208.0 %all-gather.21.cloned.1.call-start = ((), (), s32[]{:S(2)}) async-start(), calls=%async_computation.10 | async-start | bytes 25952256 | tf_op jit(solution)/shard_map/all_gather | solution.py:1024
  18.6 73.1 %collective-permute-start = (bf16[1000,1024]{1,0:T(8,128)(2,1)}, bf16[1000,1024]{1,0:T(8,128)(2,1)}, u32[]{:S(2)}, u32[]{:S(2)}) collective-permute-start(bf16[1000,1024]{1,0:T(8,128)(2,1)} %get-tuple-element.170), channel_id=1, source_target_pairs={{0,16},{8,24},{16,0},{24,8},{1,17},{9,25},{17,1},{25,9},{2,18},{10... | collective-permute-start | bytes 6144008 | tf_op jit(solution)/shard_map/ppermute | solution.py:78
  21.5 76.7 %collective-permute-start.1 = (bf16[1000,1024]{1,0:T(8,128)(2,1)}, bf16[1000,1024]{1,0:T(8,128)(2,1)}, u32[]{:S(2)}, u32[]{:S(2)}) collective-permute-start(bf16[1000,1024]{1,0:T(8,128)(2,1)} %get-tuple-element.170), channel_id=1, source_target_pairs={{0,8},{8,0},{16,24},{24,16},{1,9},{9,1},{17,25},{25,17},{2,10},{10... | collective-permute-start | bytes 6144008 | tf_op jit(solution)/shard_map/ppermute | solution.py:78
  22.4 70.7 %all-to-all-start = ((s32[8,3,128]{2,1,0:T(4,128)}), s32[8,3,128]{2,1,0:T(4,128)S(1)}, u32[]{:S(2)}, u32[]{:S(2)}) async-start(s32[8,3,128]{2,1,0:T(4,128)} %broadcast_in_dim.83), calls=%async_computation | async-start | bytes 32768 | tf_op jit(solution)/shard_map/all_to_all | solution.py:183
  28.2 389.8 %all-gather.9.cloned.1.call-start = ((), (), s32[]{:S(2)}) async-start(), calls=%async_computation.4 | async-start | bytes 2359296 | tf_op jit(solution)/shard_map/all_gather | solution.py:1116
  91.6 9.6 %collective-permute-start.2 = (bf16[1000,1024]{1,0:T(8,128)(2,1)}, bf16[1000,1024]{1,0:T(8,128)(2,1)S(1)}, u32[]{:S(2)}, u32[]{:S(2)}) collective-permute-start(bf16[1000,1024]{1,0:T(8,128)(2,1)} %collective-permute-done), channel_id=1, source_target_pairs={{0,8},{8,0},{16,24},{24,16},{1,9},{9,1},{17,25},{25,17},{2,10},{10... | collective-permute-start | bytes 6144008 | tf_op jit(solution)/shard_map/ppermute | solution.py:78
  114.8 25.6 %collective-permute-start.3 = (bf16[2,2,128,512]{3,2,0,1:T(8,128)(2,1)S(1)}, bf16[2,2,128,512]{3,2,0,1:T(8,128)(2,1)S(1)}, u32[]{:S(2)}, u32[]{:S(2)}) collective-permute-start(bf16[2,2,128,512]{3,2,0,1:T(8,128)(2,1)S(1)} %bitcast.491), channel_id=1, source_target_pairs={{0,1},{1,0},{2,3},{3,2},{4,5},{5,4},{6,7},{7,6},{8,9},{9,8},{10,11... | collective-permute-start | bytes 1572872 | tf_op jit(solution)/shard_map/ppermute | solution.py:78
  116.2 44.7 %collective-permute-start.6 = (bf16[2,2,128,512]{3,2,0,1:T(8,128)(2,1)S(1)}, bf16[2,2,128,512]{3,2,0,1:T(8,128)(2,1)S(1)}, u32[]{:S(2)}, u32[]{:S(2)}) collective-permute-start(bf16[2,2,128,512]{3,2,0,1:T(8,128)(2,1)S(1)} %bitcast.490), channel_id=1, source_target_pairs={{0,2},{1,3},{2,0},{3,1},{4,6},{5,7},{6,4},{7,5},{8,10},{9,11},{10,... | collective-permute-start | bytes 1572872 | tf_op jit(solution)/shard_map/ppermute | solution.py:78
  140.4 34.4 %collective-permute-start.4 = (bf16[2,128,512]{2,1,0:T(8,128)(2,1)S(1)}, bf16[2,128,512]{2,1,0:T(8,128)(2,1)S(1)}, u32[]{:S(2)}, u32[]{:S(2)}) collective-permute-start(bf16[2,128,512]{2,1,0:T(8,128)(2,1)S(1)} %slice_bitcast_fusion.6), channel_id=1, source_target_pairs={{0,2},{1,3},{2,0},{3,1},{4,6},{5,7},{6,4},{7,5},{8,10},{9,11},{10,... | collective-permute-start | bytes 786440 | tf_op jit(solution)/shard_map/ppermute | solution.py:78
  161.1 15.4 %collective-permute-start.7 = (bf16[2,128,512]{2,1,0:T(8,128)(2,1)S(1)}, bf16[2,128,512]{2,1,0:T(8,128)(2,1)S(1)}, u32[]{:S(2)}, u32[]{:S(2)}) collective-permute-start(bf16[2,128,512]{2,1,0:T(8,128)(2,1)S(1)} %slice_bitcast_fusion.4), channel_id=1, source_target_pairs={{0,1},{1,0},{2,3},{3,2},{4,5},{5,4},{6,7},{7,6},{8,9},{9,8},{10,11... | collective-permute-start | bytes 786440 | tf_op jit(solution)/shard_map/ppermute | solution.py:78
  174.9 17.2 %collective-permute-start.5 = (bf16[128,512]{1,0:T(8,128)(2,1)S(1)}, bf16[128,512]{1,0:T(8,128)(2,1)S(1)}, u32[]{:S(2)}, u32[]{:S(2)}) collective-permute-start(bf16[128,512]{1,0:T(8,128)(2,1)S(1)} %slice_bitcast_fusion.12), channel_id=1, source_target_pairs={{0,4},{1,5},{2,6},{3,7},{4,0},{5,1},{6,2},{7,3},{8,12},{9,13},{10,... | collective-permute-start | bytes 393224 | tf_op jit(solution)/shard_map/ppermute | solution.py:78
  176.5 25.5 %collective-permute-start.8 = (bf16[128,512]{1,0:T(8,128)(2,1)S(1)}, bf16[128,512]{1,0:T(8,128)(2,1)S(1)}, u32[]{:S(2)}, u32[]{:S(2)}) collective-permute-start(bf16[128,512]{1,0:T(8,128)(2,1)S(1)} %slice_bitcast_fusion.10), channel_id=1, source_target_pairs={{0,4},{1,5},{2,6},{3,7},{4,0},{5,1},{6,2},{7,3},{8,12},{9,13},{10,... | collective-permute-start | bytes 393224 | tf_op jit(solution)/shard_map/ppermute | solution.py:78
  203.6 214.4 %all-gather.13.cloned.1.call-start = ((), (), s32[]{:S(2)}) async-start(), calls=%async_computation.6 | async-start | bytes 2359296 | tf_op jit(solution)/shard_map/all_gather | solution.py:1116
  245.6 172.4 %all-gather.11.cloned.1.call-start = ((), (), s32[]{:S(2)}) async-start(), calls=%async_computation.5 | async-start | bytes 2359296 | tf_op jit(solution)/shard_map/all_gather | solution.py:1116
  258.8 17.6 %collective-permute-start.9 = (bf16[1,128,512]{2,1,0:T(8,128)(2,1)S(1)}, bf16[1,128,512]{2,1,0:T(8,128)(2,1)S(1)}, u32[]{:S(2)}, u32[]{:S(2)}) collective-permute-start(bf16[1,128,512]{2,1,0:T(8,128)(2,1)S(1)} %get-tuple-element.186), channel_id=1, source_target_pairs={{0,4},{1,5},{2,6},{3,7},{4,0},{5,1},{6,2},{7,3},{8,12},{9,13},{10,... | collective-permute-start | bytes 393224 | tf_op jit(solution)/shard_map/ppermute | solution.py:78
  259.0 20.1 %collective-permute-start.12 = (bf16[1,128,512]{2,1,0:T(8,128)(2,1)S(1)}, bf16[1,128,512]{2,1,0:T(8,128)(2,1)S(1)}, u32[]{:S(2)}, u32[]{:S(2)}) collective-permute-start(bf16[1,128,512]{2,1,0:T(8,128)(2,1)S(1)} %get-tuple-element.187), channel_id=1, source_target_pairs={{0,4},{1,5},{2,6},{3,7},{4,0},{5,1},{6,2},{7,3},{8,12},{9,13},{10,... | collective-permute-start | bytes 393224 | tf_op jit(solution)/shard_map/ppermute | solution.py:78
  263.2 16.5 %collective-permute-start.18 = (f32[8,128]{1,0:T(8,128)S(1)}, f32[8,128]{1,0:T(8,128)S(1)}, u32[]{:S(2)}, u32[]{:S(2)}) collective-permute-start(f32[8,128]{1,0:T(8,128)S(1)} %broadcast_in_dim.87), channel_id=1, source_target_pairs={{0,8},{8,0},{16,24},{24,16},{1,9},{9,1},{17,25},{25,17},{2,10},{10... | collective-permute-start | bytes 12296 | tf_op jit(solution)/shard_map/ppermute | solution.py:78
  285.6 16.1 %collective-permute-start.11 = (bf16[4,128,512]{2,1,0:T(8,128)(2,1)}, bf16[4,128,512]{2,1,0:T(8,128)(2,1)}, u32[]{:S(2)}, u32[]{:S(2)}) collective-permute-start(bf16[4,128,512]{2,1,0:T(8,128)(2,1)} %pad_maximum_fusion.3), channel_id=1, source_target_pairs={{0,1},{1,0},{2,3},{3,2},{4,5},{5,4},{6,7},{7,6},{8,9},{9,8},{10,11... | collective-permute-start | bytes 1572872 | tf_op jit(solution)/shard_map/ppermute | solution.py:78
  288.3 19.2 %collective-permute-start.14 = (bf16[4,128,512]{2,1,0:T(8,128)(2,1)}, bf16[4,128,512]{2,1,0:T(8,128)(2,1)}, u32[]{:S(2)}, u32[]{:S(2)}) collective-permute-start(bf16[4,128,512]{2,1,0:T(8,128)(2,1)} %pad_maximum_fusion.4), channel_id=1, source_target_pairs={{0,2},{1,3},{2,0},{3,1},{4,6},{5,7},{6,4},{7,5},{8,10},{9,11},{10,... | collective-permute-start | bytes 1572872 | tf_op jit(solution)/shard_map/ppermute | solution.py:78
  290.7 180.8 %all-gather.15.cloned.1.call-start = ((), (), s32[]{:S(2)}) async-start(), calls=%async_computation.7 | async-start | bytes 2359296 | tf_op jit(solution)/shard_map/all_gather | solution.py:1149
  371.2 25.6 %collective-permute-start.20 = (bf16[2,2,128,512]{3,2,0,1:T(8,128)(2,1)}, bf16[2,2,128,512]{3,2,0,1:T(8,128)(2,1)}, u32[]{:S(2)}, u32[]{:S(2)}) collective-permute-start(bf16[2,2,128,512]{3,2,0,1:T(8,128)(2,1)} %fusion.48), channel_id=1, source_target_pairs={{0,1},{1,0},{2,3},{3,2},{4,5},{5,4},{6,7},{7,6},{8,9},{9,8},{10,11... | collective-permute-start | bytes 1572872 | tf_op jit(solution)/shard_map/ppermute | solution.py:78
  372.7 27.0 %collective-permute-start.23 = (bf16[2,2,128,512]{3,2,0,1:T(8,128)(2,1)}, bf16[2,2,128,512]{3,2,0,1:T(8,128)(2,1)}, u32[]{:S(2)}, u32[]{:S(2)}) collective-permute-start(bf16[2,2,128,512]{3,2,0,1:T(8,128)(2,1)} %fusion.49), channel_id=1, source_target_pairs={{0,2},{1,3},{2,0},{3,1},{4,6},{5,7},{6,4},{7,5},{8,10},{9,11},{10,... | collective-permute-start | bytes 1572872 | tf_op jit(solution)/shard_map/ppermute | solution.py:78
  401.0 8.7 %collective-permute-start.24 = (bf16[2,128,512]{2,1,0:T(8,128)(2,1)S(1)}, bf16[2,128,512]{2,1,0:T(8,128)(2,1)S(1)}, u32[]{:S(2)}, u32[]{:S(2)}) collective-permute-start(bf16[2,128,512]{2,1,0:T(8,128)(2,1)S(1)} %fusion.56), channel_id=1, source_target_pairs={{0,1},{1,0},{2,3},{3,2},{4,5},{5,4},{6,7},{7,6},{8,9},{9,8},{10,11... | collective-permute-start | bytes 786440 | tf_op jit(solution)/shard_map/ppermute | solution.py:78
  422.1 163.4 %all-gather.17.cloned.1.call-start = ((), (), s32[]{:S(2)}) async-start(), calls=%async_computation.8 | async-start | bytes 2359296 | tf_op jit(solution)/shard_map/all_gather | solution.py:1149
  518.7 47.9 %all-to-all-start.1 = ((bf16[8,128,384]{2,1,0:T(8,128)(2,1)}), bf16[8,128,384]{2,1,0:T(8,128)(2,1)}, u32[]{:S(2)}, u32[]{:S(2)}) async-start(bf16[8,128,384]{2,1,0:T(8,128)(2,1)} %copy-done.51), calls=%async_computation.1 | async-start | bytes 1572864 | tf_op jit(solution)/shard_map/all_to_all | solution.py:1152
  522.9 153.2 %all-gather.19.cloned.1.call-start = ((), (), s32[]{:S(2)}) async-start(), calls=%async_computation.9 | async-start | bytes 2359296 | tf_op jit(solution)/shard_map/all_gather | solution.py:1149
  524.7 17.0 %collective-permute-start.33 = (f32[33,8,128]{2,1,0:T(8,128)S(1)}, f32[33,8,128]{2,1,0:T(8,128)S(1)}, u32[]{:S(2)}, u32[]{:S(2)}) collective-permute-start(f32[33,8,128]{2,1,0:T(8,128)S(1)} %pad_maximum_fusion.17), channel_id=1, source_target_pairs={{0,1},{1,0},{2,3},{3,2},{4,5},{5,4},{6,7},{7,6},{8,9},{9,8},{10,11... | collective-permute-start | bytes 405512 | tf_op jit(solution)/shard_map/ppermute | solution.py:78
  596.6 10.6 %collective-permute-start.39 = (f32[1,8,1408]{2,1,0:T(8,128)S(1)}, f32[1,8,1408]{2,1,0:T(8,128)S(1)}, u32[]{:S(2)}, u32[]{:S(2)}) collective-permute-start(f32[1,8,1408]{2,1,0:T(8,128)S(1)} %add_bitcast_fusion), channel_id=1, source_target_pairs={{0,4},{1,5},{2,6},{3,7},{4,0},{5,1},{6,2},{7,3},{8,12},{9,13},{10,... | collective-permute-start | bytes 135176 | tf_op jit(solution)/shard_map/ppermute | solution.py:78
  603.0 39.2 %all-to-all-start.2 = ((bf16[8,128,384]{2,1,0:T(8,128)(2,1)}), bf16[8,128,384]{2,1,0:T(8,128)(2,1)}, u32[]{:S(2)}, u32[]{:S(2)}) async-start(bf16[8,128,384]{2,1,0:T(8,128)(2,1)} %copy-done.33), calls=%async_computation.2 | async-start | bytes 1572864 | tf_op jit(solution)/shard_map/all_to_all | solution.py:1152
  607.2 18.5 %collective-permute-start.40 = (f32[2,8,1408]{2,1,0:T(8,128)S(1)}, f32[2,8,1408]{2,1,0:T(8,128)S(1)}, u32[]{:S(2)}, u32[]{:S(2)}) collective-permute-start(f32[2,8,1408]{2,1,0:T(8,128)S(1)} %pad_maximum_fusion.20), channel_id=1, source_target_pairs={{0,2},{1,3},{2,0},{3,1},{4,6},{5,7},{6,4},{7,5},{8,10},{9,11},{10,... | collective-permute-start | bytes 270344 | tf_op jit(solution)/shard_map/ppermute | solution.py:78
  625.7 10.2 %collective-permute-start.41 = (f32[4,8,1408]{2,1,0:T(8,128)S(1)}, f32[4,8,1408]{2,1,0:T(8,128)S(1)}, u32[]{:S(2)}, u32[]{:S(2)}) collective-permute-start(f32[4,8,1408]{2,1,0:T(8,128)S(1)} %pad_maximum_fusion.14), channel_id=1, source_target_pairs={{0,1},{1,0},{2,3},{3,2},{4,5},{5,4},{6,7},{7,6},{8,9},{9,8},{10,11... | collective-permute-start | bytes 540680 | tf_op jit(solution)/shard_map/ppermute | solution.py:78
  642.2 27.7 %all-to-all-start.3 = ((bf16[8,128,512]{2,1,0:T(8,128)(2,1)}), bf16[8,128,512]{2,1,0:T(8,128)(2,1)}, u32[]{:S(2)}, u32[]{:S(2)}) async-start(bf16[8,128,512]{2,1,0:T(8,128)(2,1)} %copy-done.48), calls=%async_computation.3 | async-start | bytes 2097152 | tf_op jit(solution)/shard_map/all_to_all | solution.py:1152
  (176 other events, 1597.3 us)
Sparse Core Ops, SparseCore 0:
  11.5 203.6 all-gather.20
  217.9 58.9 all-gather.8
  279.0 53.6 all-gather.12
  335.3 52.6 all-gather.10
  422.2 49.2 all-gather.14
  518.8 56.6 all-gather.16
  585.6 61.9 all-gather.18

commit v3 on v2

--- a/solution.py
+++ b/solution.py
@@ -906,13 +906,13 @@
     new_master_ref[...] = master_ref[...] - LEARN_RATE * moment
 
 
-def finish(shrink, ortho, own_ortho, right_all, first, grad, error, moment, master, step):
+def finish(shrink, ortho, own_ortho, right_all, first, grad, grad_at, error, moment, master, step):
     height, width = error.shape
     own = moment.shape[0]
     row, own_row = pl.BlockSpec((height, step), lambda j: (0, j)), pl.BlockSpec((own, step), lambda j: (0, j))
     if grad.ndim == 3:
         grad_spec = pl.BlockSpec(
-            (grad.shape[0], height, step // grad.shape[0]), lambda j: (0, 0, j)
+            (grad.shape[0], height, step // grad.shape[0]), lambda j: (0, 0, grad_at + j)
         )
     else:
         grad_spec = row
@@ -1272,9 +1272,12 @@
     if not weights.plain:
         qkv_send = qkv_part(one_all, qkv_in_part, qkv_height, shard_count, rep_count)
         out_grad = out_part(shard_at, attended_all, out_all, shard_count, rep_count)
-        slab_grads = [exchange(qkv_send), out_grad, exchange(up_send), down_grad]
     own_piece = sum_over(own_piece, "rep")
     pieces, unused_arrival = gather_arrivals(own_piece, "shard")
+    if not weights.plain:
+        pieces, qkv_late, up_late = lax.optimization_barrier((pieces, qkv_send, up_send))
+        both = exchange(jnp.concatenate([qkv_late, up_late], axis=2))
+        slab_grads = [both, out_grad, both, down_grad]
     gain_count = gain_grad.shape[0]
     right_all, right_grams = whole_and_grams(arrival, pieces, widths)
     extra = right_all[:, sum(widths) :].reshape(-1)
@@ -1294,8 +1297,8 @@
         first = sum(widths[:k])
         if k < 4:
             new_error, new_moment, new_weight = finish(
-                shrink, slab_orthos[k], own_ortho, right_all, first, slab_grads[k], flat_errors[k],
-                moments[k], masters[k], model_width,
+                shrink, slab_orthos[k], own_ortho, right_all, first, slab_grads[k], 3 if k == 2 else 0,
+                flat_errors[k], moments[k], masters[k], model_width,
             )
         else:
             new_moment, new_weight = finish_table(

time: 713 us -> 762 us (1.069)
  local copies, waits for them, and re-layouts: 61.8 us -> 81.1 us
  waiting for transfers between devices: 238 us -> 255 us
  other arithmetic: 48.8 us -> 60.6 us
    all_gather x3, waiting for transfers between devices: 4.27 us -> 41.4 us  [everyone_of(): return lax.all_gather(array, 'shard', axis=0, tiled=True)]
    ppermute x42, waiting for transfers between devices: 221 us -> 202 us  [swap(): return lax.ppermute(array, axis, [(i, i ^ bit) for i in range(size)])]
    unnamed x324 -> x332, local copies, waits for them, and re-layouts: 32.5 us -> 38.1 us
  transfers between devices with their start and end apart: 53 -> 52, of which waited for: 33 -> 35; matrix products, arithmetic and copies ran while one was open for 18% -> 20% of each run, Pallas kernels for 26% -> 25%
where the time goes in v3:
time: 762 us; the launch traced here: 752 us
  waiting for transfers between devices  255 us (33%)
  Pallas kernels  202 us (27%)
  local copies, waits for them, and re-layouts  81.1 us (11%)
  starting transfers between devices  70.2 us (9%)
  matrix products  64.1 us (8%)
  other arithmetic  60.6 us (8%)
  between operations  19.1 us (3%)
    ppermute x42, waiting for transfers between devices, swap(): return lax.ppermute(array, axis, [(i, i ^ bit) for i in range(size)])  202 us
    dot_general x15, matrix products, dot_over(): lax.dot_general(left, right, (((left_dim,), (right_dim,)), ((), ())), pre...  63.8 us
    ppermute x42, starting transfers between devices, swap(): return lax.ppermute(array, axis, [(i, i ^ bit) for i in range(size)])  52.9 us
    all_gather x3, waiting for transfers between devices, everyone_of(): return lax.all_gather(array, 'shard', axis=0, tiled=True)  41.4 us
    unnamed x332, local copies, waits for them, and re-layouts  38.1 us
    pallas_call x8, Pallas kernels, packed_call(): pl.pallas_call(kernel, grid=(steps,), in_specs=[pl.BlockSpec((tokens, row...  37.4 us
    pallas_call x1, Pallas kernels, logits_back(): pl.pallas_call(functools.partial(logits_back_kernel, total), grid=(pl.cdi...  22.5 us
    pallas_call x1, Pallas kernels, attend(): pl.pallas_call(functools.partial(attend_kernel, length), grid=(HEADS,), i...  21.6 us
  transfers between devices with their start and end apart: 52, of which 35 were waited for; matrix products, arithmetic and copies ran while one was open for 20% of the time, Pallas kernels for 25%

profile of v3, /device:TPU:0, one launch (start us, length us, event | category | flops | bytes accessed | tf_op | source)
XLA Modules:
  0.0 752.1 jit_solution(12291797501158942092)
XLA Ops:
  22.4 5.8 all-to-all-start
  40.8 17.7 %fusion.163 = f32[8,4000]{1,0:T(8,128)} fusion(f32[1024,8]{0,1:T(8,128)S(1)} %copy-done.50, f32[4000,1024]{1,0:T(8,128)} %bitcast.469), kind=kOutput, calls=%fused_computation.407 | convolution fusion | flops 393216000 | bytes 16544768 | tf_op jit(solution)/shard_map/dot_general | solution.py:26
  60.3 31.3 %collective-permute-done = bf16[1000,1024]{1,0:T(8,128)(2,1)} collective-permute-done((bf16[1000,1024]{1,0:T(8,128)(2,1)}, bf16[1000,1024]{1,0:T(8,128)(2,1)}, u32[]{:S(2)}, u32[]{:S(2)}) %collective-permute-start) | collective-permute-done | bytes 2048032 | tf_op jit(solution)/shard_map/ppermute | solution.py:78
  102.0 11.6 %fusion.17 = bf16[1024,1024]{1,0:T(8,128)(2,1)S(1)} fusion(bf16[4000,1024]{1,0:T(8,128)(2,1)} %bitcast.466, s32[1024]{0:T(1024)S(1)} %fusion.118), kind=kOutput, calls=%fused_computation.29 | convolution fusion | flops 8393752576 | bytes 10293248 | tf_op jit(solution)/shard_map/dot_general | solution.py:26
  118.0 21.7 %collective-permute-done.3 = bf16[2,2,128,512]{3,2,0,1:T(8,128)(2,1)S(1)} collective-permute-done((bf16[2,2,128,512]{3,2,0,1:T(8,128)(2,1)S(1)}, bf16[2,2,128,512]{3,2,0,1:T(8,128)(2,1)S(1)}, u32[]{:S(2)}, u32[]{:S(2)}) %collective-permute-start.3) | collective-permute-done | bytes 524320 | tf_op jit(solution)/shard_map/ppermute | solution.py:78
  141.3 19.1 %collective-permute-done.6 = bf16[2,2,128,512]{3,2,0,1:T(8,128)(2,1)S(1)} collective-permute-done((bf16[2,2,128,512]{3,2,0,1:T(8,128)(2,1)S(1)}, bf16[2,2,128,512]{3,2,0,1:T(8,128)(2,1)S(1)}, u32[]{:S(2)}, u32[]{:S(2)}) %collective-permute-start.6) | collective-permute-done | bytes 524320 | tf_op jit(solution)/shard_map/ppermute | solution.py:78
  161.6 12.7 %collective-permute-done.4 = bf16[2,128,512]{2,1,0:T(8,128)(2,1)S(1)} collective-permute-done((bf16[2,128,512]{2,1,0:T(8,128)(2,1)S(1)}, bf16[2,128,512]{2,1,0:T(8,128)(2,1)S(1)}, u32[]{:S(2)}, u32[]{:S(2)}) %collective-permute-start.4) | collective-permute-done | bytes 262176 | tf_op jit(solution)/shard_map/ppermute | solution.py:78
  177.5 13.6 %collective-permute-done.5 = bf16[128,512]{1,0:T(8,128)(2,1)S(1)} collective-permute-done((bf16[128,512]{1,0:T(8,128)(2,1)S(1)}, bf16[128,512]{1,0:T(8,128)(2,1)S(1)}, u32[]{:S(2)}, u32[]{:S(2)}) %collective-permute-start.5) | collective-permute-done | bytes 131104 | tf_op jit(solution)/shard_map/ppermute | solution.py:78
  191.1 10.3 %collective-permute-done.8 = bf16[128,512]{1,0:T(8,128)(2,1)S(1)} collective-permute-done((bf16[128,512]{1,0:T(8,128)(2,1)S(1)}, bf16[128,512]{1,0:T(8,128)(2,1)S(1)}, u32[]{:S(2)}, u32[]{:S(2)}) %collective-permute-start.8) | collective-permute-done | bytes 131104 | tf_op jit(solution)/shard_map/ppermute | solution.py:78
  204.0 11.0 %all-gather.21.cloned.1.call-done = bf16[12288,1024]{1,0:T(8,128)(2,1)} async-done(((bf16[384,1024]{1,0:T(8,128)(2,1)}), bf16[12288,1024]{1,0:T(8,128)(2,1)}) %all-gather.21.cloned.1.call-update) | async-done | bytes 25165840 | tf_op jit(solution)/shard_map/all_gather | solution.py:1024
  219.3 21.6 %attend.1 = (bf16[128,1024]{1,0:T(8,128)(2,1)}, f32[128,1024]{1,0:T(8,128)S(1)}, f32[8,128,4096]{2,1,0:T(8,128)}) custom-call(bf16[128,3072]{1,0:T(8,128)(2,1)S(1)} %columns_kernel.3.queries_ref.keys_ref.values_ref, bf16[128,3072]{1,0:T(8,128)(2,1)S(1)} %columns_kernel.3.queries_ref.keys_ref.values_ref, ...), custom_call_target="tpu_custom_call" | custom-call | flops 1000000 | bytes 100000 | tf_op jit(solution)/shard_map/attend/pallas_call | solution.py:326
  245.7 5.0 columns_kernel.5
  251.4 5.5 rows_kernel.1
  263.4 12.8 %collective-permute-done.9 = bf16[1,128,512]{2,1,0:T(8,128)(2,1)S(1)} collective-permute-done((bf16[1,128,512]{2,1,0:T(8,128)(2,1)S(1)}, bf16[1,128,512]{2,1,0:T(8,128)(2,1)S(1)}, u32[]{:S(2)}, u32[]{:S(2)}) %collective-permute-start.9) | collective-permute-done | bytes 131104 | tf_op jit(solution)/shard_map/ppermute | solution.py:78
  290.6 10.8 %collective-permute-done.11 = bf16[4,128,512]{2,1,0:T(8,128)(2,1)} collective-permute-done((bf16[4,128,512]{2,1,0:T(8,128)(2,1)}, bf16[4,128,512]{2,1,0:T(8,128)(2,1)}, u32[]{:S(2)}, u32[]{:S(2)}) %collective-permute-start.11) | collective-permute-done | bytes 524320 | tf_op jit(solution)/shard_map/ppermute | solution.py:78
  310.6 18.7 %logits.1 = (f32[4000,1024]{1,0:T(8,128)}, f32[3,1024]{1,0:T(4,128)}) custom-call(bf16[4000,1024]{1,0:T(8,128)(2,1)} %bitcast.467, bf16[1024,1024]{1,0:T(8,128)(2,1)} %pad_maximum_fusion.final_ref, s32[1,1024]{1,0:T(1,128)S(1)} %copy-done.57), custom_call_target="tpu_custom_call" | custom-call | flops 1000000 | bytes 100000 | tf_op jit(solution)/shard_map/logits/pallas_call | solution.py:403
  360.2 22.5 %logits_back.1 = (bf16[4000,1024]{1,0:T(8,128)(2,1)}, f32[1024,1024]{1,0:T(8,128)}) custom-call(f32[4000,1024]{1,0:T(8,128)} %get-tuple-element.92.logits_ref, bf16[4000,1024]{1,0:T(8,128)(2,1)} %bitcast.468, f32[1,1024]{1,0:T(1,128)} %log_add_fusion.log_ref, f32[1,1024]{1,0:T(1,128)} %divide_bitcast_fusion.scale_ref, s32[1,1024]{1,0:T(1,128)} %compare_select_fusion.target_ref), custom_call_target="tpu_custom_call" | custom-call | flops 1000000 | bytes 100000 | tf_op jit(solution)/shard_map/logits_back/pallas_call | solution.py:450
  391.6 20.6 %table_gradient.1.moved_ref = f32[4000,1024]{1,0:T(8,128)} custom-call(bf16[4000,1024]{1,0:T(8,128)(2,1)} %get-tuple-element.99.grad_ref, bf16[1024,1024]{1,0:T(8,128)(2,1)} %pad_maximum_fusion.final_ref, f32[4000,1024]{1,0:T(8,128)} %bitcast.470), custom_call_target="tpu_custom_call" | custom-call | flops 1000000 | bytes 100000 | tf_op jit(solution)/shard_map/table_gradient/pallas_call | solution.py:481
  425.2 5.6 collective-permute-done.22
  439.1 5.9 rows_back_kernel.1
  446.6 6.8 columns_back_kernel.3
  457.9 17.1 %attend_back.1 = (bf16[128,1024]{1,0:T(8,128)(2,1)S(1)}, bf16[128,1024]{1,0:T(8,128)(2,1)S(1)}, bf16[128,1024]{1,0:T(8,128)(2,1)S(1)}, bf16[8,128,384]{2,1,0:T(8,128)(2,1)S(1)}, f32[1,1024]{1,0:T(1,128)S(1)}) custom-call(bf16[128,3072]{1,0:T(8,128)(2,1)S(1)} %columns_kernel.3.queries_ref.keys_ref.values_ref, ...), custom_call_target="tpu_custom_call" | custom-call | flops 1000000 | bytes 100000 | tf_op jit(solution)/shard_map/attend_back/pallas_call | solution.py:350
  475.1 5.3 columns_back_kernel.5
  481.5 5.3 all-gather.15.cloned.1.call-done.down_in_ref
  550.6 12.7 %mlp_part.1 = (bf16[8,128,512]{2,1,0:T(8,128)(2,1)S(1)}, f32[512,1024]{1,0:T(8,128)S(1)}) custom-call(s32[1]{0:T(128)} %bitcast.129.at_ref, bf16[1024,1024]{1,0:T(8,128)(2,1)S(1)} %copy-done.28, bf16[1024,1024]{1,0:T(8,128)(2,1)S(1)} %copy-done.29, bf16[32,384,1024]{2,1,0:T(8,128)(2,1)} %bitcast.464, bf16[32,384,1024]{2,1,0:T(8,128)(2,1)} %bitcast.465), custom_call_target="tpu_custom_call" | custom-call | flops 1000000 | bytes 100000 | tf_op jit(solution)/shard_map/mlp_part/pallas_call | solution.py:819
  563.5 6.2 right_pieces.1
  577.6 7.8 %fusion.162 = f32[8,1024]{1,0:T(8,128)S(1)} fusion(f32[8,1024]{1,0:T(8,128)S(1)} %copy-done.61, f32[8,4000]{1,0:T(8,128)S(1)} %get-tuple-element.122.ortho_ref, f32[4000,1024]{1,0:T(8,128)} %table_gradient.1.moved_ref), kind=kOutput, calls=%fused_computation.406 | convolution fusion | flops 196616192 | bytes 16577536 | tf_op jit(solution)/shard_map/dot_general | solution.py:26
  593.1 5.6 collective-permute-done.34
  624.4 7.2 collective-permute-done.40
  642.1 7.0 all-to-all-start.2
  679.3 36.0 %all-gather.19.cloned.1.call-done.start_ref = bf16[1024,1024]{1,0:T(8,128)(2,1)} async-done(((bf16[128,1024]{1,0:T(8,128)(2,1)}), bf16[1024,1024]{1,0:T(8,128)(2,1)}) %all-gather.19.cloned.1.call-update) | async-done | bytes 2097168 | tf_op jit(solution)/shard_map/all_gather | solution.py:1149
  716.9 18.0 %table_error.1 = f32[4000,1024]{1,0:T(8,128)} custom-call(f32[4000,1024]{1,0:T(8,128)} %table_gradient.1.moved_ref, s32[1,1024]{1,0:T(1,128)S(1)} %bitcast.454, bf16[1024,1024]{1,0:T(8,128)(2,1)S(1)} %copy-done.38, f32[8,4000]{1,0:T(8,128)S(1)} %get-tuple-element.122.ortho_ref, f32[8,1024]{1,0:T(8,128)S(1)} %get-tuple-element.188.right_ref), custom_call_target="tpu_custom_call" | custom-call | flops 1000000 | bytes 100000 | tf_op jit(solution)/shard_map/table_error/pallas_call | solution.py:656
  (690 shorter events, 314.2 us)
Async XLA Ops:
  7.2 207.8 %all-gather.21.cloned.1.call-start = ((), (), s32[]{:S(2)}) async-start(), calls=%async_computation.9 | async-start | bytes 25952256 | tf_op jit(solution)/shard_map/all_gather | solution.py:1024
  18.6 73.1 %collective-permute-start = (bf16[1000,1024]{1,0:T(8,128)(2,1)}, bf16[1000,1024]{1,0:T(8,128)(2,1)}, u32[]{:S(2)}, u32[]{:S(2)}) collective-permute-start(bf16[1000,1024]{1,0:T(8,128)(2,1)} %get-tuple-element.176), channel_id=1, source_target_pairs={{0,16},{8,24},{16,0},{24,8},{1,17},{9,25},{17,1},{25,9},{2,18},{10... | collective-permute-start | bytes 6144008 | tf_op jit(solution)/shard_map/ppermute | solution.py:78
  21.5 76.0 %collective-permute-start.1 = (bf16[1000,1024]{1,0:T(8,128)(2,1)}, bf16[1000,1024]{1,0:T(8,128)(2,1)}, u32[]{:S(2)}, u32[]{:S(2)}) collective-permute-start(bf16[1000,1024]{1,0:T(8,128)(2,1)} %get-tuple-element.176), channel_id=1, source_target_pairs={{0,8},{8,0},{16,24},{24,16},{1,9},{9,1},{17,25},{25,17},{2,10},{10... | collective-permute-start | bytes 6144008 | tf_op jit(solution)/shard_map/ppermute | solution.py:78
  22.4 70.7 %all-to-all-start = ((s32[8,3,128]{2,1,0:T(4,128)}), s32[8,3,128]{2,1,0:T(4,128)S(1)}, u32[]{:S(2)}, u32[]{:S(2)}) async-start(s32[8,3,128]{2,1,0:T(4,128)} %broadcast_in_dim.83), calls=%async_computation | async-start | bytes 32768 | tf_op jit(solution)/shard_map/all_to_all | solution.py:183
  28.2 404.9 %all-gather.9.cloned.1.call-start = ((), (), s32[]{:S(2)}) async-start(), calls=%async_computation.3 | async-start | bytes 2359296 | tf_op jit(solution)/shard_map/all_gather | solution.py:1116
  91.6 8.9 %collective-permute-start.2 = (bf16[1000,1024]{1,0:T(8,128)(2,1)}, bf16[1000,1024]{1,0:T(8,128)(2,1)S(1)}, u32[]{:S(2)}, u32[]{:S(2)}) collective-permute-start(bf16[1000,1024]{1,0:T(8,128)(2,1)} %collective-permute-done), channel_id=1, source_target_pairs={{0,8},{8,0},{16,24},{24,16},{1,9},{9,1},{17,25},{25,17},{2,10},{10... | collective-permute-start | bytes 6144008 | tf_op jit(solution)/shard_map/ppermute | solution.py:78
  114.1 25.6 %collective-permute-start.3 = (bf16[2,2,128,512]{3,2,0,1:T(8,128)(2,1)S(1)}, bf16[2,2,128,512]{3,2,0,1:T(8,128)(2,1)S(1)}, u32[]{:S(2)}, u32[]{:S(2)}) collective-permute-start(bf16[2,2,128,512]{3,2,0,1:T(8,128)(2,1)S(1)} %bitcast.491), channel_id=1, source_target_pairs={{0,1},{1,0},{2,3},{3,2},{4,5},{5,4},{6,7},{7,6},{8,9},{9,8},{10,11... | collective-permute-start | bytes 1572872 | tf_op jit(solution)/shard_map/ppermute | solution.py:78
  115.7 44.7 %collective-permute-start.6 = (bf16[2,2,128,512]{3,2,0,1:T(8,128)(2,1)S(1)}, bf16[2,2,128,512]{3,2,0,1:T(8,128)(2,1)S(1)}, u32[]{:S(2)}, u32[]{:S(2)}) collective-permute-start(bf16[2,2,128,512]{3,2,0,1:T(8,128)(2,1)S(1)} %bitcast.490), channel_id=1, source_target_pairs={{0,2},{1,3},{2,0},{3,1},{4,6},{5,7},{6,4},{7,5},{8,10},{9,11},{10,... | collective-permute-start | bytes 1572872 | tf_op jit(solution)/shard_map/ppermute | solution.py:78
  139.7 34.6 %collective-permute-start.4 = (bf16[2,128,512]{2,1,0:T(8,128)(2,1)S(1)}, bf16[2,128,512]{2,1,0:T(8,128)(2,1)S(1)}, u32[]{:S(2)}, u32[]{:S(2)}) collective-permute-start(bf16[2,128,512]{2,1,0:T(8,128)(2,1)S(1)} %slice_bitcast_fusion.6), channel_id=1, source_target_pairs={{0,2},{1,3},{2,0},{3,1},{4,6},{5,7},{6,4},{7,5},{8,10},{9,11},{10,... | collective-permute-start | bytes 786440 | tf_op jit(solution)/shard_map/ppermute | solution.py:78
  160.5 16.0 %collective-permute-start.7 = (bf16[2,128,512]{2,1,0:T(8,128)(2,1)S(1)}, bf16[2,128,512]{2,1,0:T(8,128)(2,1)S(1)}, u32[]{:S(2)}, u32[]{:S(2)}) collective-permute-start(bf16[2,128,512]{2,1,0:T(8,128)(2,1)S(1)} %slice_bitcast_fusion.4), channel_id=1, source_target_pairs={{0,1},{1,0},{2,3},{3,2},{4,5},{5,4},{6,7},{7,6},{8,9},{9,8},{10,11... | collective-permute-start | bytes 786440 | tf_op jit(solution)/shard_map/ppermute | solution.py:78
  174.4 16.7 %collective-permute-start.5 = (bf16[128,512]{1,0:T(8,128)(2,1)S(1)}, bf16[128,512]{1,0:T(8,128)(2,1)S(1)}, u32[]{:S(2)}, u32[]{:S(2)}) collective-permute-start(bf16[128,512]{1,0:T(8,128)(2,1)S(1)} %slice_bitcast_fusion.12), channel_id=1, source_target_pairs={{0,4},{1,5},{2,6},{3,7},{4,0},{5,1},{6,2},{7,3},{8,12},{9,13},{10,... | collective-permute-start | bytes 393224 | tf_op jit(solution)/shard_map/ppermute | solution.py:78
  176.5 25.0 %collective-permute-start.8 = (bf16[128,512]{1,0:T(8,128)(2,1)S(1)}, bf16[128,512]{1,0:T(8,128)(2,1)S(1)}, u32[]{:S(2)}, u32[]{:S(2)}) collective-permute-start(bf16[128,512]{1,0:T(8,128)(2,1)S(1)} %slice_bitcast_fusion.10), channel_id=1, source_target_pairs={{0,4},{1,5},{2,6},{3,7},{4,0},{5,1},{6,2},{7,3},{8,12},{9,13},{10,... | collective-permute-start | bytes 393224 | tf_op jit(solution)/shard_map/ppermute | solution.py:78
  203.0 230.0 %all-gather.13.cloned.1.call-start = ((), (), s32[]{:S(2)}) async-start(), calls=%async_computation.5 | async-start | bytes 2359296 | tf_op jit(solution)/shard_map/all_gather | solution.py:1116
  244.7 188.4 %all-gather.11.cloned.1.call-start = ((), (), s32[]{:S(2)}) async-start(), calls=%async_computation.4 | async-start | bytes 2359296 | tf_op jit(solution)/shard_map/all_gather | solution.py:1116
  258.4 17.8 %collective-permute-start.9 = (bf16[1,128,512]{2,1,0:T(8,128)(2,1)S(1)}, bf16[1,128,512]{2,1,0:T(8,128)(2,1)S(1)}, u32[]{:S(2)}, u32[]{:S(2)}) collective-permute-start(bf16[1,128,512]{2,1,0:T(8,128)(2,1)S(1)} %get-tuple-element.192), channel_id=1, source_target_pairs={{0,4},{1,5},{2,6},{3,7},{4,0},{5,1},{6,2},{7,3},{8,12},{9,13},{10,... | collective-permute-start | bytes 393224 | tf_op jit(solution)/shard_map/ppermute | solution.py:78
  259.2 19.7 %collective-permute-start.12 = (bf16[1,128,512]{2,1,0:T(8,128)(2,1)S(1)}, bf16[1,128,512]{2,1,0:T(8,128)(2,1)S(1)}, u32[]{:S(2)}, u32[]{:S(2)}) collective-permute-start(bf16[1,128,512]{2,1,0:T(8,128)(2,1)S(1)} %get-tuple-element.193), channel_id=1, source_target_pairs={{0,4},{1,5},{2,6},{3,7},{4,0},{5,1},{6,2},{7,3},{8,12},{9,13},{10,... | collective-permute-start | bytes 393224 | tf_op jit(solution)/shard_map/ppermute | solution.py:78
  263.4 16.2 %collective-permute-start.18 = (f32[8,128]{1,0:T(8,128)S(1)}, f32[8,128]{1,0:T(8,128)S(1)}, u32[]{:S(2)}, u32[]{:S(2)}) collective-permute-start(f32[8,128]{1,0:T(8,128)S(1)} %broadcast_in_dim.87), channel_id=1, source_target_pairs={{0,8},{8,0},{16,24},{24,16},{1,9},{9,1},{17,25},{25,17},{2,10},{10... | collective-permute-start | bytes 12296 | tf_op jit(solution)/shard_map/ppermute | solution.py:78
  276.3 8.2 %collective-permute-start.10 = (bf16[2,128,512]{2,1,0:T(8,128)(2,1)S(1)}, bf16[2,128,512]{2,1,0:T(8,128)(2,1)S(1)}, u32[]{:S(2)}, u32[]{:S(2)}) collective-permute-start(bf16[2,128,512]{2,1,0:T(8,128)(2,1)S(1)} %pad_maximum_fusion.10), channel_id=1, source_target_pairs={{0,2},{1,3},{2,0},{3,1},{4,6},{5,7},{6,4},{7,5},{8,10},{9,11},{10,... | collective-permute-start | bytes 786440 | tf_op jit(solution)/shard_map/ppermute | solution.py:78
  279.0 8.2 %collective-permute-start.13 = (bf16[2,128,512]{2,1,0:T(8,128)(2,1)S(1)}, bf16[2,128,512]{2,1,0:T(8,128)(2,1)S(1)}, u32[]{:S(2)}, u32[]{:S(2)}) collective-permute-start(bf16[2,128,512]{2,1,0:T(8,128)(2,1)S(1)} %pad_maximum_fusion.11), channel_id=1, source_target_pairs={{0,1},{1,0},{2,3},{3,2},{4,5},{5,4},{6,7},{7,6},{8,9},{9,8},{10,11... | collective-permute-start | bytes 786440 | tf_op jit(solution)/shard_map/ppermute | solution.py:78
  285.4 16.0 %collective-permute-start.11 = (bf16[4,128,512]{2,1,0:T(8,128)(2,1)}, bf16[4,128,512]{2,1,0:T(8,128)(2,1)}, u32[]{:S(2)}, u32[]{:S(2)}) collective-permute-start(bf16[4,128,512]{2,1,0:T(8,128)(2,1)} %pad_maximum_fusion.4), channel_id=1, source_target_pairs={{0,1},{1,0},{2,3},{3,2},{4,5},{5,4},{6,7},{7,6},{8,9},{9,8},{10,11... | collective-permute-start | bytes 1572872 | tf_op jit(solution)/shard_map/ppermute | solution.py:78
  288.0 19.6 %collective-permute-start.14 = (bf16[4,128,512]{2,1,0:T(8,128)(2,1)}, bf16[4,128,512]{2,1,0:T(8,128)(2,1)}, u32[]{:S(2)}, u32[]{:S(2)}) collective-permute-start(bf16[4,128,512]{2,1,0:T(8,128)(2,1)} %pad_maximum_fusion.5), channel_id=1, source_target_pairs={{0,2},{1,3},{2,0},{3,1},{4,6},{5,7},{6,4},{7,5},{8,10},{9,11},{10,... | collective-permute-start | bytes 1572872 | tf_op jit(solution)/shard_map/ppermute | solution.py:78
  290.5 196.3 %all-gather.15.cloned.1.call-start = ((), (), s32[]{:S(2)}) async-start(), calls=%async_computation.6 | async-start | bytes 2359296 | tf_op jit(solution)/shard_map/all_gather | solution.py:1149
  388.1 24.7 %collective-permute-start.20 = (bf16[2,2,128,512]{3,2,0,1:T(8,128)(2,1)}, bf16[2,2,128,512]{3,2,0,1:T(8,128)(2,1)}, u32[]{:S(2)}, u32[]{:S(2)}) collective-permute-start(bf16[2,2,128,512]{3,2,0,1:T(8,128)(2,1)} %fusion.48), channel_id=1, source_target_pairs={{0,1},{1,0},{2,3},{3,2},{4,5},{5,4},{6,7},{7,6},{8,9},{9,8},{10,11... | collective-permute-start | bytes 1572872 | tf_op jit(solution)/shard_map/ppermute | solution.py:78
  388.9 26.9 %collective-permute-start.23 = (bf16[2,2,128,512]{3,2,0,1:T(8,128)(2,1)}, bf16[2,2,128,512]{3,2,0,1:T(8,128)(2,1)}, u32[]{:S(2)}, u32[]{:S(2)}) collective-permute-start(bf16[2,2,128,512]{3,2,0,1:T(8,128)(2,1)} %fusion.49), channel_id=1, source_target_pairs={{0,2},{1,3},{2,0},{3,1},{4,6},{5,7},{6,4},{7,5},{8,10},{9,11},{10,... | collective-permute-start | bytes 1572872 | tf_op jit(solution)/shard_map/ppermute | solution.py:78
  417.0 7.9 %collective-permute-start.24 = (bf16[2,128,512]{2,1,0:T(8,128)(2,1)S(1)}, bf16[2,128,512]{2,1,0:T(8,128)(2,1)S(1)}, u32[]{:S(2)}, u32[]{:S(2)}) collective-permute-start(bf16[2,128,512]{2,1,0:T(8,128)(2,1)S(1)} %fusion.56), channel_id=1, source_target_pairs={{0,1},{1,0},{2,3},{3,2},{4,5},{5,4},{6,7},{7,6},{8,9},{9,8},{10,11... | collective-permute-start | bytes 786440 | tf_op jit(solution)/shard_map/ppermute | solution.py:78
  422.0 8.7 %collective-permute-start.22 = (bf16[128,512]{1,0:T(8,128)(2,1)S(1)}, bf16[128,512]{1,0:T(8,128)(2,1)S(1)}, u32[]{:S(2)}, u32[]{:S(2)}) collective-permute-start(bf16[128,512]{1,0:T(8,128)(2,1)S(1)} %fusion.73), channel_id=1, source_target_pairs={{0,4},{1,5},{2,6},{3,7},{4,0},{5,1},{6,2},{7,3},{8,12},{9,13},{10,... | collective-permute-start | bytes 393224 | tf_op jit(solution)/shard_map/ppermute | solution.py:78
  538.8 51.6 %all-to-all-start.1 = ((bf16[8,128,384]{2,1,0:T(8,128)(2,1)}), bf16[8,128,384]{2,1,0:T(8,128)(2,1)}, u32[]{:S(2)}, u32[]{:S(2)}) async-start(bf16[8,128,384]{2,1,0:T(8,128)(2,1)} %copy-done.44), calls=%async_computation.1 | async-start | bytes 1572864 | tf_op jit(solution)/shard_map/all_to_all | solution.py:1152
  543.1 106.9 %all-gather.17.cloned.1.call-start = ((), (), s32[]{:S(2)}) async-start(), calls=%async_computation.7 | async-start | bytes 2359296 | tf_op jit(solution)/shard_map/all_gather | solution.py:1149
  544.8 18.6 %collective-permute-start.33 = (f32[33,8,128]{2,1,0:T(8,128)S(1)}, f32[33,8,128]{2,1,0:T(8,128)S(1)}, u32[]{:S(2)}, u32[]{:S(2)}) collective-permute-start(f32[33,8,128]{2,1,0:T(8,128)S(1)} %pad_maximum_fusion.18), channel_id=1, source_target_pairs={{0,1},{1,0},{2,3},{3,2},{4,5},{5,4},{6,7},{7,6},{8,9},{9,8},{10,11... | collective-permute-start | bytes 405512 | tf_op jit(solution)/shard_map/ppermute | solution.py:78
  593.0 122.3 %all-gather.19.cloned.1.call-start = ((), (), s32[]{:S(2)}) async-start(), calls=%async_computation.8 | async-start | bytes 2359296 | tf_op jit(solution)/shard_map/all_gather | solution.py:1149
  620.6 11.0 %collective-permute-start.40 = (f32[2,8,1408]{2,1,0:T(8,128)S(1)}, f32[2,8,1408]{2,1,0:T(8,128)S(1)}, u32[]{:S(2)}, u32[]{:S(2)}) collective-permute-start(f32[2,8,1408]{2,1,0:T(8,128)S(1)} %pad_maximum_fusion.21), channel_id=1, source_target_pairs={{0,2},{1,3},{2,0},{3,1},{4,6},{5,7},{6,4},{7,5},{8,10},{9,11},{10,... | collective-permute-start | bytes 270344 | tf_op jit(solution)/shard_map/ppermute | solution.py:78
  642.1 92.9 %all-to-all-start.2 = ((bf16[8,128,896]{2,1,0:T(8,128)(2,1)}), bf16[8,128,896]{2,1,0:T(8,128)(2,1)}, u32[]{:S(2)}, u32[]{:S(2)}) async-start(bf16[8,128,896]{2,1,0:T(8,128)(2,1)} %pad_maximum_fusion.1), calls=%async_computation.2 | async-start | bytes 3670016 | tf_op jit(solution)/shard_map/all_to_all | solution.py:1152
  (179 other events, 1551.8 us)
Sparse Core Ops, SparseCore 0:
  11.5 203.4 all-gather.20
  217.8 58.9 all-gather.8
  279.5 53.6 all-gather.12
  335.7 48.1 all-gather.10
  437.8 49.0 all-gather.14
  593.1 52.9 all-gather.16
  648.9 66.4 all-gather.18
